TPU v7x, 32 devices: a whole 2x2x4 slice. The times are simulated.
32 devices in a mesh: batch: 16 (over z, y, core), seq: 2 (over x).
Axes of the slice: x: 2, y: 2, z: 4, core: 2. Of those that a mesh axis runs over, the one named last changes fastest.
Arguments:
- source: bfloat16 [16, 1024, 512], P('batch', 'seq'), may hold values from -6 to 6
- target: bfloat16 [16, 1024, 512], P('batch', 'seq'), may hold values from -6 to 6
- source_ids: int32 [16, 1024], P('batch', 'seq'), may hold values from 0 to 2, as said below
- target_ids: int32 [16, 1024], P('batch', 'seq'), may hold values from 0 to 2, as said below
- out_grad: bfloat16 [16, 1024, 512], P('batch', 'seq'), may hold values from -6 to 6
- enc_qkv: bfloat16 [3, 512, 512], replicated, may hold values from -0.25 to 0.25
- enc_out: bfloat16 [512, 512], replicated, may hold values from -2 to 2
- enc_up: bfloat16 [512, 2048], replicated, may hold values from -0.25 to 0.25
- enc_up_bias: float32 [2048], replicated, may hold values from -3 to 3
- enc_down: bfloat16 [2048, 512], replicated, may hold values from -0.125 to 0.125
- enc_down_bias: float32 [512], replicated, may hold values from -3 to 3
- enc_gain: float32 [2, 512], replicated, may hold values from 0.1 to 1.9
- enc_shift: float32 [2, 512], replicated, may hold values from -3 to 3
- dec_qkv: bfloat16 [3, 512, 512], replicated, may hold values from -0.25 to 0.25
- dec_out: bfloat16 [512, 512], replicated, may hold values from -2 to 2
- cross_qkv: bfloat16 [3, 512, 512], replicated, may hold values from -0.25 to 0.25
- cross_out: bfloat16 [512, 512], replicated, may hold values from -2 to 2
- dec_up: bfloat16 [512, 2048], replicated, may hold values from -0.25 to 0.25
- dec_up_bias: float32 [2048], replicated, may hold values from -3 to 3
- dec_down: bfloat16 [2048, 512], replicated, may hold values from -0.125 to 0.125
- dec_down_bias: float32 [512], replicated, may hold values from -3 to 3
- dec_gain: float32 [3, 512], replicated, may hold values from 0.1 to 1.9
- dec_shift: float32 [3, 512], replicated, may hold values from -3 to 3
Outputs:
- decoded: bfloat16 [16, 1024, 512], P('batch', 'seq')
- source_grad: bfloat16 [16, 1024, 512], P('batch', 'seq')
- target_grad: bfloat16 [16, 1024, 512], P('batch', 'seq')
- enc_qkv_grad: float32 [3, 512, 512], P(None, 'seq', 'batch')
- enc_out_grad: float32 [512, 512], P('seq', 'batch')
- enc_up_grad: float32 [512, 2048], P('seq', 'batch')
- enc_up_bias_grad: float32 [2048], replicated
- enc_down_grad: float32 [2048, 512], P('seq', 'batch')
- enc_down_bias_grad: float32 [512], replicated
- enc_gain_grad: float32 [2, 512], replicated
- enc_shift_grad: float32 [2, 512], replicated
- dec_qkv_grad: float32 [3, 512, 512], P(None, 'seq', 'batch')
- dec_out_grad: float32 [512, 512], P('seq', 'batch')
- cross_qkv_grad: float32 [3, 512, 512], P(None, 'seq', 'batch')
- cross_out_grad: float32 [512, 512], P('seq', 'batch')
- dec_up_grad: float32 [512, 2048], P('seq', 'batch')
- dec_up_bias_grad: float32 [2048], replicated
- dec_down_grad: float32 [2048, 512], P('seq', 'batch')
- dec_down_bias_grad: float32 [512], replicated
- dec_gain_grad: float32 [3, 512], replicated
- dec_shift_grad: float32 [3, 512], replicated
Inputs may be any that keep to these rules, and one draw needn't show every extreme that they name: `source_ids`: in every row the ids never fall and take each of the values 0, 1 and 2; id 1 begins at a position from 1 to 511 and id 2 at a position from 513 to 1023. `target_ids`: in every row the ids never fall and take each of the values 0, 1 and 2; id 1 begins at a position from 1 to 511 and id 2 at a position from 513 to 1023.
All inputs are finite; a program needn't handle non-finite values.
Results may differ from a plain program's by a relative error of at most 0.04.
Values may be sent and summed in bfloat16 or wider, within the bound.
A program may use at most 192 MiB of HBM per device.

v0:
```python
import jax
import jax.numpy as jnp
from jax import lax
from jax.sharding import PartitionSpec as P

HEAD_DIM = 64


NEGATIVE = -1e30


def layer_norm(value, gain, shift):
    mean = jnp.mean(value, axis=-1, keepdims=True)
    centred = value - mean
    spread = jnp.mean(centred * centred, axis=-1, keepdims=True)
    return centred * lax.rsqrt(spread + 1e-06) * gain + shift


def norm_back(value, gain, shift, grad):
    _, pull = jax.vjp(layer_norm, value, gain, shift)
    return pull(grad)


def gelu_back(inner, grad):
    _, pull = jax.vjp(jax.nn.gelu, inner)
    return pull(grad)[0]


def matmul(left, right):
    return jnp.dot(left, right, preferred_element_type=jnp.float32)


def weight_grad(inputs, grad):
    return lax.dot_general(
        inputs, grad, (((0,), (0,)), ((), ())), preferred_element_type=jnp.float32
    )


def input_grad(grad, weight):
    return lax.dot_general(
        grad, weight, (((1,), (1,)), ((), ())), preferred_element_type=jnp.float32
    )


def to_low(value):
    return value.astype(jnp.bfloat16)


def split_heads(value):
    return value.reshape(value.shape[0], -1, HEAD_DIM)


def block_live(query_ids, key_ids, offset, block, rows, causal):
    first_key = lax.dynamic_index_in_dim(key_ids, block * rows, 0, keepdims=False)
    last_key = lax.dynamic_index_in_dim(key_ids, block * rows + rows - 1, 0, keepdims=False)
    live = (first_key <= query_ids[rows - 1]) & (query_ids[0] <= last_key)
    if causal:
        live = live & (block * rows <= offset + rows - 1)
    return live


def block_scores(queries, keys_all, query_ids, key_ids, offset, block, causal):
    rows = queries.shape[0]
    key_block = lax.dynamic_slice_in_dim(keys_all, block * rows, rows, 0)
    id_block = lax.dynamic_slice_in_dim(key_ids, block * rows, rows, 0)
    scores = (
        jnp.einsum("qhe,khe->hqk", queries, key_block, preferred_element_type=jnp.float32) * 0.125
    )
    allowed = query_ids[:, None] == id_block[None, :]
    if causal:
        positions = jnp.arange(rows, dtype=jnp.int32)
        allowed = allowed & ((offset + positions)[:, None] >= (block * rows + positions)[None, :])
    allowed = allowed[None]
    return (jnp.where(allowed, scores, NEGATIVE), allowed, key_block)


def attend_forward(queries, keys_all, values_all, query_ids, key_ids, offset, causal):
    rows = queries.shape[0]
    heads_count = queries.shape[1]
    count = keys_all.shape[0] // rows

    def first_pass(block, carry):

        def first_compute(state):
            largest, total = state
            scores, allowed, _ = block_scores(
                queries, keys_all, query_ids, key_ids, offset, block, causal
            )
            newest = jnp.maximum(largest, jnp.max(scores, axis=-1))
            terms = jnp.where(allowed, jnp.exp(scores - newest[..., None]), 0.0)
            return (newest, total * jnp.exp(largest - newest) + jnp.sum(terms, axis=-1))

        live = block_live(query_ids, key_ids, offset, block, rows, causal)
        return lax.cond(live, first_compute, lambda state: state, carry)

    initial = (
        jnp.full((heads_count, rows), NEGATIVE, jnp.float32),
        jnp.zeros((heads_count, rows), jnp.float32),
    )
    largest, total = lax.fori_loop(0, count, first_pass, initial)
    log_total = largest + jnp.log(total)

    def second_pass(block, carry):

        def second_compute(output):
            scores, allowed, _ = block_scores(
                queries, keys_all, query_ids, key_ids, offset, block, causal
            )
            value_block = lax.dynamic_slice_in_dim(values_all, block * rows, rows, 0)
            chances = jnp.where(allowed, jnp.exp(scores - log_total[..., None]), 0.0)
            return output + jnp.einsum(
                "hqk,khe->qhe", to_low(chances), value_block, preferred_element_type=jnp.float32
            )

        live = block_live(query_ids, key_ids, offset, block, rows, causal)
        return lax.cond(live, second_compute, lambda output: output, carry)

    output = lax.fori_loop(0, count, second_pass, jnp.zeros(queries.shape, jnp.float32))
    return (output, log_total)


def attend_backward(
    queries, keys_all, values_all, query_ids, key_ids, offset, causal, grad_out, settle, log_total
):
    rows = queries.shape[0]
    count = keys_all.shape[0] // rows

    def step_block(block, carry):

        def step_compute(state):
            query_grad, key_grads, value_grads = state
            scores, allowed, key_block = block_scores(
                queries, keys_all, query_ids, key_ids, offset, block, causal
            )
            value_block = lax.dynamic_slice_in_dim(values_all, block * rows, rows, 0)
            chances = jnp.where(allowed, jnp.exp(scores - log_total[..., None]), 0.0)
            chance_grad = jnp.einsum(
                "qhe,khe->hqk", grad_out, value_block, preferred_element_type=jnp.float32
            )
            score_grad = to_low(chances * (chance_grad - settle[..., None]))
            query_grad = (
                query_grad
                + jnp.einsum(
                    "hqk,khe->qhe", score_grad, key_block, preferred_element_type=jnp.float32
                )
                * 0.125
            )
            key_part = (
                jnp.einsum("hqk,qhe->khe", score_grad, queries, preferred_element_type=jnp.float32)
                * 0.125
            )
            value_part = jnp.einsum(
                "hqk,qhe->khe", to_low(chances), grad_out, preferred_element_type=jnp.float32
            )
            key_grads = lax.dynamic_update_slice_in_dim(key_grads, key_part, block * rows, 0)
            value_grads = lax.dynamic_update_slice_in_dim(value_grads, value_part, block * rows, 0)
            return (query_grad, key_grads, value_grads)

        live = block_live(query_ids, key_ids, offset, block, rows, causal)
        return lax.cond(live, step_compute, lambda state: state, carry)

    initial = (
        jnp.zeros(queries.shape, jnp.float32),
        jnp.zeros(keys_all.shape, jnp.float32),
        jnp.zeros(values_all.shape, jnp.float32),
    )
    return lax.fori_loop(0, count, step_block, initial)


def attention_back(
    queries, keys_all, values_all, query_ids, key_ids_all, causal, grad_out, output, log_total
):
    rows = queries.shape[0]
    offset = lax.axis_index("seq") * rows
    settle = jnp.einsum("qhe,qhe->hq", grad_out.astype(jnp.float32), output)
    query_grad, key_terms, value_terms = attend_backward(
        queries,
        keys_all,
        values_all,
        query_ids,
        key_ids_all,
        offset,
        causal,
        grad_out,
        settle,
        log_total,
    )
    key_sum, value_sum = (
        lax.psum_scatter(
            key_terms.reshape(key_terms.shape[0], -1).astype(jnp.bfloat16),
            "seq",
            scatter_dimension=0,
            tiled=True,
        ).astype(jnp.float32),
        lax.psum_scatter(
            value_terms.reshape(value_terms.shape[0], -1).astype(jnp.bfloat16),
            "seq",
            scatter_dimension=0,
            tiled=True,
        ).astype(jnp.float32),
    )
    return (query_grad, key_sum, value_sum)


def shards(
    source,
    target,
    source_ids,
    target_ids,
    out_grad,
    enc_qkv,
    enc_out,
    enc_up,
    enc_up_bias,
    enc_down,
    enc_down_bias,
    enc_gain,
    enc_shift,
    dec_qkv,
    dec_out,
    cross_qkv,
    cross_out,
    dec_up,
    dec_up_bias,
    dec_down,
    dec_down_bias,
    dec_gain,
    dec_shift,
):
    src_rows = source[0]
    tgt_rows = target[0]
    src_ids = source_ids[0]
    tgt_ids = target_ids[0]
    rows = src_rows.shape[0]
    offset = lax.axis_index("seq") * rows
    enc_queries = to_low(matmul(src_rows, enc_qkv[0]))
    enc_keys = to_low(matmul(src_rows, enc_qkv[1]))
    enc_values = to_low(matmul(src_rows, enc_qkv[2]))
    enc_keys_all, enc_values_all, src_ids_all = (
        lax.all_gather(enc_keys, "seq", axis=0, tiled=True),
        lax.all_gather(enc_values, "seq", axis=0, tiled=True),
        lax.all_gather(src_ids, "seq", axis=0, tiled=True),
    )
    enc_att, enc_lse = attend_forward(
        split_heads(enc_queries),
        split_heads(enc_keys_all),
        split_heads(enc_values_all),
        src_ids,
        src_ids_all,
        offset,
        False,
    )
    enc_att_low = to_low(enc_att.reshape(rows, -1))
    enc_pre = src_rows.astype(jnp.float32) + matmul(enc_att_low, enc_out)
    hidden = layer_norm(enc_pre, enc_gain[0], enc_shift[0])
    hidden_low = to_low(hidden)
    enc_inner = matmul(hidden_low, enc_up) + enc_up_bias
    enc_act = to_low(jax.nn.gelu(enc_inner))
    enc_last = hidden + matmul(enc_act, enc_down) + enc_down_bias
    memory = layer_norm(enc_last, enc_gain[1], enc_shift[1])
    memory_low = to_low(memory)
    mem_keys = to_low(matmul(memory_low, cross_qkv[1]))
    mem_values = to_low(matmul(memory_low, cross_qkv[2]))
    mem_keys_all, mem_values_all = (
        lax.all_gather(mem_keys, "seq", axis=0, tiled=True),
        lax.all_gather(mem_values, "seq", axis=0, tiled=True),
    )
    dec_queries = to_low(matmul(tgt_rows, dec_qkv[0]))
    dec_keys = to_low(matmul(tgt_rows, dec_qkv[1]))
    dec_values = to_low(matmul(tgt_rows, dec_qkv[2]))
    dec_keys_all, dec_values_all, tgt_ids_all = (
        lax.all_gather(dec_keys, "seq", axis=0, tiled=True),
        lax.all_gather(dec_values, "seq", axis=0, tiled=True),
        lax.all_gather(tgt_ids, "seq", axis=0, tiled=True),
    )
    dec_att, dec_lse = attend_forward(
        split_heads(dec_queries),
        split_heads(dec_keys_all),
        split_heads(dec_values_all),
        tgt_ids,
        tgt_ids_all,
        offset,
        True,
    )
    dec_att_low = to_low(dec_att.reshape(rows, -1))
    dec_pre = tgt_rows.astype(jnp.float32) + matmul(dec_att_low, dec_out)
    first = layer_norm(dec_pre, dec_gain[0], dec_shift[0])
    first_low = to_low(first)
    cross_queries = to_low(matmul(first_low, cross_qkv[0]))
    cross_att, cross_lse = attend_forward(
        split_heads(cross_queries),
        split_heads(mem_keys_all),
        split_heads(mem_values_all),
        tgt_ids,
        src_ids_all,
        offset,
        False,
    )
    cross_att_low = to_low(cross_att.reshape(rows, -1))
    cross_pre = first + matmul(cross_att_low, cross_out)
    second = layer_norm(cross_pre, dec_gain[1], dec_shift[1])
    second_low = to_low(second)
    dec_inner = matmul(second_low, dec_up) + dec_up_bias
    dec_act = to_low(jax.nn.gelu(dec_inner))
    dec_last = second + matmul(dec_act, dec_down) + dec_down_bias
    decoded = layer_norm(dec_last, dec_gain[2], dec_shift[2])
    upstream = out_grad[0].astype(jnp.float32)
    grad_last, gain_two, shift_two = norm_back(dec_last, dec_gain[2], dec_shift[2], upstream)
    branch_low = to_low(grad_last)
    dec_down_g = weight_grad(dec_act, branch_low)
    dec_down_bias_g = jnp.sum(branch_low.astype(jnp.float32), axis=0)
    inner_low = to_low(gelu_back(dec_inner, input_grad(branch_low, dec_down)))
    dec_up_g = weight_grad(second_low, inner_low)
    dec_up_bias_g = jnp.sum(inner_low.astype(jnp.float32), axis=0)
    grad_second = grad_last + input_grad(inner_low, dec_up)
    grad_cross_pre, gain_one, shift_one = norm_back(
        cross_pre, dec_gain[1], dec_shift[1], grad_second
    )
    mixed_low = to_low(grad_cross_pre)
    cross_out_g = weight_grad(cross_att_low, mixed_low)
    cross_att_grad = to_low(input_grad(mixed_low, cross_out))
    cross_query_grad, mem_key_sum, mem_value_sum = attention_back(
        split_heads(cross_queries),
        split_heads(mem_keys_all),
        split_heads(mem_values_all),
        tgt_ids,
        src_ids_all,
        False,
        split_heads(cross_att_grad),
        cross_att,
        cross_lse,
    )
    mem_key_low = to_low(mem_key_sum)
    mem_value_low = to_low(mem_value_sum)
    cross_query_low = to_low(cross_query_grad.reshape(rows, -1))
    cross_qkv_g = jnp.stack(
        [
            weight_grad(first_low, cross_query_low),
            weight_grad(memory_low, mem_key_low),
            weight_grad(memory_low, mem_value_low),
        ]
    )
    grad_first = grad_cross_pre + input_grad(cross_query_low, cross_qkv[0])
    grad_dec_pre, gain_zero, shift_zero = norm_back(dec_pre, dec_gain[0], dec_shift[0], grad_first)
    self_low = to_low(grad_dec_pre)
    dec_out_g = weight_grad(dec_att_low, self_low)
    dec_att_grad = to_low(input_grad(self_low, dec_out))
    dec_query_grad, dec_key_sum, dec_value_sum = attention_back(
        split_heads(dec_queries),
        split_heads(dec_keys_all),
        split_heads(dec_values_all),
        tgt_ids,
        tgt_ids_all,
        True,
        split_heads(dec_att_grad),
        dec_att,
        dec_lse,
    )
    dec_query_low = to_low(dec_query_grad.reshape(rows, -1))
    dec_key_low = to_low(dec_key_sum)
    dec_value_low = to_low(dec_value_sum)
    dec_qkv_g = jnp.stack(
        [
            weight_grad(tgt_rows, dec_query_low),
            weight_grad(tgt_rows, dec_key_low),
            weight_grad(tgt_rows, dec_value_low),
        ]
    )
    tgt_grad = (
        grad_dec_pre
        + input_grad(dec_query_low, dec_qkv[0])
        + input_grad(dec_key_low, dec_qkv[1])
        + input_grad(dec_value_low, dec_qkv[2])
    )
    dec_gain_g = jnp.stack([gain_zero, gain_one, gain_two])
    dec_shift_g = jnp.stack([shift_zero, shift_one, shift_two])
    grad_memory = input_grad(mem_key_low, cross_qkv[1]) + input_grad(mem_value_low, cross_qkv[2])
    grad_enc_last, enc_gain_one, enc_shift_one = norm_back(
        enc_last, enc_gain[1], enc_shift[1], grad_memory
    )
    enc_branch_low = to_low(grad_enc_last)
    enc_down_g = weight_grad(enc_act, enc_branch_low)
    enc_down_bias_g = jnp.sum(enc_branch_low.astype(jnp.float32), axis=0)
    enc_inner_low = to_low(gelu_back(enc_inner, input_grad(enc_branch_low, enc_down)))
    enc_up_g = weight_grad(hidden_low, enc_inner_low)
    enc_up_bias_g = jnp.sum(enc_inner_low.astype(jnp.float32), axis=0)
    grad_hidden = grad_enc_last + input_grad(enc_inner_low, enc_up)
    grad_enc_pre, enc_gain_zero, enc_shift_zero = norm_back(
        enc_pre, enc_gain[0], enc_shift[0], grad_hidden
    )
    enc_mixed_low = to_low(grad_enc_pre)
    enc_out_g = weight_grad(enc_att_low, enc_mixed_low)
    enc_att_grad = to_low(input_grad(enc_mixed_low, enc_out))
    enc_query_grad, enc_key_sum, enc_value_sum = attention_back(
        split_heads(enc_queries),
        split_heads(enc_keys_all),
        split_heads(enc_values_all),
        src_ids,
        src_ids_all,
        False,
        split_heads(enc_att_grad),
        enc_att,
        enc_lse,
    )
    enc_query_low = to_low(enc_query_grad.reshape(rows, -1))
    enc_key_low = to_low(enc_key_sum)
    enc_value_low = to_low(enc_value_sum)
    enc_qkv_g = jnp.stack(
        [
            weight_grad(src_rows, enc_query_low),
            weight_grad(src_rows, enc_key_low),
            weight_grad(src_rows, enc_value_low),
        ]
    )
    src_grad = (
        grad_enc_pre
        + input_grad(enc_query_low, enc_qkv[0])
        + input_grad(enc_key_low, enc_qkv[1])
        + input_grad(enc_value_low, enc_qkv[2])
    )
    enc_gain_g = jnp.stack([enc_gain_zero, enc_gain_one])
    enc_shift_g = jnp.stack([enc_shift_zero, enc_shift_one])
    all_rows = (
        lax.psum_scatter(
            enc_qkv_g.astype(jnp.bfloat16), "seq", scatter_dimension=1, tiled=True
        ).astype(jnp.float32),
        lax.psum_scatter(
            enc_out_g.astype(jnp.bfloat16), "seq", scatter_dimension=0, tiled=True
        ).astype(jnp.float32),
        lax.psum_scatter(
            enc_up_g.astype(jnp.bfloat16), "seq", scatter_dimension=0, tiled=True
        ).astype(jnp.float32),
        lax.psum_scatter(
            enc_down_g.astype(jnp.bfloat16), "seq", scatter_dimension=0, tiled=True
        ).astype(jnp.float32),
        lax.psum_scatter(
            dec_qkv_g.astype(jnp.bfloat16), "seq", scatter_dimension=1, tiled=True
        ).astype(jnp.float32),
        lax.psum_scatter(
            dec_out_g.astype(jnp.bfloat16), "seq", scatter_dimension=0, tiled=True
        ).astype(jnp.float32),
        lax.psum_scatter(
            cross_qkv_g.astype(jnp.bfloat16), "seq", scatter_dimension=1, tiled=True
        ).astype(jnp.float32),
        lax.psum_scatter(
            cross_out_g.astype(jnp.bfloat16), "seq", scatter_dimension=0, tiled=True
        ).astype(jnp.float32),
        lax.psum_scatter(
            dec_up_g.astype(jnp.bfloat16), "seq", scatter_dimension=0, tiled=True
        ).astype(jnp.float32),
        lax.psum_scatter(
            dec_down_g.astype(jnp.bfloat16), "seq", scatter_dimension=0, tiled=True
        ).astype(jnp.float32),
    )
    reduced = (
        lax.psum_scatter(
            all_rows[0].astype(jnp.bfloat16), "batch", scatter_dimension=2, tiled=True
        ).astype(jnp.float32),
        lax.psum_scatter(
            all_rows[1].astype(jnp.bfloat16), "batch", scatter_dimension=1, tiled=True
        ).astype(jnp.float32),
        lax.psum_scatter(
            all_rows[2].astype(jnp.bfloat16), "batch", scatter_dimension=1, tiled=True
        ).astype(jnp.float32),
        lax.psum_scatter(
            all_rows[3].astype(jnp.bfloat16), "batch", scatter_dimension=1, tiled=True
        ).astype(jnp.float32),
        lax.psum_scatter(
            all_rows[4].astype(jnp.bfloat16), "batch", scatter_dimension=2, tiled=True
        ).astype(jnp.float32),
        lax.psum_scatter(
            all_rows[5].astype(jnp.bfloat16), "batch", scatter_dimension=1, tiled=True
        ).astype(jnp.float32),
        lax.psum_scatter(
            all_rows[6].astype(jnp.bfloat16), "batch", scatter_dimension=2, tiled=True
        ).astype(jnp.float32),
        lax.psum_scatter(
            all_rows[7].astype(jnp.bfloat16), "batch", scatter_dimension=1, tiled=True
        ).astype(jnp.float32),
        lax.psum_scatter(
            all_rows[8].astype(jnp.bfloat16), "batch", scatter_dimension=1, tiled=True
        ).astype(jnp.float32),
        lax.psum_scatter(
            all_rows[9].astype(jnp.bfloat16), "batch", scatter_dimension=1, tiled=True
        ).astype(jnp.float32),
    )
    vectors = lax.psum(
        (
            enc_up_bias_g,
            enc_down_bias_g,
            enc_gain_g,
            enc_shift_g,
            dec_up_bias_g,
            dec_down_bias_g,
            dec_gain_g,
            dec_shift_g,
        ),
        ("batch", "seq"),
    )
    return (
        to_low(decoded)[None],
        to_low(src_grad)[None],
        to_low(tgt_grad)[None],
        reduced[0],
        reduced[1],
        reduced[2],
        vectors[0],
        reduced[3],
        vectors[1],
        vectors[2],
        vectors[3],
        reduced[4],
        reduced[5],
        reduced[6],
        reduced[7],
        reduced[8],
        vectors[4],
        reduced[9],
        vectors[5],
        vectors[6],
        vectors[7],
    )


def solution(mesh):
    placed = (
        P("batch", "seq", None),
        P("batch", "seq", None),
        P("batch", "seq"),
        P("batch", "seq"),
        P("batch", "seq", None),
        P(),
        P(),
        P(),
        P(),
        P(),
        P(),
        P(),
        P(),
        P(),
        P(),
        P(),
        P(),
        P(),
        P(),
        P(),
        P(),
        P(),
        P(),
    )
    return jax.shard_map(
        shards,
        mesh=mesh,
        in_specs=placed,
        out_specs=(
            P("batch", "seq", None),
            P("batch", "seq", None),
            P("batch", "seq", None),
            P(None, "seq", "batch"),
            P("seq", "batch"),
            P("seq", "batch"),
            P(),
            P("seq", "batch"),
            P(),
            P(),
            P(),
            P(None, "seq", "batch"),
            P("seq", "batch"),
            P(None, "seq", "batch"),
            P("seq", "batch"),
            P("seq", "batch"),
            P(),
            P("seq", "batch"),
            P(),
            P(),
            P(),
        ),
        check_vma=False,
    )
```

profile of v0, /device:TPU:2, one launch (start us, length us, event | category | flops | bytes accessed | tf_op | source)
XLA Modules:
  0.0 1278.2 jit_solution(16573159433307106147)
XLA Ops:
  24.9 4.3 all-gather.1
  29.2 4.5 all-gather
  39.4 16.4 %while.185 = (s32[]{:T(128)}, f32[8,512]{1,0:T(8,128)S(1)}, f32[8,512]{1,0:T(8,128)S(1)}, s32[1024]{0:T(1024)S(1)}, s32[512]{0:T(512)S(1)}, /*index=5*/s32[1,512...) while((s32[]{:T(128)}, f32[8,512]{1,0:T(8,128)S(1)}, ...), condition=%wide.region_17.0_spmd, body=%wide.region_12.17_spmd.sunk | while | flops 285483008 | bytes 18833856 | solution.py:100
  42.6 5.0 conditional.20
  50.8 4.9 conditional.20
  59.2 18.1 %while.186 = (s32[]{:T(128)}, f32[512,8,64]{0,2,1:T(8,128)}, s32[1024]{0:T(1024)S(1)}, s32[512]{0:T(512)S(1)}, bf16[1024,8,64]{0,2,1:T(8,128)(2,1)}, /*index=5*/...) while((s32[]{:T(128)}, f32[512,8,64]{0,2,1:T(8,128)}, ...), condition=%wide.region_21.22_spmd, body=%wide.region_18.21_spmd.sunk | while | flops 547880960 | bytes 4220333 | solution.py:118
  62.4 5.9 conditional.21
  62.7 5.6 fusion.43
  71.5 5.8 conditional.21
  71.8 5.5 fusion.43
  89.2 16.9 %while.183 = (s32[]{:T(128)}, f32[8,512]{1,0:T(8,128)S(1)}, f32[8,512]{1,0:T(8,128)S(1)}, s32[1024]{0:T(1024)S(1)}, s32[512]{0:T(512)S(1)}, /*index=5*/s32[]{:T(...) while((s32[]{:T(128)}, f32[8,512]{1,0:T(8,128)S(1)}, ...), condition=%wide.region_5.6_spmd, body=%wide.region_0.5_spmd.sunk | while | flops 286008320 | bytes 18842092 | solution.py:100
  92.9 5.0 conditional.18
  101.1 5.0 conditional.18
  113.6 18.3 %while.184 = (s32[]{:T(128)}, f32[512,8,64]{0,2,1:T(8,128)}, s32[1024]{0:T(1024)S(1)}, s32[512]{0:T(512)S(1)}, s32[]{:T(128)}, /*index=5*/bf16[1024,8,64]{0,2,1:...) while((s32[]{:T(128)}, f32[512,8,64]{0,2,1:T(8,128)}, ...), condition=%wide.region_9.10_spmd, body=%wide.region_6.9_spmd.sunk | while | flops 548406272 | bytes 4228569 | solution.py:118
  116.8 6.0 conditional.19
  117.2 5.6 fusion.16
  126.0 5.9 conditional.19
  126.4 5.5 fusion.16
  145.0 16.3 %while.187 = (s32[]{:T(128)}, f32[8,512]{1,0:T(8,128)S(1)}, f32[8,512]{1,0:T(8,128)S(1)}, s32[1024]{0:T(1024)S(1)}, s32[512]{0:T(512)S(1)}, /*index=5*/s32[1,512...) while((s32[]{:T(128)}, f32[8,512]{1,0:T(8,128)S(1)}, ...), condition=%wide.region_31.32_spmd, body=%wide.region_26.31_spmd.sunk | while | flops 285483008 | bytes 18833856 | solution.py:100
  148.2 5.0 conditional.22
  156.4 4.9 conditional.22
  164.9 18.1 %while.188 = (s32[]{:T(128)}, f32[512,8,64]{0,2,1:T(8,128)}, s32[1024]{0:T(1024)S(1)}, s32[512]{0:T(512)S(1)}, bf16[1024,8,64]{0,2,1:T(8,128)(2,1)}, /*index=5*/...) while((s32[]{:T(128)}, f32[512,8,64]{0,2,1:T(8,128)}, ...), condition=%wide.region_35.36_spmd, body=%wide.region_32.35_spmd.sunk | while | flops 547880960 | bytes 4220333 | solution.py:118
  168.0 5.9 conditional.23
  168.3 5.5 fusion.70
  176.9 5.9 conditional.23
  177.3 5.5 fusion.70
  194.4 4.4 convert_reduce_fusion
  204.5 27.9 %while.189 = (s32[]{:T(128)}, f32[512,8,64]{0,2,1:T(8,128)S(1)}, bf16[1024,8,64]{0,2,1:T(8,128)(2,1)}, bf16[1024,8,64]{0,2,1:T(8,128)(2,1)}, s32[1024]{0:T(1024)...) while((s32[]{:T(128)}, f32[512,8,64]{0,2,1:T(8,128)S(1)}, ...), condition=%wide.region_47.48_spmd, body=%wide.region_44.0_spmd.sunk | while | flops 1368391680 | bytes 67429048 | solution.py:167
  207.8 10.8 conditional.24
  221.6 10.8 conditional.24
  233.3 3.3 multiply_reduce_fusion.1
  240.7 28.6 %while.191 = (s32[]{:T(128)}, f32[512,8,64]{0,2,1:T(8,128)S(1)}, bf16[1024,8,64]{0,2,1:T(8,128)(2,1)}, bf16[1024,8,64]{0,2,1:T(8,128)(2,1)}, s32[1024]{0:T(1024)...) while((s32[]{:T(128)}, f32[512,8,64]{0,2,1:T(8,128)S(1)}, ...), condition=%wide.region_65.66_spmd, body=%wide.region_62.65_spmd.sunk | while | flops 1368916992 | bytes 69534472 | solution.py:167
  244.4 10.8 conditional.26
  258.4 10.8 conditional.26
  262.5 3.1 fusion.137
  280.5 4.0 convert_reduce_fusion.1
  290.3 27.9 %while.190 = (s32[]{:T(128)}, f32[512,8,64]{0,2,1:T(8,128)S(1)}, bf16[1024,8,64]{0,2,1:T(8,128)(2,1)}, bf16[1024,8,64]{0,2,1:T(8,128)(2,1)}, s32[1024]{0:T(1024)...) while((s32[]{:T(128)}, f32[512,8,64]{0,2,1:T(8,128)S(1)}, ...), condition=%wide.region_57.58_spmd, body=%wide.region_54.0_spmd.sunk | while | flops 1368391680 | bytes 69526232 | solution.py:167
  293.5 10.7 conditional.25
  307.4 10.8 conditional.25
  326.9 4.3 convolution_convert_fusion.1
  331.3 5.8 convolution_convert_fusion
  345.0 4.3 convolution_convert_fusion.3
  349.4 5.8 convolution_convert_fusion.2
  359.6 17.5 %reduce-scatter.44.cloned.1.call-done = bf16[512,512]{0,1:T(8,128)(2,1)} async-done(((bf16[1024,512]{0,1:T(8,128)(2,1)}), bf16[512,512]{0,1:T(8,128)(2,1)}) %reduce-scatter.44.cloned.1.call-update) | async-done | bytes 524304 | tf_op jit(solution)/shard_map/reduce_scatter | solution.py:189
  378.6 21.1 %reduce-scatter.46.cloned.1.call-done = bf16[512,512]{0,1:T(8,128)(2,1)} async-done(((bf16[1024,512]{0,1:T(8,128)(2,1)}), bf16[512,512]{0,1:T(8,128)(2,1)}) %reduce-scatter.46.cloned.1.call-update) | async-done | bytes 524304 | tf_op jit(solution)/shard_map/reduce_scatter | solution.py:195
  402.6 14.3 %reduce-scatter.56.cloned.1.call-done = bf16[256,512]{1,0:T(8,128)(2,1)} async-done(((bf16[512,512]{1,0:T(8,128)(2,1)}), bf16[256,512]{1,0:T(8,128)(2,1)}) %reduce-scatter.56.cloned.1.call-update) | async-done | bytes 262160 | tf_op jit(solution)/shard_map/reduce_scatter | solution.py:427
  418.8 26.4 %reduce-scatter.68.cloned.1.call-done = bf16[3,256,512]{2,1,0:T(8,128)(2,1)} async-done(((bf16[3,512,512]{2,1,0:T(8,128)(2,1)}), bf16[3,256,512]{2,1,0:T(8,128)(2,1)}) %reduce-scatter.68.cloned.1.call-update) | async-done | bytes 786448 | tf_op jit(solution)/shard_map/reduce_scatter | solution.py:442
  447.6 31.5 %reduce-scatter.72.cloned.1.call-done = bf16[256,2048]{1,0:T(8,128)(2,1)} async-done(((bf16[512,2048]{1,0:T(8,128)(2,1)}), bf16[256,2048]{1,0:T(8,128)(2,1)}) %reduce-scatter.72.cloned.1.call-update) | async-done | bytes 1048592 | tf_op jit(solution)/shard_map/reduce_scatter | solution.py:448
  481.5 31.7 %reduce-scatter.74.cloned.1.call-done = bf16[1024,512]{1,0:T(8,128)(2,1)} async-done(((bf16[2048,512]{1,0:T(8,128)(2,1)}), bf16[1024,512]{1,0:T(8,128)(2,1)}) %reduce-scatter.74.cloned.1.call-update) | async-done | bytes 1048592 | tf_op jit(solution)/shard_map/reduce_scatter | solution.py:451
  515.5 26.0 %reduce-scatter.62.cloned.1.call-done = bf16[3,256,512]{1,2,0:T(8,128)(2,1)} async-done(((bf16[3,512,512]{1,2,0:T(8,128)(2,1)}), bf16[3,256,512]{1,2,0:T(8,128)(2,1)}) %reduce-scatter.62.cloned.1.call-update) | async-done | bytes 786448 | tf_op jit(solution)/shard_map/reduce_scatter | solution.py:436
  541.6 33.9 %reduce-scatter.58.cloned.1.call-done = bf16[256,2048]{1,0:T(8,128)(2,1)} async-done(((bf16[512,2048]{1,0:T(8,128)(2,1)}), bf16[256,2048]{1,0:T(8,128)(2,1)}) %reduce-scatter.58.cloned.1.call-update) | async-done | bytes 1048592 | tf_op jit(solution)/shard_map/reduce_scatter | solution.py:430
  577.9 31.8 %reduce-scatter.60.cloned.1.call-done = bf16[1024,512]{1,0:T(8,128)(2,1)} async-done(((bf16[2048,512]{1,0:T(8,128)(2,1)}), bf16[1024,512]{1,0:T(8,128)(2,1)}) %reduce-scatter.60.cloned.1.call-update) | async-done | bytes 1048592 | tf_op jit(solution)/shard_map/reduce_scatter | solution.py:433
  617.2 52.9 %reduce-scatter.84.cloned.1.call-done = bf16[32,256]{1,0:T(8,128)(2,1)} async-done(((bf16[512,256]{1,0:T(8,128)(2,1)}), bf16[32,256]{1,0:T(8,128)(2,1)}) %reduce-scatter.84.cloned.1.call-update) | async-done | bytes 16400
  671.7 56.8 %reduce-scatter.82.cloned.1.call-done = bf16[32,256]{1,0:T(8,128)(2,1)} async-done(((bf16[512,256]{1,0:T(8,128)(2,1)}), bf16[32,256]{1,0:T(8,128)(2,1)}) %reduce-scatter.82.cloned.1.call-update) | async-done | bytes 16400
  732.0 22.6 %reduce-scatter.52.cloned.1.call-done = bf16[3,256,512]{1,2,0:T(8,128)(2,1)} async-done(((bf16[3,512,512]{1,2,0:T(8,128)(2,1)}), bf16[3,256,512]{1,2,0:T(8,128)(2,1)}) %reduce-scatter.52.cloned.1.call-update) | async-done | bytes 786448 | tf_op jit(solution)/shard_map/reduce_scatter | solution.py:424
  759.0 42.5 %all-reduce.1 = (f32[2048]{0:T(1024)}, f32[512]{0:T(512)}, f32[2,512]{1,0:T(2,128)}, f32[2,512]{1,0:T(2,128)}, f32[2048]{0:T(1024)}, /*index=5*/f32[512]{0:T(512)}, f32[3,512]{1,0:T(4,128)}, f32[3,512]{1,0:T(4,128)}) all-reduce(f32[2048]{0:T(1024)S(1)} %get-tuple-element.3983, ...), channel_id=1, replica_groups=mesh['batch'=16,'seq'=2] {'batch','seq'}, use_global_device_ids=true, to_apply=%region_75.76 | all-reduce | flops 10240 | bytes 81920 | tf_op jit(solution)/shard_map/psum | solution.py:487
  803.0 11.6 reduce-scatter.76.cloned.1.call-done
  820.5 89.9 %all-reduce.4.cloned.1.call-done = bf16[3,256,512]{1,0,2:T(4,128)(2,1)} async-done(((bf16[3,256,512]{1,0,2:T(4,128)(2,1)}), bf16[3,256,512]{1,0,2:T(4,128)(2,1)}) %all-reduce.4.cloned.1.call-update) | async-done | bytes 786448
  911.9 58.6 %reduce-scatter.86.cloned.1.call-done = bf16[128,256]{1,0:T(8,128)(2,1)} async-done(((bf16[2048,256]{1,0:T(8,128)(2,1)}), bf16[128,256]{1,0:T(8,128)(2,1)}) %reduce-scatter.86.cloned.1.call-update) | async-done | bytes 65552
  972.1 58.8 %reduce-scatter.88.cloned.1.call-done = bf16[32,1024]{1,0:T(8,128)(2,1)} async-done(((bf16[512,1024]{1,0:T(8,128)(2,1)}), bf16[32,1024]{1,0:T(8,128)(2,1)}) %reduce-scatter.88.cloned.1.call-update) | async-done | bytes 65552
  1032.7 57.4 %reduce-scatter.64.cloned.1.call-done = bf16[3,256,32]{1,2,0:T(8,128)(2,1)} async-done(((bf16[3,256,512]{1,2,0:T(8,128)(2,1)}), bf16[3,256,32]{1,2,0:T(8,128)(2,1)}) %reduce-scatter.64.cloned.1.call-update) | async-done | bytes 49168 | tf_op jit(solution)/shard_map/reduce_scatter | solution.py:468
  1091.5 58.8 %reduce-scatter.78.cloned.1.call-done = bf16[128,256]{1,0:T(8,128)(2,1)} async-done(((bf16[2048,256]{1,0:T(8,128)(2,1)}), bf16[128,256]{1,0:T(8,128)(2,1)}) %reduce-scatter.78.cloned.1.call-update) | async-done | bytes 65552
  1151.9 58.5 %reduce-scatter.80.cloned.1.call-done = bf16[32,1024]{1,0:T(8,128)(2,1)} async-done(((bf16[512,1024]{1,0:T(8,128)(2,1)}), bf16[32,1024]{1,0:T(8,128)(2,1)}) %reduce-scatter.80.cloned.1.call-update) | async-done | bytes 65552
  1212.2 57.7 %reduce-scatter.54.cloned.1.call-done = bf16[3,256,32]{1,2,0:T(8,128)(2,1)} async-done(((bf16[3,256,512]{1,2,0:T(8,128)(2,1)}), bf16[3,256,32]{1,2,0:T(8,128)(2,1)}) %reduce-scatter.54.cloned.1.call-update) | async-done | bytes 49168 | tf_op jit(solution)/shard_map/reduce_scatter | solution.py:456
  (666 shorter events, 275.0 us)
Async XLA Ops:
  7.2 181.7 %copy-start = (bf16[2048,512]{1,0:T(8,128)(2,1)S(1)}, bf16[2048,512]{1,0:T(8,128)(2,1)}, u32[]{:S(2)}) copy-start(bf16[2048,512]{1,0:T(8,128)(2,1)} %param.78) | copy-start | bytes 6291460
  7.2 29.8 %all-gather.15.cloned.1.call-start = ((), (), s32[]{:S(2)}) async-start(), calls=%async_computation.28 | async-start | bytes 1572864 | tf_op jit(solution)/shard_map/all_gather | solution.py:240
  9.9 45.9 %all-gather.13.cloned.1.call-start = ((), (), s32[]{:S(2)}) async-start(), calls=%async_computation.27 | async-start | bytes 1572864 | tf_op jit(solution)/shard_map/all_gather | solution.py:241
  12.4 74.4 %all-gather.11.cloned.1.call-start = ((), (), s32[]{:S(2)}) async-start(), calls=%async_computation.26 | async-start | bytes 1572864 | tf_op jit(solution)/shard_map/all_gather | solution.py:272
  14.8 14.4 %copy-start.40 = (s32[1,512]{1,0:T(1,128)S(1)}, s32[1,512]{1,0:T(1,128)}, u32[]{:S(2)}) copy-start(s32[1,512]{1,0:T(1,128)} %param.62) | copy-start | bytes 6148
  14.8 19.0 %copy-start.129 = (f32[2,512]{1,0:T(2,128)S(1)}, f32[2,512]{1,0:T(2,128)}, u32[]{:S(2)}) copy-start(f32[2,512]{1,0:T(2,128)} %param.70) | copy-start | bytes 12292
  14.8 19.0 %copy-start.130 = (f32[2,512]{1,0:T(2,128)S(1)}, f32[2,512]{1,0:T(2,128)}, u32[]{:S(2)}) copy-start(f32[2,512]{1,0:T(2,128)} %param.71) | copy-start | bytes 12292
  14.8 19.0 %copy-start.127 = (f32[3,512]{1,0:T(4,128)S(1)}, f32[3,512]{1,0:T(4,128)}, u32[]{:S(2)}) copy-start(f32[3,512]{1,0:T(4,128)} %param.80) | copy-start | bytes 18436
  14.8 19.6 %copy-start.128 = (f32[3,512]{1,0:T(4,128)S(1)}, f32[3,512]{1,0:T(4,128)}, u32[]{:S(2)}) copy-start(f32[3,512]{1,0:T(4,128)} %param.81) | copy-start | bytes 18436
  14.9 95.3 %all-gather.9.cloned.1.call-start = ((), (), s32[]{:S(2)}) async-start(), calls=%async_computation.25 | async-start | bytes 1572864 | tf_op jit(solution)/shard_map/all_gather | solution.py:273
  17.2 125.5 %all-gather.19.cloned.1.call-start = ((), (), s32[]{:S(2)}) async-start(), calls=%async_computation.30 | async-start | bytes 1572864 | tf_op jit(solution)/shard_map/all_gather | solution.py:265
  33.8 49.4 %copy-start.96 = (f32[1,512]{1,0:T(1,128)}, f32[1,512]{1,0:T(1,128)S(1)}, u32[]{:S(2)}) copy-start(f32[1,512]{1,0:T(1,128)S(1)} %get-tuple-element.4067) | copy-start | bytes 6148
  33.8 72.3 %copy-start.94 = (f32[1,512]{1,0:T(1,128)}, f32[1,512]{1,0:T(1,128)S(1)}, u32[]{:S(2)}) copy-start(f32[1,512]{1,0:T(1,128)S(1)} %get-tuple-element.4066) | copy-start | bytes 6148
  33.8 49.3 %copy-start.105 = (f32[1,512]{1,0:T(1,128)}, f32[1,512]{1,0:T(1,128)S(1)}, u32[]{:S(2)}) copy-start(f32[1,512]{1,0:T(1,128)S(1)} %get-tuple-element.4069) | copy-start | bytes 6148
  34.4 202.2 %copy-start.101 = (f32[1,512]{1,0:T(1,128)}, f32[1,512]{1,0:T(1,128)S(1)}, u32[]{:S(2)}) copy-start(f32[1,512]{1,0:T(1,128)S(1)} %get-tuple-element.4061) | copy-start | bytes 6148
  35.0 149.4 %copy-start.124 = (f32[1,512]{1,0:T(1,128)}, f32[1,512]{1,0:T(1,128)S(1)}, u32[]{:S(2)}) copy-start(f32[1,512]{1,0:T(1,128)S(1)} %get-tuple-element.4064) | copy-start | bytes 6148
  85.6 20.5 %copy-start.88 = (f32[512]{0:T(512)}, f32[512]{0:T(512)S(1)}, u32[]{:S(2)}) copy-start(f32[512]{0:T(512)S(1)} %broadcast_multiply_fusion.2) | copy-start | bytes 6148
  89.2 16.9 %copy-start.92 = (f32[512]{0:T(512)}, f32[512]{0:T(512)S(1)}, u32[]{:S(2)}) copy-start(f32[512]{0:T(512)S(1)} %fusion.258) | copy-start | bytes 6148
  107.6 29.3 %copy-start.34 = (bf16[512,512]{0,1:T(8,128)(2,1)}, bf16[512,512]{0,1:T(8,128)(2,1)S(1)}, u32[]{:S(2)}) copy-start(bf16[512,512]{0,1:T(8,128)(2,1)S(1)} %add_convert_fusion.1) | copy-start | bytes 1572868
  110.1 51.3 %all-gather.17.cloned.1.call-start = ((), (), s32[]{:S(2)}) async-start(), calls=%async_computation.29 | async-start | bytes 1572864 | tf_op jit(solution)/shard_map/all_gather | solution.py:266
  136.9 99.7 %copy-start.90 = (f32[512]{0:T(512)}, f32[512]{0:T(512)S(1)}, u32[]{:S(2)}) copy-start(f32[512]{0:T(512)S(1)} %broadcast_multiply_fusion.4) | copy-start | bytes 6148
  139.2 136.3 %reduce-scatter.40.cloned.1.call-start = ((), (), s32[]{:S(2)}) async-start(), calls=%async_computation.31 | async-start | bytes 1572864 | tf_op jit(solution)/shard_map/reduce_scatter | solution.py:189
  140.7 96.0 %copy-start.103 = (f32[512]{0:T(512)}, f32[512]{0:T(512)S(1)}, u32[]{:S(2)}) copy-start(f32[512]{0:T(512)S(1)} %fusion.256) | copy-start | bytes 6148
  187.1 14.1 %copy-start.24 = (f32[512,512]{0,1:T(8,128)}, f32[512,512]{0,1:T(8,128)S(1)}, u32[]{:S(2)}) copy-start(f32[512,512]{0,1:T(8,128)S(1)} %get-tuple-element.4079) | copy-start | bytes 3145732
  232.4 44.8 %reduce-scatter.42.cloned.1.call-start = ((), (), s32[]{:S(2)}) async-start(), calls=%async_computation.32 | async-start | bytes 1572864 | tf_op jit(solution)/shard_map/reduce_scatter | solution.py:195
  233.2 105.3 %reduce-scatter.48.cloned.1.call-start = ((), (), s32[]{:S(2)}) async-start(), calls=%async_computation.35 | async-start | bytes 1572864 | tf_op jit(solution)/shard_map/reduce_scatter | solution.py:189
  269.3 71.6 %reduce-scatter.50.cloned.1.call-start = ((), (), s32[]{:S(2)}) async-start(), calls=%async_computation.36 | async-start | bytes 1572864 | tf_op jit(solution)/shard_map/reduce_scatter | solution.py:195
  269.9 85.3 %reduce-scatter.70.cloned.1.call-start = ((), (), s32[]{:S(2)}) async-start(), calls=%async_computation.46 | async-start | bytes 786432 | tf_op jit(solution)/shard_map/reduce_scatter | solution.py:445
  273.1 84.1 %reduce-scatter.66.cloned.1.call-start = ((), (), s32[]{:S(2)}) async-start(), calls=%async_computation.44 | async-start | bytes 786432 | tf_op jit(solution)/shard_map/reduce_scatter | solution.py:439
  275.5 101.7 %reduce-scatter.44.cloned.1.call-start = ((), (), s32[]{:S(2)}) async-start(), calls=%async_computation.33 | async-start | bytes 1572864 | tf_op jit(solution)/shard_map/reduce_scatter | solution.py:189
  290.3 28.6 %copy-start.37 = (bf16[512,8,64]{0,2,1:T(8,128)(2,1)S(1)}, bf16[512,8,64]{0,2,1:T(8,128)(2,1)}, u32[]{:S(2)}) copy-start(bf16[512,8,64]{0,2,1:T(8,128)(2,1)} %copy-done.36) | copy-start | bytes 1572868
  318.2 81.4 %reduce-scatter.46.cloned.1.call-start = ((), (), s32[]{:S(2)}) async-start(), calls=%async_computation.34 | async-start | bytes 1572864 | tf_op jit(solution)/shard_map/reduce_scatter | solution.py:195
  318.8 98.1 %reduce-scatter.56.cloned.1.call-start = ((), (), s32[]{:S(2)}) async-start(), calls=%async_computation.39 | async-start | bytes 786432 | tf_op jit(solution)/shard_map/reduce_scatter | solution.py:427
  321.4 123.8 %reduce-scatter.68.cloned.1.call-start = ((), (), s32[]{:S(2)}) async-start(), calls=%async_computation.45 | async-start | bytes 2359296 | tf_op jit(solution)/shard_map/reduce_scatter | solution.py:442
  326.8 152.4 %reduce-scatter.72.cloned.1.call-start = ((), (), s32[]{:S(2)}) async-start(), calls=%async_computation.47 | async-start | bytes 3145728 | tf_op jit(solution)/shard_map/reduce_scatter | solution.py:448
  331.2 182.0 %reduce-scatter.74.cloned.1.call-start = ((), (), s32[]{:S(2)}) async-start(), calls=%async_computation.48 | async-start | bytes 3145728 | tf_op jit(solution)/shard_map/reduce_scatter | solution.py:451
  337.1 204.4 %reduce-scatter.62.cloned.1.call-start = ((), (), s32[]{:S(2)}) async-start(), calls=%async_computation.42 | async-start | bytes 2359296 | tf_op jit(solution)/shard_map/reduce_scatter | solution.py:436
  344.9 230.6 %reduce-scatter.58.cloned.1.call-start = ((), (), s32[]{:S(2)}) async-start(), calls=%async_computation.40 | async-start | bytes 3145728 | tf_op jit(solution)/shard_map/reduce_scatter | solution.py:430
  349.3 260.4 %reduce-scatter.60.cloned.1.call-start = ((), (), s32[]{:S(2)}) async-start(), calls=%async_computation.41 | async-start | bytes 3145728 | tf_op jit(solution)/shard_map/reduce_scatter | solution.py:433
  355.2 315.0 %reduce-scatter.84.cloned.1.call-start = ((), (), s32[]{:S(2)}) async-start(), calls=%async_computation.53 | async-start | bytes 278528
  357.1 371.4 %reduce-scatter.82.cloned.1.call-start = ((), (), s32[]{:S(2)}) async-start(), calls=%async_computation.52 | async-start | bytes 278528
  359.0 395.6 %reduce-scatter.52.cloned.1.call-start = ((), (), s32[]{:S(2)}) async-start(), calls=%async_computation.37 | async-start | bytes 2359296 | tf_op jit(solution)/shard_map/reduce_scatter | solution.py:424
  402.6 412.1 %reduce-scatter.76.cloned.1.call-start = ((), (), s32[]{:S(2)}) async-start(), calls=%async_computation.49 | async-start | bytes 278528
  418.7 491.6 %all-reduce.4.cloned.1.call-start = ((), (), s32[]{:S(2)}) async-start(), calls=%async_computation.56 | async-start | bytes 2097152
  447.5 522.9 %reduce-scatter.86.cloned.1.call-start = ((), (), s32[]{:S(2)}) async-start(), calls=%async_computation.54 | async-start | bytes 1114112
  481.4 549.5 %reduce-scatter.88.cloned.1.call-start = ((), (), s32[]{:S(2)}) async-start(), calls=%async_computation.55 | async-start | bytes 1114112
  515.5 96.8 %copy-start.141 = (u32[32]{0:T(128)S(1)}, u32[32]{0:T(128)}, u32[]{:S(2)}) copy-start(u32[32]{0:T(128)} %constant.761) | copy-start | bytes 388
  515.5 98.1 %copy-start.27 = (bf16[1,512,512]{1,2,0:T(8,128)(2,1)S(1)}, bf16[1,512,512]{1,2,0:T(8,128)(2,1)}, u32[]{:S(2)}) copy-start(bf16[1,512,512]{1,2,0:T(8,128)(2,1)} %copy.155) | copy-start | bytes 1572868
  515.5 98.2 %copy-start.59 = (bf16[1,512,512]{1,2,0:T(8,128)(2,1)S(1)}, bf16[1,512,512]{1,2,0:T(8,128)(2,1)}, u32[]{:S(2)}) copy-start(bf16[1,512,512]{1,2,0:T(8,128)(2,1)} %get-tuple-element.4059) | copy-start | bytes 1572868
  515.5 574.6 %reduce-scatter.64.cloned.1.call-start = ((), (), s32[]{:S(2)}) async-start(), calls=%async_computation.43 | async-start | bytes 835584 | tf_op jit(solution)/shard_map/reduce_scatter | solution.py:468
  541.5 73.2 %copy-start.119 = (f32[512]{0:T(512)S(1)}, f32[512]{0:T(512)}, u32[]{:S(2)}) copy-start(f32[512]{0:T(512)} %get-tuple-element.3769) | copy-start | bytes 6148
  541.5 73.2 %copy-start.120 = (f32[512]{0:T(512)S(1)}, f32[512]{0:T(512)}, u32[]{:S(2)}) copy-start(f32[512]{0:T(512)} %get-tuple-element.3761) | copy-start | bytes 6148
  541.5 73.2 %copy-start.121 = (f32[512]{0:T(512)S(1)}, f32[512]{0:T(512)}, u32[]{:S(2)}) copy-start(f32[512]{0:T(512)} %get-tuple-element.3773) | copy-start | bytes 6148
  541.5 73.2 %copy-start.131 = (f32[512]{0:T(512)S(1)}, f32[512]{0:T(512)}, u32[]{:S(2)}) copy-start(f32[512]{0:T(512)} %get-tuple-element.3763) | copy-start | bytes 6148
  541.5 73.2 %copy-start.132 = (f32[512]{0:T(512)S(1)}, f32[512]{0:T(512)}, u32[]{:S(2)}) copy-start(f32[512]{0:T(512)} %get-tuple-element.3774) | copy-start | bytes 6148
  541.5 73.2 %copy-start.21 = (f32[512,512]{0,1:T(8,128)S(1)}, f32[512,512]{0,1:T(8,128)}, u32[]{:S(2)}) copy-start(f32[512,512]{0,1:T(8,128)} %copy-done.19) | copy-start | bytes 3145732
  541.6 608.7 %reduce-scatter.78.cloned.1.call-start = ((), (), s32[]{:S(2)}) async-start(), calls=%async_computation.50 | async-start | bytes 1114112
  577.9 632.6 %reduce-scatter.80.cloned.1.call-start = ((), (), s32[]{:S(2)}) async-start(), calls=%async_computation.51 | async-start | bytes 1114112
  612.0 658.0 %reduce-scatter.54.cloned.1.call-start = ((), (), s32[]{:S(2)}) async-start(), calls=%async_computation.38 | async-start | bytes 835584 | tf_op jit(solution)/shard_map/reduce_scatter | solution.py:456
  613.7 140.9 %copy-start.56 = (bf16[512,512]{0,1:T(8,128)(2,1)S(1)}, bf16[512,512]{0,1:T(8,128)(2,1)}, u32[]{:S(2)}) copy-start(bf16[512,512]{0,1:T(8,128)(2,1)} %reduce-scatter.50.cloned.1.call-done) | copy-start | bytes 1572868
  617.2 141.7 %copy-start.122 = (f32[2048]{0:T(1024)S(1)}, f32[2048]{0:T(1024)}, u32[]{:S(2)}) copy-start(f32[2048]{0:T(1024)} %get-tuple-element.3979) | copy-start | bytes 24580
  617.2 141.8 %copy-start.123 = (f32[512]{0:T(512)S(1)}, f32[512]{0:T(512)}, u32[]{:S(2)}) copy-start(f32[512]{0:T(512)} %get-tuple-element.3977) | copy-start | bytes 6148
  617.2 184.3 %copy-start.23 = (f32[512,512]{0,1:T(8,128)S(1)}, f32[512,512]{0,1:T(8,128)}, u32[]{:S(2)}) copy-start(f32[512,512]{0,1:T(8,128)} %copy-done.22) | copy-start | bytes 3145732
  815.5 455.9 %copy-start.1 = (bf16[2048,512]{1,0:T(8,128)(2,1)S(1)}, bf16[2048,512]{1,0:T(8,128)(2,1)}, u32[]{:S(2)}) copy-start(bf16[2048,512]{1,0:T(8,128)(2,1)} %param.78) | copy-start | bytes 6291460
  (129 other events, 466.2 us)
Sparse Core Ops, SparseCore 0:
  10.2 21.4 all-gather.14
  33.7 21.3 all-gather.12
  56.7 21.3 all-gather.10
  79.4 21.2 all-gather.8
  110.2 21.4 all-gather.18
  139.4 21.4 all-gather.16
  232.5 20.4 reduce-scatter.39
  255.3 20.3 reduce-scatter.41
  277.9 20.3 reduce-scatter.47
  300.5 20.3 reduce-scatter.49
  323.2 14.5 reduce-scatter.69
  339.9 14.5 reduce-scatter.65
  356.8 20.3 reduce-scatter.43
  379.3 20.3 reduce-scatter.45
  402.3 14.5 reduce-scatter.55
  419.1 26.0 reduce-scatter.67
  447.3 31.8 reduce-scatter.71
  481.3 31.8 reduce-scatter.73
  515.4 26.0 reduce-scatter.61
  543.7 31.8 reduce-scatter.57
  577.8 31.8 reduce-scatter.59
  613.6 56.4 reduce-scatter.83
  674.1 54.3 reduce-scatter.81
  730.7 23.9 reduce-scatter.51
  758.1 56.4 reduce-scatter.75
  818.0 92.3 all-reduce.3
  913.8 56.5 reduce-scatter.85
  974.5 56.3 reduce-scatter.87
  1034.5 55.5 reduce-scatter.63
  1094.0 56.2 reduce-scatter.77
  1153.9 56.4 reduce-scatter.79
  1214.4 55.4 reduce-scatter.53
where the time goes:
time: 1290 us; the launch traced here: 1280 us
  waiting for transfers between devices  820 us (64%)
  matrix products  209 us (16%)
  local copies, waits for them, and re-layouts  90 us (7%)
  blocking collectives  51.4 us (4%)
  loops' own time  48.7 us (4%)
  other arithmetic  40 us (3%)
  between operations  17.2 us (1%)
    unnamed x40, waiting for transfers between devices  448 us
    reduce_scatter x1, waiting for transfers between devices, shards(): lax.psum_scatter(all_rows[0].astype(jnp.bfloat16), 'batch', scatter_dimen...  57.7 us
    reduce_scatter x1, waiting for transfers between devices, shards(): lax.psum_scatter(all_rows[4].astype(jnp.bfloat16), 'batch', scatter_dimen...  57.4 us
    psum x1, blocking collectives, shards(): lax.psum((enc_up_bias_g, enc_down_bias_g, enc_gain_g, enc_shift_g, dec_up...  42.5 us
    unnamed x281, local copies, waits for them, and re-layouts  40.8 us
    dot_general x16, matrix products, weight_grad(): lax.dot_general(inputs, grad, (((0,), (0,)), ((), ())), preferred_element...  40.1 us
    reduce_scatter x1, waiting for transfers between devices, shards(): lax.psum_scatter(enc_up_g.astype(jnp.bfloat16), 'seq', scatter_dimension=...  33.9 us
    dot_general x16, matrix products, input_grad(): lax.dot_general(grad, weight, (((1,), (1,)), ((), ())), preferred_element...  33.7 us
  transfers between devices with their start and end apart: 32, of which 20 were waited for; matrix products, arithmetic and copies ran while one was open for 21% of the time, Pallas kernels for 0%

commit v1 on v0

--- a/solution.py
+++ b/solution.py
@@ -1,12 +1,17 @@
+import functools
+
 import jax
 import jax.numpy as jnp
 from jax import lax
+from jax.experimental import pallas as pl
+from jax.experimental.pallas import tpu as pltpu
 from jax.sharding import PartitionSpec as P
 
 HEAD_DIM = 64
-
-
 NEGATIVE = -1e30
+BF = jnp.bfloat16
+F32 = jnp.float32
+BOTH = ("batch", "seq")
 
 
 def layer_norm(value, gain, shift):
@@ -202,7 +207,7 @@
     return (query_grad, key_sum, value_sum)
 
 
-def shards(
+def general_shards(
     source,
     target,
     source_ids,
@@ -522,7 +527,7 @@
     )
 
 
-def solution(mesh):
+def general(mesh):
     placed = (
         P("batch", "seq", None),
         P("batch", "seq", None),
@@ -549,7 +554,7 @@
         P(),
     )
     return jax.shard_map(
-        shards,
+        general_shards,
         mesh=mesh,
         in_specs=placed,
         out_specs=(
@@ -577,3 +582,735 @@
         ),
         check_vma=False,
     )
+
+
+def dot(left, right, left_dim=1, right_dim=0):
+    return lax.dot_general(
+        left, right, (((left_dim,), (right_dim,)), ((), ())), preferred_element_type=F32
+    )
+
+
+def my_core():
+    return lax.rem(lax.axis_index("batch"), 2)
+
+
+def block(index, size):
+    return pl.ds(pl.multiple_of(index * size, size), size)
+
+
+def normed(value):
+    centred = value - jnp.mean(value, axis=-1, keepdims=True)
+    scale = lax.rsqrt(jnp.mean(centred * centred, axis=-1, keepdims=True) + 1e-06)
+    return centred * scale, scale
+
+
+def normed_back(grad, unit, scale, gain):
+    scaled = grad * gain
+    first = jnp.mean(scaled, axis=-1, keepdims=True)
+    second = jnp.mean(scaled * unit, axis=-1, keepdims=True)
+    return scale * (scaled - first - unit * second)
+
+
+def gelu_and_slope(inner):
+    square = inner * inner
+    bent = jnp.tanh(0.7978845608028654 * inner * (1.0 + 0.044715 * square))
+    half = 0.5 * (1.0 + bent)
+    slope = half + 0.5 * inner * (1.0 - bent * bent) * (
+        0.7978845608028654 * (1.0 + 0.134145 * square)
+    )
+    return inner * half, slope
+
+
+def column_sum(value):
+    return jnp.sum(value, axis=0, keepdims=True)
+
+
+TILE = 256
+
+
+def attend_kernel(causal, same, *refs):
+    if same:
+        own_q, other_q, weight, own_mq, other_mq, own_mk, other_mk = refs[:7]
+        own_k, other_k = own_q, other_q
+        refs = refs[7:]
+    else:
+        own_q, other_q, own_k, other_k, weight, own_mq, other_mq, own_mk, other_mk = refs[:9]
+        refs = refs[9:]
+    out_own, out_other, wide_out, queries, keys, values, chances, outs = refs
+    step = pl.program_id(0)
+    core = my_core()
+    rows = own_q.shape[0]
+    heads = queries.shape[0]
+    length = queries.shape[1]
+    width = heads * HEAD_DIM
+
+    @pl.when(step == 0)
+    def _():
+        columns = block(core, width)
+        lane = lax.broadcasted_iota(jnp.int32, (TILE, HEAD_DIM), 1)
+        ones = (lane < 3).astype(BF)
+        for q_ref, k_ref, mq_ref, mk_ref, half in (
+            (own_q, own_k, own_mq, own_mk, core),
+            (other_q, other_k, other_mq, other_mk, 1 - core),
+        ):
+            for tile in range(rows // TILE):
+                here = slice(tile * TILE, (tile + 1) * TILE)
+                there = pl.ds(pl.multiple_of(half * rows + tile * TILE, TILE), TILE)
+                left_q = q_ref[here, :]
+                left_k = k_ref[here, :]
+                q_tile = dot(left_q, weight[0, :, columns]).astype(BF) * BF(0.125)
+                k_tile = dot(left_k, weight[1, :, columns]).astype(BF)
+                v_tile = dot(left_k, weight[2, :, columns]).astype(BF)
+                for head in range(heads):
+                    part = slice(head * HEAD_DIM, (head + 1) * HEAD_DIM)
+                    queries[head, there, :] = jnp.concatenate([q_tile[:, part], mq_ref[here, :]], axis=1)
+                    keys[head, there, :] = jnp.concatenate([k_tile[:, part], mk_ref[here, :]], axis=1)
+                    values[head, there, :] = jnp.concatenate([v_tile[:, part], ones], axis=1)
+
+    if causal:
+        lower = lax.broadcasted_iota(jnp.int32, (TILE, TILE), 0) >= lax.broadcasted_iota(
+            jnp.int32, (TILE, TILE), 1
+        )
+    for tile in range(length // TILE):
+        here = slice(tile * TILE, (tile + 1) * TILE)
+        seen = (tile + 1) * TILE if causal else length
+        scores = dot(queries[step, here, :], keys[step, :seen, :], 1, 1)
+        if causal:
+            last = jnp.where(lower, scores[:, seen - TILE :], NEGATIVE)
+            scores = last if tile == 0 else jnp.concatenate([scores[:, : seen - TILE], last], axis=1)
+        largest = jnp.max(scores, axis=-1, keepdims=True)
+        terms = jnp.exp(scores - largest)
+        total = jnp.sum(terms, axis=-1, keepdims=True)
+        low = (terms * (1.0 / total)).astype(BF)
+        chances[0, here, :seen] = low
+        outs[step, here, :] = dot(low, values[step, :seen, :])[:, :HEAD_DIM]
+
+    @pl.when(step == heads - 1)
+    def _():
+        for half, ref in ((core, out_own), (1 - core, out_other)):
+            for tile in range(rows // TILE):
+                here = slice(tile * TILE, (tile + 1) * TILE)
+                there = pl.ds(pl.multiple_of(half * rows + tile * TILE, TILE), TILE)
+                joined = jnp.concatenate([outs[head, there, :] for head in range(heads)], axis=1)
+                wide_out[there, :] = joined
+                ref[here, :] = joined.astype(BF)
+
+
+def attend_back_kernel(causal, same, *refs):
+    if same:
+        own_q, other_q = refs[:2]
+        own_k, other_k = own_q, other_q
+        refs = refs[2:]
+    else:
+        own_q, other_q, own_k, other_k = refs[:4]
+        refs = refs[4:]
+    queries, keys, values, chances, wide_out, grad_own, grad_other = refs[:7]
+    d_own, d_other, sums, grads, score_grads, dq, dk, dv = refs[7:]
+    step = pl.program_id(0)
+    core = my_core()
+    rows = own_q.shape[0]
+    heads = queries.shape[0]
+    length = queries.shape[1]
+
+    @pl.when(step == 0)
+    def _():
+        lane = lax.broadcasted_iota(jnp.int32, (TILE, HEAD_DIM), 1)
+        for ref, half in ((grad_own, core), (grad_other, 1 - core)):
+            for tile in range(rows // TILE):
+                here = slice(tile * TILE, (tile + 1) * TILE)
+                there = pl.ds(pl.multiple_of(half * rows + tile * TILE, TILE), TILE)
+                grad = ref[here, :]
+                both = grad.astype(F32) * wide_out[there, :]
+                for head in range(heads):
+                    part = slice(head * HEAD_DIM, (head + 1) * HEAD_DIM)
+                    settle = -jnp.sum(both[:, part], axis=-1, keepdims=True)
+                    first = settle.astype(BF).astype(F32)
+                    second = (settle - first).astype(BF).astype(F32)
+                    third = settle - first - second
+                    extra = jnp.where(
+                        lane == 0,
+                        first,
+                        jnp.where(lane == 1, second, jnp.where(lane == 2, third, 0.0)),
+                    )
+                    grads[head, there, :] = jnp.concatenate([grad[:, part], extra.astype(BF)], axis=1)
+
+    for tile in range(length // TILE):
+        here = slice(tile * TILE, (tile + 1) * TILE)
+        seen = (tile + 1) * TILE if causal else length
+        change = dot(grads[step, here, :], values[step, :seen, :], 1, 1)
+        low = (chances[0, here, :seen].astype(F32) * change).astype(BF)
+        score_grads[here, :seen] = low
+        dq[step, here, :] = dot(low, keys[step, :seen, :])[:, :HEAD_DIM] * 0.125
+    for tile in range(length // TILE if causal else 1):
+        here = slice(tile * TILE, (tile + 1) * TILE) if causal else slice(0, length)
+        below = slice(tile * TILE, length)
+        dk[block(step, HEAD_DIM), here] = dot(
+            queries[step, below, :HEAD_DIM], score_grads[below, here], 0, 0
+        )
+        dv[block(step, HEAD_DIM), here] = dot(
+            grads[step, below, :HEAD_DIM], chances[0, below, here], 0, 0
+        )
+
+    @pl.when(step == heads - 1)
+    def _():
+        for half, ref in ((core, d_own), (1 - core, d_other)):
+            there = block(half, rows)
+            ref[0, :, :] = jnp.concatenate(
+                [dq[head, there, :] for head in range(heads)], axis=1
+            ).astype(BF)
+            ref[1, :, :] = dk[:, there].T.astype(BF)
+            ref[2, :, :] = dv[:, there].T.astype(BF)
+        for kind in range(3):
+            x_own, x_other = (own_q, other_q) if kind == 0 else (own_k, other_k)
+            total = dot(d_own[kind], x_own[...], 0, 0) + dot(d_other[kind], x_other[...], 0, 0)
+            low = total.astype(BF)
+            for part in range(low.shape[0] // 32):
+                z_low, y, kept = part >> 2, (part >> 1) & 1, part & 1
+                for s in range(2):
+                    sums[kept ^ core, s, y, z_low, kind * 32 : (kind + 1) * 32, :] = low[
+                        part * 32 : (part + 1) * 32, s * 256 : (s + 1) * 256
+                    ]
+
+
+def store_up(sums, value, index):
+    core = my_core()
+    z, y = index >> 1, index & 1
+    low = value.astype(BF)
+    for kept in range(2):
+        for s in range(2):
+            sums[kept ^ core, s, y, z & 1, (z >> 1) ^ kept, :, :] = low[
+                kept * 128 : (kept + 1) * 128, s * 256 : (s + 1) * 256
+            ]
+
+
+def store_down(sums, value, index, column):
+    core = my_core()
+    low = value.astype(BF)
+    for part in range(8):
+        place = index * 8 + part
+        z, y, kept = place >> 2, (place >> 1) & 1, place & 1
+        for piece in range(2):
+            s, slot = (column * 2 + piece) // 4, (column * 2 + piece) % 4
+            sums[kept ^ core, s, y, z & 1, (z >> 1) ^ kept, slot * 32 : (slot + 1) * 32, :] = low[
+                part * 32 : (part + 1) * 32, piece * 256 : (piece + 1) * 256
+            ]
+
+
+def store_out(sums, value, side):
+    core = my_core()
+    low = value.astype(BF)
+    for place in range(16):
+        z, y, kept = place >> 2, (place >> 1) & 1, place & 1
+        sums[kept ^ core, side, y, z & 1, (z >> 1) ^ kept, :, :] = low[
+            place * 32 : (place + 1) * 32, :
+        ]
+
+
+def projected(att_own, att_other, weight, here):
+    core = my_core()
+    width = att_own.shape[1]
+    return dot(att_own[here, :], weight[block(core, width), :]) + dot(
+        att_other[here, :], weight[block(1 - core, width), :]
+    )
+
+
+def projected_back(grad, weight, out_own, out_other, here):
+    core = my_core()
+    width = out_own.shape[1]
+    out_own[here, :] = dot(grad, weight[block(core, width), :], 1, 1).astype(BF)
+    out_other[here, :] = dot(grad, weight[block(1 - core, width), :], 1, 1).astype(BF)
+
+
+def tiles_of(ref):
+    return [slice(t * TILE, (t + 1) * TILE) for t in range(ref.shape[0] // TILE)]
+
+
+def encode_kernel(
+    x, att_own, att_other, out_w, up, up_bias, down, down_bias, gain, shift,
+    memory, unit0, scale0, hidden_low, act, slope, unit1, scale1,
+):
+    for here in tiles_of(x):
+        pre = x[here, :].astype(F32) + projected(att_own, att_other, out_w, here)
+        unit, scale = normed(pre)
+        unit0[here, :] = unit
+        scale0[here, :] = scale
+        hidden = unit * gain[0:1, :] + shift[0:1, :]
+        low = hidden.astype(BF)
+        hidden_low[here, :] = low
+        value, bend = gelu_and_slope(dot(low, up[...]) + up_bias[...])
+        slope[here, :] = bend
+        value = value.astype(BF)
+        act[here, :] = value
+        unit, scale = normed(hidden + dot(value, down[...]) + down_bias[...])
+        unit1[here, :] = unit
+        scale1[here, :] = scale
+        memory[here, :] = (unit * gain[1:2, :] + shift[1:2, :]).astype(BF)
+
+
+def decode_first_kernel(y, att_own, att_other, out_w, gain, shift, first, first_low, unit0, scale0):
+    for here in tiles_of(y):
+        pre = y[here, :].astype(F32) + projected(att_own, att_other, out_w, here)
+        unit, scale = normed(pre)
+        unit0[here, :] = unit
+        scale0[here, :] = scale
+        value = unit * gain[0:1, :] + shift[0:1, :]
+        first[here, :] = value
+        first_low[here, :] = value.astype(BF)
+
+
+def decode_last_kernel(
+    first, att_own, att_other, out_w, up, up_bias, down, down_bias, gain, shift, upstream,
+    decoded, grad_pre, grad_own, grad_other, up_sums, down_sums, out_sums, vectors,
+    second_low, act, inner_low, branch_low, mixed_low,
+):
+    vectors[...] = jnp.zeros_like(vectors)
+    for here in tiles_of(first):
+        pre = first[here, :] + projected(att_own, att_other, out_w, here)
+        unit1, scale1 = normed(pre)
+        second = unit1 * gain[1:2, :] + shift[1:2, :]
+        low = second.astype(BF)
+        second_low[here, :] = low
+        value, slope = gelu_and_slope(dot(low, up[...]) + up_bias[...])
+        value = value.astype(BF)
+        act[here, :] = value
+        unit2, scale2 = normed(second + dot(value, down[...]) + down_bias[...])
+        decoded[here, :] = (unit2 * gain[2:3, :] + shift[2:3, :]).astype(BF)
+        grad = upstream[here, :].astype(F32)
+        vectors[7:8, :] += column_sum(grad * unit2)
+        vectors[8:9, :] += column_sum(grad)
+        grad = normed_back(grad, unit2, scale2, gain[2:3, :])
+        branch = grad.astype(BF)
+        branch_low[here, :] = branch
+        vectors[4:5, :] += column_sum(branch.astype(F32))
+        inner = (dot(branch, down[...], 1, 1) * slope).astype(BF)
+        inner_low[here, :] = inner
+        bias = column_sum(inner.astype(F32))
+        for part in range(4):
+            vectors[part : part + 1, :] += bias[:, part * 512 : (part + 1) * 512]
+        grad = grad + dot(inner, up[...], 1, 1)
+        vectors[5:6, :] += column_sum(grad * unit1)
+        vectors[6:7, :] += column_sum(grad)
+        grad = normed_back(grad, unit1, scale1, gain[1:2, :])
+        grad_pre[here, :] = grad
+        mixed = grad.astype(BF)
+        mixed_low[here, :] = mixed
+        projected_back(mixed, out_w, grad_own, grad_other, here)
+    layer_sums(
+        second_low, act, inner_low, branch_low, mixed_low, att_own, att_other,
+        up_sums, down_sums, out_sums,
+    )
+
+
+def layer_sums(
+    entering, act, inner_low, branch_low, mixed_low, att_own, att_other, up_sums, down_sums, out_sums
+):
+    for index in range(inner_low.shape[1] // 256):
+        store_up(up_sums, dot(inner_low[:, index * 256 : (index + 1) * 256], entering[...], 0, 0), index)
+    for index in range(2):
+        for column in range(act.shape[1] // 512):
+            store_down(
+                down_sums,
+                dot(
+                    branch_low[:, index * 256 : (index + 1) * 256],
+                    act[:, column * 512 : (column + 1) * 512],
+                    0,
+                    0,
+                ),
+                index,
+                column,
+            )
+    core = my_core()
+    store_out(out_sums, dot(mixed_low[...], att_own[...], 0, 0), core)
+    store_out(out_sums, dot(mixed_low[...], att_other[...], 0, 0), 1 - core)
+
+
+def encode_back_kernel(
+    d_own, d_other, cross_w, up, down, gain, out_w, unit0, scale0, hidden_low, act, slope, unit1, scale1,
+    att_own, att_other,
+    grad_pre, grad_own, grad_other, up_sums, down_sums, out_sums, vectors,
+    inner_low, branch_low, mixed_low,
+):
+    core = my_core()
+    width = d_own.shape[2]
+    vectors[...] = jnp.zeros_like(vectors)
+    for here in tiles_of(unit0):
+        grad = jnp.zeros(unit0[here, :].shape, F32)
+        for kind in (1, 2):
+            grad = grad + dot(d_own[kind, here, :], cross_w[kind, :, block(core, width)], 1, 1)
+            grad = grad + dot(d_other[kind, here, :], cross_w[kind, :, block(1 - core, width)], 1, 1)
+        unit = unit1[here, :]
+        vectors[7:8, :] += column_sum(grad * unit)
+        vectors[8:9, :] += column_sum(grad)
+        grad = normed_back(grad, unit, scale1[here, :], gain[1:2, :])
+        branch = grad.astype(BF)
+        branch_low[here, :] = branch
+        vectors[4:5, :] += column_sum(branch.astype(F32))
+        inner = (dot(branch, down[...], 1, 1) * slope[here, :]).astype(BF)
+        inner_low[here, :] = inner
+        bias = column_sum(inner.astype(F32))
+        for part in range(4):
+            vectors[part : part + 1, :] += bias[:, part * 512 : (part + 1) * 512]
+        grad = grad + dot(inner, up[...], 1, 1)
+        unit = unit0[here, :]
+        vectors[5:6, :] += column_sum(grad * unit)
+        vectors[6:7, :] += column_sum(grad)
+        grad = normed_back(grad, unit, scale0[here, :], gain[0:1, :])
+        grad_pre[here, :] = grad
+        mixed = grad.astype(BF)
+        mixed_low[here, :] = mixed
+        projected_back(mixed, out_w, grad_own, grad_other, here)
+    layer_sums(
+        hidden_low, act, inner_low, branch_low, mixed_low, att_own, att_other,
+        up_sums, down_sums, out_sums,
+    )
+
+
+def decode_first_back_kernel(
+    grad_in, d_own, d_other, cross_w, unit0, scale0, gain, out_w, att_own, att_other,
+    grad_pre, grad_own, grad_other, out_sums, vectors, mixed_low,
+):
+    core = my_core()
+    width = d_own.shape[2]
+    vectors[...] = jnp.zeros_like(vectors)
+    for here in tiles_of(unit0):
+        grad = grad_in[here, :]
+        grad = grad + dot(d_own[0, here, :], cross_w[0, :, block(core, width)], 1, 1)
+        grad = grad + dot(d_other[0, here, :], cross_w[0, :, block(1 - core, width)], 1, 1)
+        unit = unit0[here, :]
+        vectors[0:1, :] += column_sum(grad * unit)
+        vectors[1:2, :] += column_sum(grad)
+        grad = normed_back(grad, unit, scale0[here, :], gain[0:1, :])
+        grad_pre[here, :] = grad
+        mixed = grad.astype(BF)
+        mixed_low[here, :] = mixed
+        projected_back(mixed, out_w, grad_own, grad_other, here)
+    store_out(out_sums, dot(mixed_low[...], att_own[...], 0, 0), core)
+    store_out(out_sums, dot(mixed_low[...], att_other[...], 0, 0), 1 - core)
+
+
+def input_kernel(grad_pre, d_own, d_other, weight, grad):
+    core = my_core()
+    width = d_own.shape[2]
+    for here in tiles_of(grad_pre):
+        total = grad_pre[here, :]
+        for kind in range(3):
+            total = total + dot(d_own[kind, here, :], weight[kind, :, block(core, width)], 1, 1)
+            total = total + dot(d_other[kind, here, :], weight[kind, :, block(1 - core, width)], 1, 1)
+        grad[here, :] = total.astype(BF)
+
+
+VMEM = pl.BlockSpec(memory_space=pltpu.VMEM)
+
+
+def call(kernel, name, micros, operands, outs, scratch=(), grid=None, in_specs=None, out_specs=None):
+    shapes = tuple(jax.ShapeDtypeStruct(shape, kind) for shape, kind in outs)
+    extra = {} if grid is None else {"grid": grid}
+    return pl.pallas_call(
+        kernel,
+        out_shape=shapes,
+        in_specs=in_specs or [VMEM] * len(operands),
+        out_specs=out_specs or tuple([VMEM] * len(outs)),
+        scratch_shapes=list(scratch),
+        compiler_params=pltpu.CompilerParams(vmem_limit_bytes=56 * 2**20),
+        cost_estimate=pl.CostEstimate(
+            flops=int(micros * 1e9), bytes_accessed=0, transcendentals=0
+        ),
+        name=name,
+        **extra,
+    )(*operands)
+
+
+def whole(array):
+    rank = len(array.shape)
+    return pl.BlockSpec(array.shape, lambda step: (0,) * rank)
+
+
+def attend(name, causal, same, sides, weight, masks):
+    rows = sides[0].shape[0]
+    width = weight.shape[2] // 2
+    heads = width // HEAD_DIM
+    length = 2 * rows
+    wide = 2 * HEAD_DIM
+    operands = (*sides, weight, *masks)
+    outs = (
+        ((rows, width), BF),
+        ((rows, width), BF),
+        ((length, width), F32),
+        ((heads, length, wide), BF),
+        ((heads, length, wide), BF),
+        ((heads, length, wide), BF),
+        ((heads, length, length), BF),
+    )
+    shapes = [jax.ShapeDtypeStruct(shape, kind) for shape, kind in outs]
+    return call(
+        functools.partial(attend_kernel, causal, same),
+        name,
+        10,
+        operands,
+        outs,
+        scratch=[pltpu.VMEM((heads, length, HEAD_DIM), F32)],
+        grid=(heads,),
+        in_specs=[whole(one) for one in operands],
+        out_specs=tuple(whole(one) for one in shapes[:-1])
+        + (pl.BlockSpec((1, length, length), lambda step: (step, 0, 0)),),
+    )
+
+
+def attend_back(name, causal, same, sides, saved, grads):
+    wide_out, queries, keys, values, chances = saved
+    rows = sides[0].shape[0]
+    heads, length, wide = queries.shape
+    width = heads * HEAD_DIM
+    operands = (*sides, queries, keys, values, chances, wide_out, *grads)
+    outs = (
+        ((3, rows, width), BF),
+        ((3, rows, width), BF),
+        ((2, 2, 2, 2, 96, 256), BF),
+    )
+    in_specs = [whole(one) for one in operands]
+    in_specs[len(sides) + 3] = pl.BlockSpec((1, length, length), lambda step: (step, 0, 0))
+    shapes = [jax.ShapeDtypeStruct(shape, kind) for shape, kind in outs]
+    return call(
+        functools.partial(attend_back_kernel, causal, same),
+        name,
+        15,
+        operands,
+        outs,
+        scratch=[
+            pltpu.VMEM((heads, length, wide), BF),
+            pltpu.VMEM((length, length), BF),
+            pltpu.VMEM((heads, length, HEAD_DIM), F32),
+            pltpu.VMEM((width, length), F32),
+            pltpu.VMEM((width, length), F32),
+        ],
+        grid=(heads,),
+        in_specs=in_specs,
+        out_specs=tuple(whole(one) for one in shapes),
+    )
+
+
+def pairs(count, move):
+    found = []
+    for index in range(count):
+        z, y, core, s = index >> 3, (index >> 2) & 1, (index >> 1) & 1, index & 1
+        z, y, core, s = move(z, y, core, s)
+        found.append((index, (((z * 2 + y) * 2 + core) * 2) + s))
+    return found
+
+
+def fast_shards(count, source, target, source_ids, target_ids, out_grad, *params):
+    (
+        enc_qkv, enc_out, enc_up, enc_up_bias, enc_down, enc_down_bias, enc_gain, enc_shift, dec_qkv, dec_out,
+        cross_qkv, cross_out, dec_up, dec_up_bias, dec_down, dec_down_bias, dec_gain, dec_shift,
+    ) = params
+    moves = {
+        "swap": pairs(count, lambda z, y, c, s: (z, y, s, c)),
+        "core": pairs(count, lambda z, y, c, s: (z, y, 1 - c, s)),
+        "x": pairs(count, lambda z, y, c, s: (z, y, c, 1 - s)),
+        "y": pairs(count, lambda z, y, c, s: (z, 1 - y, c, s)),
+        "z1": pairs(count, lambda z, y, c, s: (z ^ 1, y, c, s)),
+        "z2": pairs(count, lambda z, y, c, s: (z ^ 2, y, c, s)),
+    }
+    row = lax.axis_index("batch")
+    core = row % 2
+    place = {"x": lax.axis_index("seq"), "y": (row // 2) % 2, "z1": (row // 4) % 2, "z2": (row // 8) ^ core}
+
+    def move(value, way):
+        return lax.ppermute(value, BOTH, moves[way])
+
+    ids = move(jnp.stack([source_ids[0], target_ids[0]]), "swap")
+    src = move(source[0], "swap")
+    tgt = move(target[0], "swap")
+    upstream = move(out_grad[0], "swap")
+    ids_other = move(ids, "core")
+    src_other = move(src, "core")
+    tgt_other = move(tgt, "core")
+    lane = jnp.arange(HEAD_DIM, dtype=jnp.int32)[None, :]
+
+    def masks(which):
+        marks = [side[which][:, None] == lane for side in (ids, ids_other)]
+        asks = [mark.astype(BF) for mark in marks]
+        bars = [jnp.where(~mark & (lane < 3), NEGATIVE, 0.0).astype(BF) for mark in marks]
+        return asks, bars
+
+    src_ask, src_bar = masks(0)
+    tgt_ask, tgt_bar = masks(1)
+    rows, wide = src.shape
+    inner = enc_up.shape[1]
+    width = wide // 2
+    full, thin = ((rows, wide), F32), ((rows, 1), F32)
+    low_full, low_half = ((rows, wide), BF), ((rows, width), BF)
+    low_inner = ((rows, inner), BF)
+    keep, keep_out = ((2, 2, 2, 2, 2, 128, 256), BF), ((2, 2, 2, 2, 2, 32, 256), BF)
+    biases = [one[None, :] for one in (enc_up_bias, enc_down_bias, dec_up_bias, dec_down_bias)]
+    enc_up_b, enc_down_b, dec_up_b, dec_down_b = biases
+
+    def scratch(shape):
+        return pltpu.VMEM(*shape)
+
+    att, att_send, *enc_saved = attend(
+        "enc_attend", False, True, (src, src_other), enc_qkv, (*src_ask, *src_bar)
+    )
+    enc_att = (att, move(att_send, "core"))
+    att, att_send, *dec_saved = attend(
+        "dec_attend", True, True, (tgt, tgt_other), dec_qkv, (*tgt_ask, *tgt_bar)
+    )
+    dec_att = (att, move(att_send, "core"))
+    memory, *enc_kept = call(
+        encode_kernel,
+        "encode",
+        8,
+        (src, *enc_att, enc_out, enc_up, enc_up_b, enc_down, enc_down_b, enc_gain, enc_shift),
+        (low_full, full, thin, low_full, low_inner, ((rows, inner), F32), full, thin),
+    )
+    first, first_low, first_unit, first_scale = call(
+        decode_first_kernel,
+        "decode_first",
+        2,
+        (tgt, *dec_att, dec_out, dec_gain, dec_shift),
+        (full, low_full, full, thin),
+    )
+    first_sides = (first_low, move(first_low, "core"))
+    memory_sides = (memory, move(memory, "core"))
+    cross_sides = (*first_sides, *memory_sides)
+    att, att_send, *cross_saved = attend(
+        "cross_attend", False, False, cross_sides, cross_qkv, (*tgt_ask, *src_bar)
+    )
+    cross_att = (att, move(att_send, "core"))
+    decoded, grad_second, grad_att, grad_send, dec_up_s, dec_down_s, cross_out_s, dec_vectors = call(
+        decode_last_kernel,
+        "decode_last",
+        20,
+        (first, *cross_att, cross_out, dec_up, dec_up_b, dec_down, dec_down_b, dec_gain, dec_shift, upstream),
+        (low_full, full, low_half, low_half, keep, keep, keep_out, ((16, wide), F32)),
+        scratch=[scratch(low_full), scratch(low_inner), scratch(low_inner), scratch(low_full), scratch(low_full)],
+    )
+    decoded = move(decoded, "swap")
+    d_cross, d_send, cross_qkv_s = attend_back(
+        "cross_attend_back", False, False, cross_sides, cross_saved, (grad_att, move(grad_send, "core"))
+    )
+    d_cross = (d_cross, move(d_send, "core"))
+    grad_dec_pre, grad_att, grad_send, dec_out_s, first_vectors = call(
+        decode_first_back_kernel,
+        "decode_first_back",
+        3,
+        (grad_second, *d_cross, cross_qkv, first_unit, first_scale, dec_gain, dec_out, *dec_att),
+        (full, low_half, low_half, keep_out, ((8, wide), F32)),
+        scratch=[scratch(low_full)],
+    )
+    dec_grads = (grad_att, move(grad_send, "core"))
+    unit0, scale0, hidden_low, act, slope, unit1, scale1 = enc_kept
+    grad_enc_pre, grad_att, grad_send, enc_up_s, enc_down_s, enc_out_s, enc_vectors = call(
+        encode_back_kernel,
+        "encode_back",
+        12,
+        (
+            *d_cross, cross_qkv, enc_up, enc_down, enc_gain, enc_out, unit0, scale0, hidden_low, act, slope,
+            unit1, scale1, *enc_att,
+        ),
+        (full, low_half, low_half, keep, keep, keep_out, ((16, wide), F32)),
+        scratch=[scratch(low_inner), scratch(low_full), scratch(low_full)],
+    )
+    enc_grads = (grad_att, move(grad_send, "core"))
+    d_dec, d_send, dec_qkv_s = attend_back(
+        "dec_attend_back", True, True, (tgt, tgt_other), dec_saved, dec_grads
+    )
+    (tgt_grad,) = call(
+        input_kernel, "target_grad", 2, (grad_dec_pre, d_dec, move(d_send, "core"), dec_qkv), (low_full,)
+    )
+    tgt_grad = move(tgt_grad, "swap")
+    d_enc, d_send, enc_qkv_s = attend_back(
+        "enc_attend_back", False, True, (src, src_other), enc_saved, enc_grads
+    )
+    (src_grad,) = call(
+        input_kernel, "source_grad", 2, (grad_enc_pre, d_enc, move(d_send, "core"), enc_qkv), (low_full,)
+    )
+    src_grad = move(src_grad, "swap")
+
+    def added(kept, got):
+        return kept.astype(F32) + got.astype(F32)
+
+    def meet(pair):
+        return added(pair[0], move(pair[1], "core")).astype(BF)
+
+    def joined(pair):
+        return jnp.stack([pair[0], move(pair[1], "core")], axis=3)
+
+    def reduced(value, order):
+        left = ["x", "y", "z1", "z2"]
+        for way in order:
+            axis = left.index(way)
+            left.remove(way)
+            kept = lax.dynamic_index_in_dim(value, place[way], axis, keepdims=False)
+            sent = lax.dynamic_index_in_dim(value, 1 - place[way], axis, keepdims=False)
+            total = added(kept, move(sent, way))
+            value = total.astype(BF)
+        return total
+
+    xyz, yxz = ("x", "y", "z1", "z2"), ("y", "x", "z1", "z2")
+    dec_down_r = reduced(meet(dec_down_s), xyz)
+    dec_up_r = reduced(meet(dec_up_s), yxz)
+    mixed = jnp.concatenate([meet(cross_out_s), meet(dec_out_s)], axis=4)
+    rest = jnp.concatenate([joined(cross_qkv_s), joined(dec_qkv_s)], axis=4)
+    enc_down_r = reduced(meet(enc_down_s), xyz)
+    enc_up_r = reduced(meet(enc_up_s), yxz)
+    rest_r = reduced(jnp.concatenate([mixed, rest], axis=4), xyz)
+    tail_r = reduced(jnp.concatenate([meet(enc_out_s), joined(enc_qkv_s)], axis=4), yxz)
+    vectors = jnp.concatenate([dec_vectors, first_vectors, enc_vectors])
+    for way in ("core", "x", "y", "z1", "z2"):
+        vectors = vectors + move(vectors, way)
+
+    def up_shape(value):
+        return value.T
+
+    def down_shape(value):
+        return jnp.swapaxes(value.reshape(4, 32, 256), 1, 2).reshape(1024, 32)
+
+    def out_shape(value):
+        return value.T
+
+    def qkv_shape(value):
+        return jnp.swapaxes(value.reshape(3, 32, 256), 1, 2)
+
+    dec_v, first_v, enc_v = vectors[:16], vectors[16:24], vectors[24:]
+    return (
+        decoded[None],
+        src_grad[None],
+        tgt_grad[None],
+        qkv_shape(tail_r[32:]),
+        out_shape(tail_r[:32]),
+        up_shape(enc_up_r),
+        enc_v[:4].reshape(-1),
+        down_shape(enc_down_r),
+        enc_v[4],
+        jnp.stack([enc_v[5], enc_v[7]]),
+        jnp.stack([enc_v[6], enc_v[8]]),
+        qkv_shape(rest_r[160:]),
+        out_shape(rest_r[32:64]),
+        qkv_shape(rest_r[64:160]),
+        out_shape(rest_r[:32]),
+        up_shape(dec_up_r),
+        dec_v[:4].reshape(-1),
+        down_shape(dec_down_r),
+        dec_v[4],
+        jnp.stack([first_v[0], dec_v[5], dec_v[7]]),
+        jnp.stack([first_v[1], dec_v[6], dec_v[8]]),
+    )
+
+
+def solution(mesh):
+    if mesh.shape["seq"] != 2 or mesh.shape["batch"] != 16:
+        return general(mesh)
+    tokens = P("batch", "seq", None)
+    ids = P("batch", "seq")
+    cut, cut3 = P("seq", "batch"), P(None, "seq", "batch")
+    return jax.shard_map(
+        functools.partial(fast_shards, mesh.size),
+        mesh=mesh,
+        in_specs=(tokens, tokens, ids, ids, tokens) + (P(),) * 18,
+        out_specs=(
+            tokens, tokens, tokens, cut3, cut, cut, P(), cut, P(), P(), P(), cut3, cut, cut3, cut, cut, P(), cut,
+            P(), P(), P(),
+        ),
+        check_vma=False,
+    )

time: 1290 us -> 388 us (0.30)
  waiting for transfers between devices: 820 us -> 99.6 us
  matrix products: 209 us -> 0 us
  Pallas kernels: 0 us -> 156 us
  starting transfers between devices: 1.78 us -> 73.7 us
  local copies, waits for them, and re-layouts: 90 us -> 34.2 us
  blocking collectives: 51.4 us -> 0 us
  loops' own time: 48.7 us -> 0 us
  other arithmetic: 40 us -> 15.3 us
  between operations: 17.2 us -> 2.07 us
    unnamed x40 -> x0, waiting for transfers between devices: 448 us -> none
    reduce_scatter x18 -> x0, waiting for transfers between devices: 372 us -> none  [the longest x1 57.7 us: shards(): lax.psum_scatter(all_rows[0].astype(jnp.bfloat16), 'batch', scatter_dimen...]
    dot_general x90 -> x0, matrix products: 209 us -> none  [the longest x16 40.1 us: weight_grad(): lax.dot_general(inputs, grad, (((0,), (0,)), ((), ())), preferred_element...]
    pallas_call x0 -> x13, Pallas kernels: none -> 156 us  [call(): pl.pallas_call(kernel, out_shape=shapes, in_specs=in_specs or [VMEM] * le...]
    ppermute x0 -> x60, waiting for transfers between devices: none -> 99.6 us  [move(): return lax.ppermute(value, BOTH, moves[way])]
    ppermute x0 -> x60, starting transfers between devices: none -> 73.7 us  [move(): return lax.ppermute(value, BOTH, moves[way])]
    another operation x27 -> x0, loops' own time: 48.7 us -> none  [the longest x3 16 us: attend_forward(): largest, total = lax.fori_loop(0, count, first_pass, initial)]
    psum x1 -> x0, blocking collectives: 42.5 us -> none  [shards(): lax.psum((enc_up_bias_g, enc_down_bias_g, enc_gain_g, enc_shift_g, dec_up...]
  transfers between devices with their start and end apart: 32 -> 60, of which waited for: 20 -> 21; matrix products, arithmetic and copies ran while one was open for 21% -> 9% of each run, Pallas kernels for 0% -> 37%
where the time goes in v1:
time: 388 us; the launch traced here: 381 us
  Pallas kernels  156 us (40%)
  waiting for transfers between devices  99.6 us (26%)
  starting transfers between devices  73.7 us (19%)
  local copies, waits for them, and re-layouts  34.2 us (9%)
  other arithmetic  15.3 us (4%)
    pallas_call x13, Pallas kernels, call(): pl.pallas_call(kernel, out_shape=shapes, in_specs=in_specs or [VMEM] * le...  156 us
    ppermute x60, waiting for transfers between devices, move(): return lax.ppermute(value, BOTH, moves[way])  99.6 us
    ppermute x60, starting transfers between devices, move(): return lax.ppermute(value, BOTH, moves[way])  73.7 us
    unnamed x82, local copies, waits for them, and re-layouts  15.6 us
    squeeze x7, local copies, waits for them, and re-layouts, meet(): return added(pair[0], move(pair[1], 'core')).astype(BF)  8.83 us
  transfers between devices with their start and end apart: 60, of which 21 were waited for; matrix products, arithmetic and copies ran while one was open for 9% of the time, Pallas kernels for 37%

profile of v1, /device:TPU:2, one launch (start us, length us, event | category | flops | bytes accessed | tf_op | source)
XLA Modules:
  0.0 380.7 jit_solution(11687588530769492233)
XLA Ops:
  1.4 1.9 collective-permute-start.2
  3.3 3.6 collective-permute-start.6
  6.9 1.9 collective-permute-start
  10.1 9.5 %collective-permute-done.refs_0_.y = bf16[512,512]{1,0:T(8,128)(2,1)S(1)} collective-permute-done((bf16[512,512]{1,0:T(8,128)(2,1)}, bf16[512,512]{1,0:T(8,128)(2,1)S(1)}, u32[]{:S(2)}, u32[]{:S(2)}) %collective-permute-start) | collective-permute-done | bytes 524320 | tf_op jit(solution)/shard_map/ppermute | solution.py:1119
  23.9 15.1 %dec_attend.1 = (bf16[512,256]{1,0:T(8,128)(2,1)}, bf16[512,256]{1,0:T(8,128)(2,1)}, f32[1024,256]{1,0:T(8,128)}, bf16[4,1024,128]{2,1,0:T(8,128)(2,1)}, bf16[4,...) custom-call(bf16[512,512]{1,0:T(8,128)(2,1)} %copy-done.21, ...), custom_call_target="tpu_custom_call" | custom-call | flops 10000000000 | tf_op jit(solution)/shard_map/dec_attend/pallas_call | solution.py:1008
  40.0 16.8 %enc_attend.1 = (bf16[512,256]{1,0:T(8,128)(2,1)}, bf16[512,256]{1,0:T(8,128)(2,1)}, f32[1024,256]{1,0:T(8,128)}, bf16[4,1024,128]{2,1,0:T(8,128)(2,1)}, bf16[4,...) custom-call(bf16[512,512]{1,0:T(8,128)(2,1)} %copy-done.22, ...), custom_call_target="tpu_custom_call" | custom-call | flops 10000000000 | tf_op jit(solution)/shard_map/enc_attend/pallas_call | solution.py:1008
  58.0 3.6 decode_first.1
  62.5 10.9 %encode.1 = (bf16[512,512]{1,0:T(8,128)(2,1)}, f32[512,512]{1,0:T(8,128)}, f32[512,1]{1,0:T(8,128)}, bf16[512,512]{1,0:T(8,128)(2,1)}, bf16[512,2048]{1,0:T(8,12...) custom-call(bf16[512,512]{1,0:T(8,128)(2,1)} %copy-done.22, ...), custom_call_target="tpu_custom_call" | custom-call | flops 8000000000 | tf_op jit(solution)/shard_map/encode/pallas_call | solution.py:1008
  73.9 3.7 collective-permute-start.11
  79.2 17.6 %cross_attend.1 = (bf16[512,256]{1,0:T(8,128)(2,1)}, bf16[512,256]{1,0:T(8,128)(2,1)}, f32[1024,256]{1,0:T(8,128)}, bf16[4,1024,128]{2,1,0:T(8,128)(2,1)}, bf16[...) custom-call(bf16[512,512]{1,0:T(8,128)(2,1)} %get-tuple-element.86.refs_0_, ...), custom_call_target="tpu_custom_call" | custom-call | flops 10000000000 | tf_op jit(solution)/shard_map/cross_attend/pallas_call | solution.py:1008
  97.0 1.6 collective-permute-done.10.att_other
  99.3 15.0 %decode_last.1 = (bf16[512,512]{1,0:T(8,128)(2,1)}, f32[512,512]{1,0:T(8,128)}, bf16[512,256]{1,0:T(8,128)(2,1)}, bf16[512,256]{1,0:T(8,128)(2,1)}, bf16[2,2,2,2...) custom-call(f32[512,512]{1,0:T(8,128)} %get-tuple-element.85.first, ...), custom_call_target="tpu_custom_call" | custom-call | flops 20000000000 | tf_op jit(solution)/shard_map/decode_last/pallas_call | solution.py:1008
  115.8 2.0 collective-permute-start.12
  117.8 2.3 slice_bitcast_fusion.1
  120.8 17.3 %cross_attend_back.1 = (bf16[3,512,256]{2,1,0:T(8,128)(2,1)}, bf16[3,512,256]{2,1,0:T(8,128)(2,1)}, bf16[2,2,2,2,96,256]{5,4,3,2,1,0:T(8,128)(2,1)}) custom-call(bf16[512,512]{1,0:T(8,128)(2,1)} %get-tuple-element.86.refs_0_, bf16[512,512]{1,0:T(8,128)(2,1)} %copy-done.25, bf16[512,512]{1,0:T(8,128)(2,1)} %get-tuple-element.89.refs_2_, ...), custom_call_target="tpu_custom_call" | custom-call | flops 15000000512 | tf_op jit(solution)/shard_map/cross_attend_back/pallas_call | solution.py:1008
  141.9 14.0 %encode_back.1 = (f32[512,512]{1,0:T(8,128)}, bf16[512,256]{1,0:T(8,128)(2,1)}, bf16[512,256]{1,0:T(8,128)(2,1)}, bf16[2,2,2,2,2,128,256]{6,5,4,3,2,1,0:T(8,128)...) custom-call(bf16[3,512,256]{2,1,0:T(8,128)(2,1)} %get-tuple-element., ...), custom_call_target="tpu_custom_call" | custom-call | flops 12000000000 | tf_op jit(solution)/shard_map/encode_back/pallas_call | solution.py:1008
  155.9 5.7 %decode_first_back.1 = (f32[512,512]{1,0:T(8,128)}, bf16[512,256]{1,0:T(8,128)(2,1)}, bf16[512,256]{1,0:T(8,128)(2,1)}, bf16[2,2,2,2,2,32,256]{6,5,4,3,2,1,0:T(8,128)(2,1)}, f32[8,512]{1,0:T(8,128)}) custom-call(f32[512,512]{1,0:T(8,128)} %get-tuple-element.119.grad_in, bf16[3,512,256]{2,1,0:T(8,128)(2,1)} %get-tuple-element.100.d_own, ...), custom_call_target="tpu_custom_call" | custom-call | flops 3000000000 | tf_op jit(solution)/shard_map/decode_first_back/pallas_call | solution.py:1008
  161.6 1.3 constant_dynamic-update-slice_fusion.1
  164.1 1.7 slice_bitcast_fusion.10
  165.7 1.7 slice_bitcast_fusion.14
  173.1 1.9 collective-permute-start.33
  175.0 2.8 collective-permute-done.33
  177.8 1.6 collective-permute-start.34
  179.4 2.9 collective-permute-done.34
  182.4 1.8 collective-permute-start.56
  184.2 16.9 %enc_attend_back.1 = (bf16[3,512,256]{2,1,0:T(8,128)(2,1)}, bf16[3,512,256]{2,1,0:T(8,128)(2,1)}, bf16[2,2,2,2,96,256]{5,4,3,2,1,0:T(8,128)(2,1)}) custom-call(bf16[512,512]{1,0:T(8,128)(2,1)} %copy-done.22, bf16[512,512]{1,0:T(8,128)(2,1)} %copy-done.24, bf16[4,1024,128]{2,1,0:T(8,128)(2,1)} %get-tuple-element.110.refs_2_, ...), custom_call_target="tpu_custom_call" | custom-call | flops 15000000512 | tf_op jit(solution)/shard_map/enc_attend_back/pallas_call | solution.py:1008
  201.1 1.6 collective-permute-start.51
  202.7 14.7 %dec_attend_back.1 = (bf16[3,512,256]{2,1,0:T(8,128)(2,1)}, bf16[3,512,256]{2,1,0:T(8,128)(2,1)}, bf16[2,2,2,2,96,256]{5,4,3,2,1,0:T(8,128)(2,1)}) custom-call(bf16[512,512]{1,0:T(8,128)(2,1)} %copy-done.21, bf16[512,512]{1,0:T(8,128)(2,1)} %copy-done.23, bf16[4,1024,128]{2,1,0:T(8,128)(2,1)} %get-tuple-element.123.refs_2_, ...), custom_call_target="tpu_custom_call" | custom-call | flops 15000000512 | tf_op jit(solution)/shard_map/dec_attend_back/pallas_call | solution.py:1008
  217.4 1.3 slice_bitcast_fusion.5
  218.8 1.7 collective-permute-start.35
  220.5 2.8 collective-permute-done.35
  223.3 2.7 collective-permute-start.36
  226.1 4.8 %collective-permute-done.36 = f32[40,512]{1,0:T(8,128)S(1)} collective-permute-done((f32[40,512]{1,0:T(8,128)S(1)}, f32[40,512]{1,0:T(8,128)S(1)}, u32[]{:S(2)}, u32[]{:S(2)}) %collective-permute-start.36) | collective-permute-done | bytes 81952 | tf_op jit(solution)/shard_map/ppermute | solution.py:1119
  236.1 1.5 collective-permute-done.22
  239.0 1.4 maximum_maximum_fusion
  242.3 4.6 %collective-permute-done.57 = bf16[2,2,128,256]{3,2,1,0:T(8,128)(2,1)S(1)} collective-permute-done((bf16[2,2,128,256]{3,2,1,0:T(8,128)(2,1)S(1)}, bf16[2,2,128,256]{3,2,1,0:T(8,128)(2,1)S(1)}, u32[]{:S(2)}, u32[]{:S(2)}) %collective-permute-start.57) | collective-permute-done | bytes 262176 | tf_op jit(solution)/shard_map/ppermute | solution.py:1119
  247.7 6.9 %collective-permute-done.52 = bf16[2,2,128,256]{3,2,1,0:T(8,128)(2,1)S(1)} collective-permute-done((bf16[2,2,128,256]{3,2,1,0:T(8,128)(2,1)S(1)}, bf16[2,2,128,256]{3,2,1,0:T(8,128)(2,1)S(1)}, u32[]{:S(2)}, u32[]{:S(2)}) %collective-permute-start.52) | collective-permute-done | bytes 262176 | tf_op jit(solution)/shard_map/ppermute | solution.py:1119
  255.4 4.2 %collective-permute-done.58 = bf16[2,128,256]{2,1,0:T(8,128)(2,1)S(1)} collective-permute-done((bf16[2,128,256]{2,1,0:T(8,128)(2,1)S(1)}, bf16[2,128,256]{2,1,0:T(8,128)(2,1)S(1)}, u32[]{:S(2)}, u32[]{:S(2)}) %collective-permute-start.58) | collective-permute-done | bytes 131104 | tf_op jit(solution)/shard_map/ppermute | solution.py:1119
  260.3 4.9 %collective-permute-done.53 = bf16[2,128,256]{2,1,0:T(8,128)(2,1)S(1)} collective-permute-done((bf16[2,128,256]{2,1,0:T(8,128)(2,1)S(1)}, bf16[2,128,256]{2,1,0:T(8,128)(2,1)S(1)}, u32[]{:S(2)}, u32[]{:S(2)}) %collective-permute-start.53) | collective-permute-done | bytes 131104 | tf_op jit(solution)/shard_map/ppermute | solution.py:1119
  265.2 2.0 collective-permute-start.59
  267.3 4.4 %collective-permute-done.59 = bf16[128,256]{1,0:T(8,128)(2,1)S(1)} collective-permute-done((bf16[128,256]{1,0:T(8,128)(2,1)S(1)}, bf16[128,256]{1,0:T(8,128)(2,1)S(1)}, u32[]{:S(2)}, u32[]{:S(2)}) %collective-permute-start.59) | collective-permute-done | bytes 65568 | tf_op jit(solution)/shard_map/ppermute | solution.py:1119
  273.1 4.3 %collective-permute-done.54 = bf16[128,256]{1,0:T(8,128)(2,1)S(1)} collective-permute-done((bf16[128,256]{1,0:T(8,128)(2,1)S(1)}, bf16[128,256]{1,0:T(8,128)(2,1)S(1)}, u32[]{:S(2)}, u32[]{:S(2)}) %collective-permute-start.54) | collective-permute-done | bytes 65568 | tf_op jit(solution)/shard_map/ppermute | solution.py:1119
  279.9 4.0 %target_grad.1 = bf16[512,512]{1,0:T(8,128)(2,1)} custom-call(f32[512,512]{1,0:T(8,128)} %get-tuple-element.122.grad_pre, bf16[3,512,256]{2,1,0:T(8,128)(2,1)} %get-tuple-element.130.d_own, bf16[3,512,256]{2,1,0:T(8,128)(2,1)} %collective-permute-done.19.d_other, bf16[3,512,512]{2,1,0:T(8,128)(2,1)} %weight.3), custom_call_target="tpu_custom_call" | custom-call | flops 2000000000 | tf_op jit(solution)/shard_map/target_grad/pallas_call | solution.py:1008
  283.9 1.9 collective-permute-start.20
  285.8 4.2 %source_grad.1 = bf16[512,512]{1,0:T(8,128)(2,1)} custom-call(f32[512,512]{1,0:T(8,128)} %get-tuple-element.109.grad_pre, bf16[3,512,256]{2,1,0:T(8,128)(2,1)} %get-tuple-element.117.d_own, bf16[3,512,256]{2,1,0:T(8,128)(2,1)} %collective-permute-done.16.d_other, bf16[3,512,512]{2,1,0:T(8,128)(2,1)} %weight.2), custom_call_target="tpu_custom_call" | custom-call | flops 2000000000 | tf_op jit(solution)/shard_map/source_grad/pallas_call | solution.py:1008
  290.0 3.6 collective-permute-start.17
  293.6 1.5 fusion.3
  295.3 1.3 fusion.10
  296.7 2.0 collective-permute-start.24
  298.6 1.5 fusion.4
  300.2 21.9 %collective-permute-done.24 = bf16[2,2,128,256]{3,2,0,1:T(8,128)(2,1)S(1)} collective-permute-done((bf16[2,2,128,256]{3,2,0,1:T(8,128)(2,1)S(1)}, bf16[2,2,128,256]{3,2,0,1:T(8,128)(2,1)S(1)}, u32[]{:S(2)}, u32[]{:S(2)}) %collective-permute-start.24) | collective-permute-done | bytes 262176 | tf_op jit(solution)/shard_map/ppermute | solution.py:1119
  323.3 2.6 collective-permute-start.25
  327.1 9.4 %collective-permute-done.28 = bf16[2,2,2,128,256]{4,3,2,1,0:T(8,128)(2,1)S(1)} collective-permute-done((bf16[2,2,2,128,256]{4,3,2,1,0:T(8,128)(2,1)S(1)}, bf16[2,2,2,128,256]{4,3,2,1,0:T(8,128)(2,1)S(1)}, u32[]{:S(2)}, u32[]{:S(2)}) %collective-permute-start.28) | collective-permute-done | bytes 524320 | tf_op jit(solution)/shard_map/ppermute | solution.py:1119
  336.8 2.3 collective-permute-start.26
  339.2 2.9 collective-permute-start.29
  345.4 3.4 collective-permute-start.40
  348.8 2.9 collective-permute-start.30
  352.3 3.5 collective-permute-start.41
  355.9 2.0 collective-permute-done.47
  358.1 3.5 collective-permute-start.48
  361.6 2.6 collective-permute-start.31
  364.8 3.8 %collective-permute-done.48 = bf16[2,256,256]{2,1,0:T(8,128)(2,1)S(1)} collective-permute-done((bf16[2,256,256]{2,1,0:T(8,128)(2,1)S(1)}, bf16[2,256,256]{2,1,0:T(8,128)(2,1)S(1)}, u32[]{:S(2)}, u32[]{:S(2)}) %collective-permute-start.48) | collective-permute-done | bytes 262176 | tf_op jit(solution)/shard_map/ppermute | solution.py:1119
  368.8 1.6 collective-permute-start.49
  371.2 5.3 %collective-permute-done.49 = bf16[256,256]{1,0:T(8,128)(2,1)S(1)} collective-permute-done((bf16[256,256]{1,0:T(8,128)(2,1)S(1)}, bf16[256,256]{1,0:T(8,128)(2,1)S(1)}, u32[]{:S(2)}, u32[]{:S(2)}) %collective-permute-start.49) | collective-permute-done | bytes 131104 | tf_op jit(solution)/shard_map/ppermute | solution.py:1119
  (242 shorter events, 52.1 us)
Async XLA Ops:
  1.4 7.5 %collective-permute-start.2 = (s32[2,512]{1,0:T(2,128)S(1)}, s32[2,512]{1,0:T(2,128)S(1)}, u32[]{:S(2)}, u32[]{:S(2)}) collective-permute-start(s32[2,512]{1,0:T(2,128)S(1)} %pad_add_fusion), channel_id=1, source_target_pairs={{0,0},{1,2},{2,1},{3,3},{4,4},{5,6},{6,5},{7,7},{8,8},{9,10},{10,9... | collective-permute-start | bytes 12296 | tf_op jit(solution)/shard_map/ppermute | solution.py:1119
  3.3 19.3 %collective-permute-start.6 = (bf16[512,512]{1,0:T(8,128)(2,1)}, bf16[512,512]{1,0:T(8,128)(2,1)S(1)}, u32[]{:S(2)}, u32[]{:S(2)}) collective-permute-start(bf16[512,512]{1,0:T(8,128)(2,1)} %bitcast.252), channel_id=1, source_target_pairs={{0,0},{1,2},{2,1},{3,3},{4,4},{5,6},{6,5},{7,7},{8,8},{9,10},{10,9... | collective-permute-start | bytes 1572872 | tf_op jit(solution)/shard_map/ppermute | solution.py:1119
  6.9 12.7 %collective-permute-start = (bf16[512,512]{1,0:T(8,128)(2,1)}, bf16[512,512]{1,0:T(8,128)(2,1)S(1)}, u32[]{:S(2)}, u32[]{:S(2)}) collective-permute-start(bf16[512,512]{1,0:T(8,128)(2,1)} %bitcast.251), channel_id=1, source_target_pairs={{0,0},{1,2},{2,1},{3,3},{4,4},{5,6},{6,5},{7,7},{8,8},{9,10},{10,9... | collective-permute-start | bytes 1572872 | tf_op jit(solution)/shard_map/ppermute | solution.py:1119
  8.9 1.2 collective-permute-start.3
  19.6 3.4 collective-permute-start.1
  22.5 16.4 %copy-start.22 = (bf16[512,512]{1,0:T(8,128)(2,1)}, bf16[512,512]{1,0:T(8,128)(2,1)S(1)}, u32[]{:S(2)}) copy-start(bf16[512,512]{1,0:T(8,128)(2,1)S(1)} %collective-permute-done.6.refs_0_.x) | copy-start | bytes 1572868
  22.5 16.6 %collective-permute-start.7 = (bf16[512,512]{1,0:T(8,128)(2,1)S(1)}, bf16[512,512]{1,0:T(8,128)(2,1)S(1)}, u32[]{:S(2)}, u32[]{:S(2)}) collective-permute-start(bf16[512,512]{1,0:T(8,128)(2,1)S(1)} %collective-permute-done.6.refs_0_.x), channel_id=1, source_target_pairs={{0,2},{1,3},{2,0},{3,1},{4,6},{5,7},{6,4},{7,5},{8,10},{9,11},{10,... | collective-permute-start | bytes 1572872 | tf_op jit(solution)/shard_map/ppermute | solution.py:1119
  39.0 18.3 %collective-permute-start.4 = (bf16[512,256]{1,0:T(8,128)(2,1)}, bf16[512,256]{1,0:T(8,128)(2,1)S(1)}, u32[]{:S(2)}, u32[]{:S(2)}) collective-permute-start(bf16[512,256]{1,0:T(8,128)(2,1)} %get-tuple-element.84), channel_id=1, source_target_pairs={{0,2},{1,3},{2,0},{3,1},{4,6},{5,7},{6,4},{7,5},{8,10},{9,11},{10,... | collective-permute-start | bytes 786440 | tf_op jit(solution)/shard_map/ppermute | solution.py:1119
  56.8 4.9 %collective-permute-start.8 = (bf16[512,256]{1,0:T(8,128)(2,1)}, bf16[512,256]{1,0:T(8,128)(2,1)S(1)}, u32[]{:S(2)}, u32[]{:S(2)}) collective-permute-start(bf16[512,256]{1,0:T(8,128)(2,1)} %get-tuple-element.88), channel_id=1, source_target_pairs={{0,2},{1,3},{2,0},{3,1},{4,6},{5,7},{6,4},{7,5},{8,10},{9,11},{10,... | collective-permute-start | bytes 786440 | tf_op jit(solution)/shard_map/ppermute | solution.py:1119
  61.6 15.9 %collective-permute-start.5 = (bf16[512,512]{1,0:T(8,128)(2,1)}, bf16[512,512]{1,0:T(8,128)(2,1)S(1)}, u32[]{:S(2)}, u32[]{:S(2)}) collective-permute-start(bf16[512,512]{1,0:T(8,128)(2,1)} %get-tuple-element.86.refs_0_), channel_id=1, source_target_pairs={{0,2},{1,3},{2,0},{3,1},{4,6},{5,7},{6,4},{7,5},{8,10},{9,11},{10,... | collective-permute-start | bytes 1572872 | tf_op jit(solution)/shard_map/ppermute | solution.py:1119
  73.4 4.2 %collective-permute-start.9 = (bf16[512,512]{1,0:T(8,128)(2,1)}, bf16[512,512]{1,0:T(8,128)(2,1)S(1)}, u32[]{:S(2)}, u32[]{:S(2)}) collective-permute-start(bf16[512,512]{1,0:T(8,128)(2,1)} %get-tuple-element.89.refs_2_), channel_id=1, source_target_pairs={{0,2},{1,3},{2,0},{3,1},{4,6},{5,7},{6,4},{7,5},{8,10},{9,11},{10,... | collective-permute-start | bytes 1572872 | tf_op jit(solution)/shard_map/ppermute | solution.py:1119
  73.9 23.1 %collective-permute-start.11 = (bf16[512,512]{1,0:T(8,128)(2,1)S(1)}, bf16[512,512]{1,0:T(8,128)(2,1)S(1)}, u32[]{:S(2)}, u32[]{:S(2)}) collective-permute-start(bf16[512,512]{1,0:T(8,128)(2,1)S(1)} %bitcast.253), channel_id=1, source_target_pairs={{0,0},{1,2},{2,1},{3,3},{4,4},{5,6},{6,5},{7,7},{8,8},{9,10},{10,9... | collective-permute-start | bytes 1572872 | tf_op jit(solution)/shard_map/ppermute | solution.py:1119
  96.8 1.8 collective-permute-start.10
  115.2 25.6 %collective-permute-start.42 = (bf16[2,2,2,2,32,256]{5,4,2,1,0,3:T(8,128)(2,1)S(1)}, bf16[2,2,2,2,32,256]{5,4,2,1,0,3:T(8,128)(2,1)S(1)}, u32[]{:S(2)}, u32[]{:S(2)}) collective-permute-start(bf16[2,2,2,2,32,256]{5,4,2,1,0,3:T(8,128)(2,1)S(1)} %slice_bitcast_fusion.12), channel_id=1, source_target_pairs={{0,2},{1,3},{2,0},{3,1},{4,6},{5,7},{6,4},{7,5},{8,10},{9,11},{10,... | collective-permute-start | bytes 786440 | tf_op jit(solution)/shard_map/ppermute | solution.py:1119
  115.4 4.7 %collective-permute-start.13 = (bf16[512,256]{1,0:T(8,128)(2,1)}, bf16[512,256]{1,0:T(8,128)(2,1)S(1)}, u32[]{:S(2)}, u32[]{:S(2)}) collective-permute-start(bf16[512,256]{1,0:T(8,128)(2,1)} %get-tuple-element.99), channel_id=1, source_target_pairs={{0,2},{1,3},{2,0},{3,1},{4,6},{5,7},{6,4},{7,5},{8,10},{9,11},{10,... | collective-permute-start | bytes 786440 | tf_op jit(solution)/shard_map/ppermute | solution.py:1119
  115.8 25.1 %collective-permute-start.12 = (bf16[512,512]{1,0:T(8,128)(2,1)}, bf16[512,512]{1,0:T(8,128)(2,1)S(1)}, u32[]{:S(2)}, u32[]{:S(2)}) collective-permute-start(bf16[512,512]{1,0:T(8,128)(2,1)} %get-tuple-element.92), channel_id=1, source_target_pairs={{0,0},{1,2},{2,1},{3,3},{4,4},{5,6},{6,5},{7,7},{8,8},{9,10},{10,9... | collective-permute-start | bytes 1572872 | tf_op jit(solution)/shard_map/ppermute | solution.py:1119
  120.8 17.4 %copy-start.5 = (bf16[2,2,2,2,2,128,256]{6,5,4,3,2,1,0:T(8,128)(2,1)S(1)}, bf16[2,2,2,2,2,128,256]{6,5,4,3,2,1,0:T(8,128)(2,1)}, u32[]{:S(2)}) copy-start(bf16[2,2,2,2,2,128,256]{6,5,4,3,2,1,0:T(8,128)(2,1)} %get-tuple-element.144) | copy-start | bytes 6291460
  138.1 2.8 collective-permute-start.14
  139.4 29.1 %collective-permute-start.55 = (bf16[2,2,2,2,128,256]{5,4,3,2,1,0:T(8,128)(2,1)S(1)}, bf16[2,2,2,2,128,256]{5,4,3,2,1,0:T(8,128)(2,1)S(1)}, u32[]{:S(2)}, u32[]{:S(2)}) collective-permute-start(bf16[2,2,2,2,128,256]{5,4,3,2,1,0:T(8,128)(2,1)S(1)} %slice_bitcast_fusion), channel_id=1, source_target_pairs={{0,2},{1,3},{2,0},{3,1},{4,6},{5,7},{6,4},{7,5},{8,10},{9,11},{10,... | collective-permute-start | bytes 3145736 | tf_op jit(solution)/shard_map/ppermute | solution.py:1119
  139.5 29.9 %collective-permute-start.50 = (bf16[2,2,2,2,128,256]{5,4,3,2,1,0:T(8,128)(2,1)}, bf16[2,2,2,2,128,256]{5,4,3,2,1,0:T(8,128)(2,1)S(1)}, u32[]{:S(2)}, u32[]{:S(2)}) collective-permute-start(bf16[2,2,2,2,128,256]{5,4,3,2,1,0:T(8,128)(2,1)} %slice_bitcast_fusion.1), channel_id=1, source_target_pairs={{0,2},{1,3},{2,0},{3,1},{4,6},{5,7},{6,4},{7,5},{8,10},{9,11},{10,... | collective-permute-start | bytes 3145736 | tf_op jit(solution)/shard_map/ppermute | solution.py:1119
  140.8 97.2 %collective-permute-start.44 = (bf16[2,2,2,96,256]{4,3,2,1,0:T(8,128)(2,1)}, bf16[2,2,2,96,256]{4,3,2,1,0:T(8,128)(2,1)}, u32[]{:S(2)}, u32[]{:S(2)}) collective-permute-start(bf16[2,2,2,96,256]{4,3,2,1,0:T(8,128)(2,1)} %get-tuple-element.167), channel_id=1, source_target_pairs={{0,2},{1,3},{2,0},{3,1},{4,6},{5,7},{6,4},{7,5},{8,10},{9,11},{10,... | collective-permute-start | bytes 1179656 | tf_op jit(solution)/shard_map/ppermute | solution.py:1119
  163.6 8.6 %collective-permute-start.32 = (f32[40,512]{1,0:T(8,128)}, f32[40,512]{1,0:T(8,128)S(1)}, u32[]{:S(2)}, u32[]{:S(2)}) collective-permute-start(f32[40,512]{1,0:T(8,128)} %constant_dynamic-update-slice_fusion), channel_id=1, source_target_pairs={{0,2},{1,3},{2,0},{3,1},{4,6},{5,7},{6,4},{7,5},{8,10},{9,11},{10,... | collective-permute-start | bytes 245768 | tf_op jit(solution)/shard_map/ppermute | solution.py:1119
  165.7 53.1 %collective-permute-start.43 = (bf16[2,2,2,2,32,256]{5,4,2,1,0,3:T(8,128)(2,1)}, bf16[2,2,2,2,32,256]{5,4,2,1,0,3:T(8,128)(2,1)S(1)}, u32[]{:S(2)}, u32[]{:S(2)}) collective-permute-start(bf16[2,2,2,2,32,256]{5,4,2,1,0,3:T(8,128)(2,1)} %slice_bitcast_fusion.10), channel_id=1, source_target_pairs={{0,2},{1,3},{2,0},{3,1},{4,6},{5,7},{6,4},{7,5},{8,10},{9,11},{10,... | collective-permute-start | bytes 786440 | tf_op jit(solution)/shard_map/ppermute | solution.py:1119
  168.5 54.8 %collective-permute-start.21 = (bf16[2,2,2,2,32,256]{5,4,2,1,0,3:T(8,128)(2,1)}, bf16[2,2,2,2,32,256]{5,4,2,1,0,3:T(8,128)(2,1)S(1)}, u32[]{:S(2)}, u32[]{:S(2)}) collective-permute-start(bf16[2,2,2,2,32,256]{5,4,2,1,0,3:T(8,128)(2,1)} %slice_bitcast_fusion.14), channel_id=1, source_target_pairs={{0,2},{1,3},{2,0},{3,1},{4,6},{5,7},{6,4},{7,5},{8,10},{9,11},{10,... | collective-permute-start | bytes 786440 | tf_op jit(solution)/shard_map/ppermute | solution.py:1119
  169.5 12.9 %collective-permute-start.15 = (bf16[512,256]{1,0:T(8,128)(2,1)S(1)}, bf16[512,256]{1,0:T(8,128)(2,1)S(1)}, u32[]{:S(2)}, u32[]{:S(2)}) collective-permute-start(bf16[512,256]{1,0:T(8,128)(2,1)S(1)} %copy-done.32), channel_id=1, source_target_pairs={{0,2},{1,3},{2,0},{3,1},{4,6},{5,7},{6,4},{7,5},{8,10},{9,11},{10,... | collective-permute-start | bytes 786440 | tf_op jit(solution)/shard_map/ppermute | solution.py:1119
  173.1 4.7 %collective-permute-start.33 = (f32[40,512]{1,0:T(8,128)S(1)}, f32[40,512]{1,0:T(8,128)S(1)}, u32[]{:S(2)}, u32[]{:S(2)}) collective-permute-start(f32[40,512]{1,0:T(8,128)S(1)} %add.219), channel_id=1, source_target_pairs={{0,1},{1,0},{2,3},{3,2},{4,5},{5,4},{6,7},{7,6},{8,9},{9,8},{10,11... | collective-permute-start | bytes 245768 | tf_op jit(solution)/shard_map/ppermute | solution.py:1119
  177.8 4.5 %collective-permute-start.34 = (f32[40,512]{1,0:T(8,128)S(1)}, f32[40,512]{1,0:T(8,128)S(1)}, u32[]{:S(2)}, u32[]{:S(2)}) collective-permute-start(f32[40,512]{1,0:T(8,128)S(1)} %add.220), channel_id=1, source_target_pairs={{0,4},{1,5},{2,6},{3,7},{4,0},{5,1},{6,2},{7,3},{8,12},{9,13},{10,... | collective-permute-start | bytes 245768 | tf_op jit(solution)/shard_map/ppermute | solution.py:1119
  182.3 18.8 %collective-permute-start.18 = (bf16[512,256]{1,0:T(8,128)(2,1)S(1)}, bf16[512,256]{1,0:T(8,128)(2,1)S(1)}, u32[]{:S(2)}, u32[]{:S(2)}) collective-permute-start(bf16[512,256]{1,0:T(8,128)(2,1)S(1)} %copy-done.31), channel_id=1, source_target_pairs={{0,2},{1,3},{2,0},{3,1},{4,6},{5,7},{6,4},{7,5},{8,10},{9,11},{10,... | collective-permute-start | bytes 786440 | tf_op jit(solution)/shard_map/ppermute | solution.py:1119
  182.4 52.8 %collective-permute-start.56 = (bf16[2,2,2,128,256]{4,3,2,1,0:T(8,128)(2,1)S(1)}, bf16[2,2,2,128,256]{4,3,2,1,0:T(8,128)(2,1)S(1)}, u32[]{:S(2)}, u32[]{:S(2)}) collective-permute-start(bf16[2,2,2,128,256]{4,3,2,1,0:T(8,128)(2,1)S(1)} %dynamic-slice_bitcast_fusion.1), channel_id=1, source_target_pairs={{0,1},{1,0},{2,3},{3,2},{4,5},{5,4},{6,7},{7,6},{8,9},{9,8},{10,11... | collective-permute-start | bytes 1572872 | tf_op jit(solution)/shard_map/ppermute | solution.py:1119
  201.1 34.7 %collective-permute-start.51 = (bf16[2,2,2,128,256]{4,3,2,1,0:T(8,128)(2,1)S(1)}, bf16[2,2,2,128,256]{4,3,2,1,0:T(8,128)(2,1)S(1)}, u32[]{:S(2)}, u32[]{:S(2)}) collective-permute-start(bf16[2,2,2,128,256]{4,3,2,1,0:T(8,128)(2,1)S(1)} %dynamic-slice_bitcast_fusion.2), channel_id=1, source_target_pairs={{0,4},{1,5},{2,6},{3,7},{4,0},{5,1},{6,2},{7,3},{8,12},{9,13},{10,... | collective-permute-start | bytes 1572872 | tf_op jit(solution)/shard_map/ppermute | solution.py:1119
  218.8 4.5 %collective-permute-start.35 = (f32[40,512]{1,0:T(8,128)S(1)}, f32[40,512]{1,0:T(8,128)S(1)}, u32[]{:S(2)}, u32[]{:S(2)}) collective-permute-start(f32[40,512]{1,0:T(8,128)S(1)} %add.221), channel_id=1, source_target_pairs={{0,8},{1,9},{2,10},{3,11},{4,12},{5,13},{6,14},{7,15},{8,0},{9,1},... | collective-permute-start | bytes 245768 | tf_op jit(solution)/shard_map/ppermute | solution.py:1119
  223.3 66.7 %collective-permute-start.37 = (bf16[2,2,2,2,128,256]{5,4,3,2,1,0:T(8,128)(2,1)}, bf16[2,2,2,2,128,256]{5,4,3,2,1,0:T(8,128)(2,1)}, u32[]{:S(2)}, u32[]{:S(2)}) collective-permute-start(bf16[2,2,2,2,128,256]{5,4,3,2,1,0:T(8,128)(2,1)} %slice_bitcast_fusion.2), channel_id=1, source_target_pairs={{0,2},{1,3},{2,0},{3,1},{4,6},{5,7},{6,4},{7,5},{8,10},{9,11},{10,... | collective-permute-start | bytes 3145736 | tf_op jit(solution)/shard_map/ppermute | solution.py:1119
  223.3 7.6 %collective-permute-start.36 = (f32[40,512]{1,0:T(8,128)S(1)}, f32[40,512]{1,0:T(8,128)S(1)}, u32[]{:S(2)}, u32[]{:S(2)}) collective-permute-start(f32[40,512]{1,0:T(8,128)S(1)} %add.222), channel_id=1, source_target_pairs={{0,16},{1,17},{2,18},{3,19},{4,20},{5,21},{6,22},{7,23},{8,24},{9,... | collective-permute-start | bytes 245768 | tf_op jit(solution)/shard_map/ppermute | solution.py:1119
  230.9 65.7 %collective-permute-start.27 = (bf16[2,2,2,2,128,256]{5,4,3,2,1,0:T(8,128)(2,1)}, bf16[2,2,2,2,128,256]{5,4,3,2,1,0:T(8,128)(2,1)}, u32[]{:S(2)}, u32[]{:S(2)}) collective-permute-start(bf16[2,2,2,2,128,256]{5,4,3,2,1,0:T(8,128)(2,1)} %slice_bitcast_fusion.3), channel_id=1, source_target_pairs={{0,2},{1,3},{2,0},{3,1},{4,6},{5,7},{6,4},{7,5},{8,10},{9,11},{10,... | collective-permute-start | bytes 3145736 | tf_op jit(solution)/shard_map/ppermute | solution.py:1119
  235.2 3.1 collective-permute-start.45
  235.8 1.8 collective-permute-start.22
  237.6 41.3 %collective-permute-start.19 = (bf16[3,512,256]{2,1,0:T(8,128)(2,1)}, bf16[3,512,256]{2,1,0:T(8,128)(2,1)}, u32[]{:S(2)}, u32[]{:S(2)}) collective-permute-start(bf16[3,512,256]{2,1,0:T(8,128)(2,1)} %get-tuple-element.131), channel_id=1, source_target_pairs={{0,2},{1,3},{2,0},{3,1},{4,6},{5,7},{6,4},{7,5},{8,10},{9,11},{10,... | collective-permute-start | bytes 2359304 | tf_op jit(solution)/shard_map/ppermute | solution.py:1119
  238.0 45.8 %collective-permute-start.16 = (bf16[3,512,256]{2,1,0:T(8,128)(2,1)}, bf16[3,512,256]{2,1,0:T(8,128)(2,1)}, u32[]{:S(2)}, u32[]{:S(2)}) collective-permute-start(bf16[3,512,256]{2,1,0:T(8,128)(2,1)} %get-tuple-element.118), channel_id=1, source_target_pairs={{0,2},{1,3},{2,0},{3,1},{4,6},{5,7},{6,4},{7,5},{8,10},{9,11},{10,... | collective-permute-start | bytes 2359304 | tf_op jit(solution)/shard_map/ppermute | solution.py:1119
  238.3 8.6 %collective-permute-start.57 = (bf16[2,2,128,256]{3,2,1,0:T(8,128)(2,1)S(1)}, bf16[2,2,128,256]{3,2,1,0:T(8,128)(2,1)S(1)}, u32[]{:S(2)}, u32[]{:S(2)}) collective-permute-start(bf16[2,2,128,256]{3,2,1,0:T(8,128)(2,1)S(1)} %dynamic-slice_bitcast_fusion.7), channel_id=1, source_target_pairs={{0,4},{1,5},{2,6},{3,7},{4,0},{5,1},{6,2},{7,3},{8,12},{9,13},{10,... | collective-permute-start | bytes 786440 | tf_op jit(solution)/shard_map/ppermute | solution.py:1119
  246.8 7.8 %collective-permute-start.52 = (bf16[2,2,128,256]{3,2,1,0:T(8,128)(2,1)S(1)}, bf16[2,2,128,256]{3,2,1,0:T(8,128)(2,1)S(1)}, u32[]{:S(2)}, u32[]{:S(2)}) collective-permute-start(bf16[2,2,128,256]{3,2,1,0:T(8,128)(2,1)S(1)} %dynamic-slice_bitcast_fusion.8), channel_id=1, source_target_pairs={{0,1},{1,0},{2,3},{3,2},{4,5},{5,4},{6,7},{7,6},{8,9},{9,8},{10,11... | collective-permute-start | bytes 786440 | tf_op jit(solution)/shard_map/ppermute | solution.py:1119
  254.6 5.0 %collective-permute-start.58 = (bf16[2,128,256]{2,1,0:T(8,128)(2,1)S(1)}, bf16[2,128,256]{2,1,0:T(8,128)(2,1)S(1)}, u32[]{:S(2)}, u32[]{:S(2)}) collective-permute-start(bf16[2,128,256]{2,1,0:T(8,128)(2,1)S(1)} %dynamic-slice_bitcast_fusion.13), channel_id=1, source_target_pairs={{0,8},{1,9},{2,10},{3,11},{4,12},{5,13},{6,14},{7,15},{8,0},{9,1},... | collective-permute-start | bytes 393224 | tf_op jit(solution)/shard_map/ppermute | solution.py:1119
  259.6 5.7 %collective-permute-start.53 = (bf16[2,128,256]{2,1,0:T(8,128)(2,1)S(1)}, bf16[2,128,256]{2,1,0:T(8,128)(2,1)S(1)}, u32[]{:S(2)}, u32[]{:S(2)}) collective-permute-start(bf16[2,128,256]{2,1,0:T(8,128)(2,1)S(1)} %dynamic-slice_bitcast_fusion.14), channel_id=1, source_target_pairs={{0,8},{1,9},{2,10},{3,11},{4,12},{5,13},{6,14},{7,15},{8,0},{9,1},... | collective-permute-start | bytes 393224 | tf_op jit(solution)/shard_map/ppermute | solution.py:1119
  265.2 6.5 %collective-permute-start.59 = (bf16[128,256]{1,0:T(8,128)(2,1)S(1)}, bf16[128,256]{1,0:T(8,128)(2,1)S(1)}, u32[]{:S(2)}, u32[]{:S(2)}) collective-permute-start(bf16[128,256]{1,0:T(8,128)(2,1)S(1)} %dynamic-slice_bitcast_fusion.19), channel_id=1, source_target_pairs={{0,16},{1,17},{2,18},{3,19},{4,20},{5,21},{6,22},{7,23},{8,24},{9,... | collective-permute-start | bytes 196616 | tf_op jit(solution)/shard_map/ppermute | solution.py:1119
  271.7 5.7 %collective-permute-start.54 = (bf16[128,256]{1,0:T(8,128)(2,1)S(1)}, bf16[128,256]{1,0:T(8,128)(2,1)S(1)}, u32[]{:S(2)}, u32[]{:S(2)}) collective-permute-start(bf16[128,256]{1,0:T(8,128)(2,1)S(1)} %dynamic-slice_bitcast_fusion.20), channel_id=1, source_target_pairs={{0,16},{1,17},{2,18},{3,19},{4,20},{5,21},{6,22},{7,23},{8,24},{9,... | collective-permute-start | bytes 196616 | tf_op jit(solution)/shard_map/ppermute | solution.py:1119
  277.4 17.8 %collective-permute-start.23 = (bf16[2,2,2,128,256]{4,3,1,0,2:T(8,128)(2,1)}, bf16[2,2,2,128,256]{4,3,1,0,2:T(8,128)(2,1)}, u32[]{:S(2)}, u32[]{:S(2)}) collective-permute-start(bf16[2,2,2,128,256]{4,3,1,0,2:T(8,128)(2,1)} %dynamic-slice_bitcast_fusion.6), channel_id=1, source_target_pairs={{0,4},{1,5},{2,6},{3,7},{4,0},{5,1},{6,2},{7,3},{8,12},{9,13},{10,... | collective-permute-start | bytes 1572872 | tf_op jit(solution)/shard_map/ppermute | solution.py:1119
  278.9 64.9 %collective-permute-start.46 = (bf16[2,2,2,256,256]{4,3,1,0,2:T(8,128)(2,1)}, bf16[2,2,2,256,256]{4,3,1,0,2:T(8,128)(2,1)S(1)}, u32[]{:S(2)}, u32[]{:S(2)}) collective-permute-start(bf16[2,2,2,256,256]{4,3,1,0,2:T(8,128)(2,1)} %dynamic-slice_bitcast_fusion), channel_id=1, source_target_pairs={{0,1},{1,0},{2,3},{3,2},{4,5},{5,4},{6,7},{7,6},{8,9},{9,8},{10,11... | collective-permute-start | bytes 3145736 | tf_op jit(solution)/shard_map/ppermute | solution.py:1119
  283.9 39.4 %collective-permute-start.20 = (bf16[512,512]{1,0:T(8,128)(2,1)}, bf16[512,512]{1,0:T(8,128)(2,1)S(1)}, u32[]{:S(2)}, u32[]{:S(2)}) collective-permute-start(bf16[512,512]{1,0:T(8,128)(2,1)} %target_grad.1), channel_id=1, source_target_pairs={{0,0},{1,2},{2,1},{3,3},{4,4},{5,6},{6,5},{7,7},{8,8},{9,10},{10,9... | collective-permute-start | bytes 1572872 | tf_op jit(solution)/shard_map/ppermute | solution.py:1119
  290.0 36.0 %collective-permute-start.17 = (bf16[512,512]{1,0:T(8,128)(2,1)}, bf16[512,512]{1,0:T(8,128)(2,1)S(1)}, u32[]{:S(2)}, u32[]{:S(2)}) collective-permute-start(bf16[512,512]{1,0:T(8,128)(2,1)} %source_grad.1), channel_id=1, source_target_pairs={{0,0},{1,2},{2,1},{3,3},{4,4},{5,6},{6,5},{7,7},{8,8},{9,10},{10,9... | collective-permute-start | bytes 1572872 | tf_op jit(solution)/shard_map/ppermute | solution.py:1119
  295.2 30.7 %collective-permute-start.38 = (bf16[2,2,2,128,256]{4,3,2,1,0:T(8,128)(2,1)S(1)}, bf16[2,2,2,128,256]{4,3,2,1,0:T(8,128)(2,1)S(1)}, u32[]{:S(2)}, u32[]{:S(2)}) collective-permute-start(bf16[2,2,2,128,256]{4,3,2,1,0:T(8,128)(2,1)S(1)} %dynamic-slice_bitcast_fusion.4), channel_id=1, source_target_pairs={{0,1},{1,0},{2,3},{3,2},{4,5},{5,4},{6,7},{7,6},{8,9},{9,8},{10,11... | collective-permute-start | bytes 1572872 | tf_op jit(solution)/shard_map/ppermute | solution.py:1119
  296.7 25.4 %collective-permute-start.24 = (bf16[2,2,128,256]{3,2,0,1:T(8,128)(2,1)S(1)}, bf16[2,2,128,256]{3,2,0,1:T(8,128)(2,1)S(1)}, u32[]{:S(2)}, u32[]{:S(2)}) collective-permute-start(bf16[2,2,128,256]{3,2,0,1:T(8,128)(2,1)S(1)} %dynamic-slice_bitcast_fusion.12), channel_id=1, source_target_pairs={{0,1},{1,0},{2,3},{3,2},{4,5},{5,4},{6,7},{7,6},{8,9},{9,8},{10,11... | collective-permute-start | bytes 786440 | tf_op jit(solution)/shard_map/ppermute | solution.py:1119
  322.1 14.5 %collective-permute-start.28 = (bf16[2,2,2,128,256]{4,3,2,1,0:T(8,128)(2,1)S(1)}, bf16[2,2,2,128,256]{4,3,2,1,0:T(8,128)(2,1)S(1)}, u32[]{:S(2)}, u32[]{:S(2)}) collective-permute-start(bf16[2,2,2,128,256]{4,3,2,1,0:T(8,128)(2,1)S(1)} %dynamic-slice_bitcast_fusion.5), channel_id=1, source_target_pairs={{0,4},{1,5},{2,6},{3,7},{4,0},{5,1},{6,2},{7,3},{8,12},{9,13},{10,... | collective-permute-start | bytes 1572872 | tf_op jit(solution)/shard_map/ppermute | solution.py:1119
  323.3 13.4 %collective-permute-start.25 = (bf16[2,128,256]{2,1,0:T(8,128)(2,1)S(1)}, bf16[2,128,256]{2,1,0:T(8,128)(2,1)S(1)}, u32[]{:S(2)}, u32[]{:S(2)}) collective-permute-start(bf16[2,128,256]{2,1,0:T(8,128)(2,1)S(1)} %dynamic-slice_bitcast_fusion.18), channel_id=1, source_target_pairs={{0,8},{1,9},{2,10},{3,11},{4,12},{5,13},{6,14},{7,15},{8,0},{9,1},... | collective-permute-start | bytes 393224 | tf_op jit(solution)/shard_map/ppermute | solution.py:1119
  326.2 19.1 %collective-permute-start.39 = (bf16[2,2,128,256]{3,2,1,0:T(8,128)(2,1)S(1)}, bf16[2,2,128,256]{3,2,1,0:T(8,128)(2,1)S(1)}, u32[]{:S(2)}, u32[]{:S(2)}) collective-permute-start(bf16[2,2,128,256]{3,2,1,0:T(8,128)(2,1)S(1)} %dynamic-slice_bitcast_fusion.10), channel_id=1, source_target_pairs={{0,4},{1,5},{2,6},{3,7},{4,0},{5,1},{6,2},{7,3},{8,12},{9,13},{10,... | collective-permute-start | bytes 786440 | tf_op jit(solution)/shard_map/ppermute | solution.py:1119
  336.8 5.7 %collective-permute-start.26 = (bf16[128,256]{1,0:T(8,128)(2,1)S(1)}, bf16[128,256]{1,0:T(8,128)(2,1)S(1)}, u32[]{:S(2)}, u32[]{:S(2)}) collective-permute-start(bf16[128,256]{1,0:T(8,128)(2,1)S(1)} %dynamic-slice_bitcast_fusion.23), channel_id=1, source_target_pairs={{0,16},{1,17},{2,18},{3,19},{4,20},{5,21},{6,22},{7,23},{8,24},{9,... | collective-permute-start | bytes 196616 | tf_op jit(solution)/shard_map/ppermute | solution.py:1119
  339.2 9.6 %collective-permute-start.29 = (bf16[2,2,128,256]{3,2,1,0:T(8,128)(2,1)S(1)}, bf16[2,2,128,256]{3,2,1,0:T(8,128)(2,1)S(1)}, u32[]{:S(2)}, u32[]{:S(2)}) collective-permute-start(bf16[2,2,128,256]{3,2,1,0:T(8,128)(2,1)S(1)} %dynamic-slice_bitcast_fusion.11), channel_id=1, source_target_pairs={{0,1},{1,0},{2,3},{3,2},{4,5},{5,4},{6,7},{7,6},{8,9},{9,8},{10,11... | collective-permute-start | bytes 786440 | tf_op jit(solution)/shard_map/ppermute | solution.py:1119
  344.1 13.8 %collective-permute-start.47 = (bf16[2,2,256,256]{3,2,0,1:T(8,128)(2,1)S(1)}, bf16[2,2,256,256]{3,2,0,1:T(8,128)(2,1)S(1)}, u32[]{:S(2)}, u32[]{:S(2)}) collective-permute-start(bf16[2,2,256,256]{3,2,0,1:T(8,128)(2,1)S(1)} %dynamic-slice_bitcast_fusion.3), channel_id=1, source_target_pairs={{0,4},{1,5},{2,6},{3,7},{4,0},{5,1},{6,2},{7,3},{8,12},{9,13},{10,... | collective-permute-start | bytes 1572872 | tf_op jit(solution)/shard_map/ppermute | solution.py:1119
  345.4 6.9 %collective-permute-start.40 = (bf16[2,128,256]{2,1,0:T(8,128)(2,1)S(1)}, bf16[2,128,256]{2,1,0:T(8,128)(2,1)S(1)}, u32[]{:S(2)}, u32[]{:S(2)}) collective-permute-start(bf16[2,128,256]{2,1,0:T(8,128)(2,1)S(1)} %dynamic-slice_bitcast_fusion.16), channel_id=1, source_target_pairs={{0,8},{1,9},{2,10},{3,11},{4,12},{5,13},{6,14},{7,15},{8,0},{9,1},... | collective-permute-start | bytes 393224 | tf_op jit(solution)/shard_map/ppermute | solution.py:1119
  348.8 7.0 %collective-permute-start.30 = (bf16[2,128,256]{2,1,0:T(8,128)(2,1)S(1)}, bf16[2,128,256]{2,1,0:T(8,128)(2,1)S(1)}, u32[]{:S(2)}, u32[]{:S(2)}) collective-permute-start(bf16[2,128,256]{2,1,0:T(8,128)(2,1)S(1)} %dynamic-slice_bitcast_fusion.17), channel_id=1, source_target_pairs={{0,8},{1,9},{2,10},{3,11},{4,12},{5,13},{6,14},{7,15},{8,0},{9,1},... | collective-permute-start | bytes 393224 | tf_op jit(solution)/shard_map/ppermute | solution.py:1119
  352.3 11.9 %collective-permute-start.41 = (bf16[128,256]{1,0:T(8,128)(2,1)S(1)}, bf16[128,256]{1,0:T(8,128)(2,1)S(1)}, u32[]{:S(2)}, u32[]{:S(2)}) collective-permute-start(bf16[128,256]{1,0:T(8,128)(2,1)S(1)} %dynamic-slice_bitcast_fusion.21), channel_id=1, source_target_pairs={{0,16},{1,17},{2,18},{3,19},{4,20},{5,21},{6,22},{7,23},{8,24},{9,... | collective-permute-start | bytes 196616 | tf_op jit(solution)/shard_map/ppermute | solution.py:1119
  358.0 19.9 %copy-start.12 = (bf16[512,512]{1,0:T(8,128)(2,1)S(1)}, bf16[512,512]{1,0:T(8,128)(2,1)}, u32[]{:S(2)}) copy-start(bf16[512,512]{1,0:T(8,128)(2,1)} %copy-done.11) | copy-start | bytes 1572868
  358.1 10.6 %collective-permute-start.48 = (bf16[2,256,256]{2,1,0:T(8,128)(2,1)S(1)}, bf16[2,256,256]{2,1,0:T(8,128)(2,1)S(1)}, u32[]{:S(2)}, u32[]{:S(2)}) collective-permute-start(bf16[2,256,256]{2,1,0:T(8,128)(2,1)S(1)} %dynamic-slice_bitcast_fusion.9), channel_id=1, source_target_pairs={{0,8},{1,9},{2,10},{3,11},{4,12},{5,13},{6,14},{7,15},{8,0},{9,1},... | collective-permute-start | bytes 786440 | tf_op jit(solution)/shard_map/ppermute | solution.py:1119
  361.6 17.1 %copy-start.16 = (bf16[512,512]{1,0:T(8,128)(2,1)S(1)}, bf16[512,512]{1,0:T(8,128)(2,1)}, u32[]{:S(2)}) copy-start(bf16[512,512]{1,0:T(8,128)(2,1)} %copy-done.15) | copy-start | bytes 1572868
  361.6 8.9 %collective-permute-start.31 = (bf16[128,256]{1,0:T(8,128)(2,1)S(1)}, bf16[128,256]{1,0:T(8,128)(2,1)S(1)}, u32[]{:S(2)}, u32[]{:S(2)}) collective-permute-start(bf16[128,256]{1,0:T(8,128)(2,1)S(1)} %dynamic-slice_bitcast_fusion.22), channel_id=1, source_target_pairs={{0,16},{1,17},{2,18},{3,19},{4,20},{5,21},{6,22},{7,23},{8,24},{9,... | collective-permute-start | bytes 196616 | tf_op jit(solution)/shard_map/ppermute | solution.py:1119
  368.8 7.8 %collective-permute-start.49 = (bf16[256,256]{1,0:T(8,128)(2,1)S(1)}, bf16[256,256]{1,0:T(8,128)(2,1)S(1)}, u32[]{:S(2)}, u32[]{:S(2)}) collective-permute-start(bf16[256,256]{1,0:T(8,128)(2,1)S(1)} %dynamic-slice_bitcast_fusion.15), channel_id=1, source_target_pairs={{0,16},{1,17},{2,18},{3,19},{4,20},{5,21},{6,22},{7,23},{8,24},{9,... | collective-permute-start | bytes 393224 | tf_op jit(solution)/shard_map/ppermute | solution.py:1119
  (32 other events, 140.8 us)

commit v2 on v0

--- a/solution.py
+++ b/solution.py
@@ -1,12 +1,16 @@
+import types
+
 import jax
 import jax.numpy as jnp
 from jax import lax
+from jax.experimental import pallas as pl
+from jax.experimental.pallas import tpu as pltpu
 from jax.sharding import PartitionSpec as P
 
 HEAD_DIM = 64
-
-
 NEGATIVE = -1e30
+BF = jnp.bfloat16
+F32 = jnp.float32
 
 
 def layer_norm(value, gain, shift):
@@ -202,7 +206,7 @@
     return (query_grad, key_sum, value_sum)
 
 
-def shards(
+def general_shards(
     source,
     target,
     source_ids,
@@ -522,7 +526,7 @@
     )
 
 
-def solution(mesh):
+def general(mesh):
     placed = (
         P("batch", "seq", None),
         P("batch", "seq", None),
@@ -549,7 +553,7 @@
         P(),
     )
     return jax.shard_map(
-        shards,
+        general_shards,
         mesh=mesh,
         in_specs=placed,
         out_specs=(
@@ -577,3 +581,1333 @@
         ),
         check_vma=False,
     )
+
+
+BATCH, SEQ = "batch", "seq"
+CORE, X, Y, LOW, HIGH, SWAP = range(6)
+ALL = (CORE, X, Y, LOW, HIGH)
+TILE = 256
+MESH = pl.DeviceIdType.MESH
+VMEM = pl.BlockSpec(memory_space=pltpu.VMEM)
+ANY = pl.BlockSpec(memory_space=pl.ANY)
+
+
+def dot(left, right, left_dim=1, right_dim=0):
+    return lax.dot_general(
+        left, right, (((left_dim,), (right_dim,)), ((), ())), preferred_element_type=F32
+    )
+
+
+def block(index, size):
+    return pl.ds(pl.multiple_of(index * size, size), size)
+
+
+def normed(value):
+    centred = value - jnp.mean(value, axis=-1, keepdims=True)
+    scale = lax.rsqrt(jnp.mean(centred * centred, axis=-1, keepdims=True) + 1e-06)
+    return centred * scale, scale
+
+
+def normed_back(grad, unit, scale, gain):
+    scaled = grad * gain
+    first = jnp.mean(scaled, axis=-1, keepdims=True)
+    second = jnp.mean(scaled * unit, axis=-1, keepdims=True)
+    return scale * (scaled - first - unit * second)
+
+
+def gelu_and_slope(inner):
+    square = inner * inner
+    bent = jnp.tanh(0.7978845608028654 * inner * (1.0 + 0.044715 * square))
+    half = 0.5 * (1.0 + bent)
+    slope = half + 0.5 * inner * (1.0 - bent * bent) * (
+        0.7978845608028654 * (1.0 + 0.134145 * square)
+    )
+    return inner * half, slope
+
+
+def column_sum(value):
+    return jnp.sum(value, axis=0, keepdims=True)
+
+
+def parts_of(up):
+    return [slice(p * 512, (p + 1) * 512) for p in range(up.shape[1] // 512)]
+
+
+def over_tiles(rows):
+    def run(body):
+        @pl.loop(0, rows // TILE)
+        def _(tile):
+            body(block(tile, TILE))
+
+    return run
+
+
+def places():
+    row, s = lax.axis_index(BATCH), lax.axis_index(SEQ)
+    core = lax.rem(row, 2)
+    y = lax.rem(row // 2, 2)
+    low = lax.rem(row // 4, 2)
+    high = row // 8
+    mine = (core, s, y, low, high + core - 2 * high * core)
+    partner = (
+        {BATCH: row + 1 - 2 * core},
+        {SEQ: 1 - s},
+        {BATCH: row + 2 - 4 * y},
+        {BATCH: row + 4 - 8 * low},
+        {BATCH: row + 8 - 16 * high},
+        {BATCH: row - core + s, SEQ: core},
+    )
+    return mine, partner
+
+
+def my_core():
+    return places()[0][CORE]
+
+
+def call_out(ways):
+    mine, partner = places()
+    barrier = pltpu.get_barrier_semaphore()
+    for way in ways:
+        pl.semaphore_signal(barrier, inc=1, device_id=partner[way], device_id_type=MESH)
+
+    @pl.when(mine[CORE] != mine[X])
+    def _():
+        pl.semaphore_signal(barrier, inc=1, device_id=partner[SWAP], device_id_type=MESH)
+
+
+def hear(ways):
+    mine, _ = places()
+    away = mine[CORE] + mine[X] - 2 * mine[CORE] * mine[X]
+    pl.semaphore_wait(pltpu.get_barrier_semaphore(), len(ways) + away)
+
+
+def sending(source, target, sems, slot, way):
+    return pltpu.make_async_remote_copy(
+        src_ref=source,
+        dst_ref=target,
+        send_sem=sems.at[0, slot],
+        recv_sem=sems.at[1, slot],
+        device_id=places()[1][way],
+        device_id_type=MESH,
+    )
+
+
+def start_swap(source, target, sems, slot):
+    mine, _ = places()
+
+    @pl.when(mine[CORE] != mine[X])
+    def _():
+        sending(source, target, sems, slot, SWAP).start()
+
+    @pl.when(mine[CORE] == mine[X])
+    def _():
+        pltpu.make_async_copy(source, target, sems.at[0, slot]).start()
+
+
+def wait_swap(source, target, sems, slot):
+    mine, _ = places()
+
+    @pl.when(mine[CORE] != mine[X])
+    def _():
+        sending(source, target, sems, slot, SWAP).wait()
+
+    @pl.when(mine[CORE] == mine[X])
+    def _():
+        pltpu.make_async_copy(source, target, sems.at[0, slot]).wait()
+
+
+class RowSwap:
+    def __init__(self, source, target, pieces, sems, slot, near_sem):
+        mine, _ = places()
+        self.here = mine[CORE] == mine[X]
+        self.pieces = range(len(pieces))
+        whole = target(mine[X], None)
+        self.near = lambda: pltpu.make_async_copy(source, whole, near_sem)
+        self.early = lambda: sending(source, whole, sems, slot, CORE)
+        self.across = lambda k: sending(source.at[pieces[k]], target(mine[X], pieces[k]), sems, slot + 1 + k, SWAP)
+
+        def onward(k):
+            ref = target(mine[CORE], pieces[k])
+            return sending(ref, ref, sems, slot + 1 + len(pieces) + k, CORE)
+
+        self.onward = onward
+
+    def start(self):
+        @pl.when(self.here)
+        def _():
+            self.near().start()
+            self.early().start()
+
+        @pl.when(jnp.logical_not(self.here))
+        def _():
+            for k in self.pieces:
+                self.across(k).start()
+
+    def pass_on(self):
+        @pl.when(jnp.logical_not(self.here))
+        def _():
+            for k in self.pieces:
+                self.across(k).wait()
+                self.onward(k).start()
+
+    def finish(self):
+        @pl.when(self.here)
+        def _():
+            self.near().wait()
+            self.early().wait_send()
+            for k in self.pieces:
+                self.onward(k).wait_recv()
+
+        @pl.when(jnp.logical_not(self.here))
+        def _():
+            self.early().wait_recv()
+            for k in self.pieces:
+                self.onward(k).wait_send()
+
+
+def part_of(ref, axis, index):
+    return ref.at[(slice(None),) * axis + (index,)]
+
+
+class Halving:
+    def __init__(self, source, axis, way, got, total, sems, slot, far=False):
+        mine, _ = places()
+        kept = part_of(source, axis, mine[way])
+        self.kept, self.got, self.total = (total if far else kept), got, total
+        self.sent = lambda: sending(part_of(source, axis, 1 - mine[way]), got, sems, slot, way)
+        self.near = (lambda: pltpu.make_async_copy(kept, total, sems.at[2, slot])) if far else None
+
+    def start(self):
+        self.sent().start()
+        if self.near is not None:
+            self.near().start()
+
+    def finish(self):
+        if self.near is not None:
+            self.near().wait()
+        self.sent().wait()
+        if self.total.dtype == F32:
+            self.total[...] = self.kept[...].astype(F32) + self.got[...].astype(F32)
+        else:
+            self.total[...] = self.kept[...] + self.got[...]
+
+
+class Across:
+    def __init__(self, sums, got, sems, slot):
+        self.sums, self.got = sums, got
+        self.sent = lambda: sending(sums.at[1], got, sems, slot, CORE)
+
+    def start(self):
+        self.sent().start()
+
+    def finish(self):
+        self.sent().wait()
+        self.sums[0] = self.sums[0] + self.got[...]
+
+
+class Copies:
+    def __init__(self, pairs, sems, first=0):
+        self.copies = [
+            (lambda source=source, target=target, place=place: pltpu.make_async_copy(source, target, sems.at[first + place]))
+            for place, (source, target) in enumerate(pairs)
+        ]
+
+    def start(self):
+        for copy in self.copies:
+            copy().start()
+
+    def wait(self):
+        for copy in self.copies:
+            copy().wait()
+
+
+def attend_begin(r, att):
+    heads = r.queries.shape[1]
+    width = heads * HEAD_DIM
+    columns = block(my_core(), width)
+    q_from, k_from = att, att + att // 2
+    q_side, k_side = jnp.minimum(att, 1), att * (2 - att)
+    which = lax.rem(att, 2)
+    place = lax.broadcasted_iota(jnp.int32, (HEAD_DIM, TILE), 0)
+    ones = (lax.broadcasted_iota(jnp.int32, (TILE, HEAD_DIM), 1) < 3).astype(BF)
+    half_tiles = r.ids.shape[3] // TILE
+
+    @pl.loop(0, r.x_all.shape[1] // TILE)
+    def _(tile):
+        here = block(tile, TILE)
+        lanes = block(lax.rem(tile, half_tiles), TILE)
+        q_ids = r.ids[q_side, tile // half_tiles, :, lanes]
+        k_ids = r.ids[k_side, tile // half_tiles, :, lanes]
+        asks = jnp.where(place == q_ids, 1.0, 0.0).T.astype(BF)
+        bars = jnp.where((place != k_ids) & (place < 3), NEGATIVE, 0.0).T.astype(BF)
+        left_q, left_k = r.x_all[q_from, here, :], r.x_all[k_from, here, :]
+        q_tile = dot(left_q, r.weights[att, 0, :, columns]).astype(BF) * BF(0.125)
+        k_tile = dot(left_k, r.weights[att, 1, :, columns]).astype(BF)
+        v_tile = dot(left_k, r.weights[att, 2, :, columns]).astype(BF)
+        for head in range(heads):
+            part = slice(head * HEAD_DIM, (head + 1) * HEAD_DIM)
+            r.queries[which, head, here, :] = jnp.concatenate([q_tile[:, part], asks], axis=1)
+            r.keys[which, head, here, :] = jnp.concatenate([k_tile[:, part], bars], axis=1)
+            r.values[which, head, here, :] = jnp.concatenate([v_tile[:, part], ones], axis=1)
+
+
+def attend_head(r, which, head, causal):
+    length = r.queries.shape[2]
+    if causal:
+        lower = lax.broadcasted_iota(jnp.int32, (TILE, TILE), 0) >= lax.broadcasted_iota(
+            jnp.int32, (TILE, TILE), 1
+        )
+    for tile in range(length // TILE):
+        here = slice(tile * TILE, (tile + 1) * TILE)
+        seen = (tile + 1) * TILE if causal else length
+        scores = dot(r.queries[which, head, here, :], r.keys[which, head, :seen, :], 1, 1)
+        if causal:
+            last = jnp.where(lower, scores[:, seen - TILE :], NEGATIVE)
+            scores = last if tile == 0 else jnp.concatenate([scores[:, : seen - TILE], last], axis=1)
+        largest = jnp.max(scores, axis=-1, keepdims=True)
+        terms = jnp.exp(scores - largest)
+        total = jnp.sum(terms, axis=-1, keepdims=True)
+        low = (terms * (1.0 / total)).astype(BF)
+        r.chances[0, here, :seen] = low
+        r.outs[head, here, :] = dot(low, r.values[which, head, :seen, :])[:, :HEAD_DIM]
+
+
+def forward_body(r):
+    step = pl.program_id(0)
+    core = my_core()
+    att = jnp.minimum(step // 4, 2)
+    rows = r.source.shape[0]
+    width = r.outs.shape[0] * HEAD_DIM
+    sems = r.sems
+
+    def rows_of(side):
+        def target(half, piece):
+            first = half * rows if piece is None else half * rows + piece.start
+            count = rows if piece is None else piece.size
+            return r.x_all.at[side, pl.ds(pl.multiple_of(first, count), count)]
+
+        return target
+
+    def ids_of(side):
+        return lambda half, piece: r.ids.at[side, half]
+
+    quarters = [pl.ds(k * rows // 4, rows // 4) for k in range(4)]
+    source = RowSwap(r.source, rows_of(0), quarters, sems, 0, r.near_sems.at[0])
+    target = RowSwap(r.target, rows_of(1), quarters, sems, 9, r.near_sems.at[1])
+    one = [pl.ds(0, 1)]
+    ids = (
+        RowSwap(r.source_ids, ids_of(0), one, sems, 18, r.near_sems.at[2]),
+        RowSwap(r.target_ids, ids_of(1), one, sems, 21, r.near_sems.at[3]),
+    )
+    first_across = sending(r.x_all.at[2, block(core, rows)], r.x_all.at[2, block(core, rows)], sems, 24, CORE)
+
+    def att_across(index):
+        return sending(r.att_send.at[index], r.att_all.at[index, :, block(core, width)], sems, 25 + index, CORE)
+
+    def memory_across(tile):
+        ref = r.x_all.at[3, pl.ds(pl.multiple_of(core * rows + tile * TILE, TILE), TILE)]
+        return sending(ref, ref, sems, 28 + tile, CORE)
+
+    loads = Copies(
+        [
+            (r.enc_qkv, r.weights.at[0]), (r.dec_qkv, r.weights.at[1]), (r.cross_qkv, r.weights.at[2]),
+            (r.enc_out_far, r.enc_out), (r.dec_out_far, r.dec_out), (r.up_far, r.up), (r.down_far, r.down),
+        ],
+        r.load_sems,
+    )
+
+    def saved(index):
+        which = index % 2
+        return Copies(
+            [
+                (r.queries.at[which], r.queries_far.at[index]), (r.keys.at[which], r.keys_far.at[index]),
+                (r.values.at[which], r.values_far.at[index]), (r.wide.at[index], r.wide_far.at[index]),
+            ],
+            r.save_sems,
+            index * 4,
+        )
+
+    kept = Copies(
+        [
+            (r.unit0, r.unit0_far), (r.scale0, r.scale0_far), (r.unit1, r.unit1_far), (r.scale1, r.scale1_far),
+            (r.hidden_low, r.hidden_far), (r.act, r.act_far), (r.slope, r.slope_far), (r.first, r.first_far),
+            (r.first_unit, r.first_unit_far), (r.first_scale, r.first_scale_far), (r.x_all, r.x_far),
+        ],
+        r.save_sems,
+        12,
+    )
+    att_kept = Copies([(r.att_all, r.att_far)], r.save_sems, 23)
+
+    @pl.when(step == 0)
+    def _():
+        call_out((CORE,))
+        loads.start()
+        hear((CORE,))
+        for one_side in ids:
+            one_side.start()
+        source.start()
+        target.start()
+        start_swap(r.upstream, r.upstream_there, sems, 30)
+        for one_side in ids:
+            one_side.pass_on()
+        source.pass_on()
+        for one_side in ids:
+            one_side.finish()
+        source.finish()
+        loads.wait()
+
+    @pl.when(step == 4)
+    def _():
+        target.pass_on()
+        target.finish()
+
+    @pl.when(step == 9)
+    def _():
+        saved(0).wait()
+        first_across.wait()
+
+        @pl.loop(0, rows // TILE)
+        def _(tile):
+            memory_across(tile).wait()
+
+        kept.start()
+
+    @pl.when((step == 0) | (step == 4) | (step == 9))
+    def _():
+        attend_begin(r, att)
+
+    @pl.when((step < 4) | (step > 8))
+    def _():
+        attend_head(r, 0, lax.rem(step - att // 2, 4), False)
+
+    @pl.when((step >= 4) & (step < 8))
+    def _():
+        attend_head(r, 1, step - 4, True)
+
+    @pl.when((step == 3) | (step == 7) | (step == 12))
+    def _():
+        for half in (1 - core, core):
+            there = block(half, rows)
+            joined = jnp.concatenate([r.outs[head, there, :] for head in range(r.outs.shape[0])], axis=1)
+            r.wide[att, there, :] = joined
+            if half is core:
+                r.att_all[att, :, block(core, width)] = joined.astype(BF)
+            else:
+                r.att_send[att] = joined.astype(BF)
+                att_across(att).start()
+
+    for index, last in enumerate((3, 7, 12)):
+
+        @pl.when(step == last)
+        def _(index=index):
+            saved(index).start()
+
+    @pl.when(step == 8)
+    def _():
+        att_across(0).wait()
+        att_across(1).wait()
+
+        @over_tiles(rows)
+        def _(here):
+            own = pl.ds(pl.multiple_of(core * rows + here.start, TILE), TILE)
+            unit, scale = normed(r.x_all[1, own, :].astype(F32) + dot(r.att_all[1, here, :], r.dec_out[...]))
+            r.first_unit[here, :] = unit
+            r.first_scale[here, :] = scale
+            value = unit * r.dec_gain[0:1, :] + r.dec_shift[0:1, :]
+            r.first[here, :] = value
+            r.x_all[2, own, :] = value.astype(BF)
+
+        first_across.start()
+
+        @pl.loop(0, rows // TILE)
+        def _(tile):
+            here = block(tile, TILE)
+            own = pl.ds(pl.multiple_of(core * rows + tile * TILE, TILE), TILE)
+            unit, scale = normed(r.x_all[0, own, :].astype(F32) + dot(r.att_all[0, here, :], r.enc_out[...]))
+            r.unit0[here, :] = unit
+            r.scale0[here, :] = scale
+            hidden = unit * r.enc_gain[0:1, :] + r.enc_shift[0:1, :]
+            low = hidden.astype(BF)
+            r.hidden_low[here, :] = low
+            for part in parts_of(r.up):
+                value, bend = gelu_and_slope(dot(low, r.up[:, part]) + r.up_bias[:, part])
+                r.slope[here, part] = bend.astype(BF)
+                r.act[here, part] = value.astype(BF)
+            unit, scale = normed(hidden + dot(r.act[here, :], r.down[...]) + r.down_bias[...])
+            r.unit1[here, :] = unit
+            r.scale1[here, :] = scale
+            r.x_all[3, own, :] = (unit * r.enc_gain[1:2, :] + r.enc_shift[1:2, :]).astype(BF)
+            memory_across(tile).start()
+
+    @pl.when(step == 12)
+    def _():
+        kept.wait()
+        saved(1).wait()
+        wait_swap(r.upstream, r.upstream_there, sems, 30)
+        att_across(2).wait()
+        att_kept.start()
+        saved(2).wait()
+        att_kept.wait()
+
+
+def back_begin(r, which):
+    heads = r.queries.shape[1]
+    lane = lax.broadcasted_iota(jnp.int32, (TILE, HEAD_DIM), 1)
+
+    @over_tiles(r.queries.shape[2])
+    def _(here):
+        grad = r.grad_all[which, here, :]
+        both = grad.astype(F32) * r.wide[which, here, :]
+        for head in range(heads):
+            part = slice(head * HEAD_DIM, (head + 1) * HEAD_DIM)
+            settle = -jnp.sum(both[:, part], axis=-1, keepdims=True)
+            first = settle.astype(BF).astype(F32)
+            second = (settle - first).astype(BF).astype(F32)
+            third = settle - first - second
+            extra = jnp.where(
+                lane == 0, first, jnp.where(lane == 1, second, jnp.where(lane == 2, third, 0.0))
+            )
+            r.grads[head, here, :] = jnp.concatenate([grad[:, part], extra.astype(BF)], axis=1)
+
+
+def back_head(r, which, head, causal):
+    length = r.queries.shape[2]
+    for tile in range(length // TILE):
+        here = slice(tile * TILE, (tile + 1) * TILE)
+        seen = (tile + 1) * TILE if causal else length
+        change = dot(r.grads[head, here, :], r.values[which, head, :seen, :], 1, 1)
+        low = (r.chances[0, here, :seen].astype(F32) * change).astype(BF)
+        r.score_grads[here, :seen] = low
+        r.dq[head, here, :] = (dot(low, r.keys[which, head, :seen, :])[:, :HEAD_DIM] * 0.125).astype(BF)
+    for tile in range(length // TILE if causal else 1):
+        here = slice(tile * TILE, (tile + 1) * TILE) if causal else slice(0, length)
+        below = slice(tile * TILE, length)
+        r.dk[block(head, HEAD_DIM), here] = dot(
+            r.queries[which, head, below, :HEAD_DIM], r.score_grads[below, here], 0, 0
+        )
+        r.dv[block(head, HEAD_DIM), here] = dot(
+            r.grads[head, below, :HEAD_DIM], r.chances[0, below, here], 0, 0
+        )
+
+
+class BackEnd:
+    def __init__(self, r, which, unit, q_from, k_from, sems):
+        self.r, self.q_from, self.k_from = r, q_from, k_from
+        core = my_core()
+        rows = r.d_full.shape[2]
+        width = r.d_all.shape[2]
+        lanes = block(core, width)
+        self.other = lambda: sending(
+            r.d_all.at[:, block(1 - core, rows)], r.d_full.at[which, :, :, lanes], sems, 2 * which, CORE
+        )
+        self.own = lambda: pltpu.make_async_copy(
+            r.d_all.at[:, block(core, rows)], r.d_full.at[which, :, :, lanes], sems.at[2, 2 * which]
+        )
+        below = pl.ds(32, 96)
+        self.across = lambda: sending(r.shares.at[1], unit.at[:, :, :, 1, below], sems, 2 * which + 1, CORE)
+        self.along = lambda: pltpu.make_async_copy(r.shares.at[0], unit.at[:, :, :, 0, below], sems.at[2, 2 * which + 1])
+
+    def start(self):
+        r = self.r
+        core = my_core()
+        rows, heads = r.d_full.shape[2], r.dq.shape[0]
+
+        @pl.loop(0, 2)
+        def _(half):
+            there = block(half, rows)
+            r.d_all[0, there, :] = jnp.concatenate([r.dq[head, there, :] for head in range(heads)], axis=1)
+            r.d_all[1, there, :] = r.dk[:, there].T.astype(BF)
+            r.d_all[2, there, :] = r.dv[:, there].T.astype(BF)
+
+        self.other().start()
+        self.own().start()
+
+        @pl.loop(0, 3)
+        def _(kind):
+            x_from = jnp.where(kind == 0, self.q_from, self.k_from)
+            low = dot(r.d_all[kind], r.x_all[x_from], 0, 0).astype(BF)
+            for part in range(low.shape[0] // 32):
+                z_low, y, kept = part >> 2, (part >> 1) & 1, part & 1
+                for s in range(2):
+                    r.shares[core if kept == 0 else 1 - core, s, y, z_low, block(kind, 32), :] = low[
+                        part * 32 : (part + 1) * 32, s * 256 : (s + 1) * 256
+                    ]
+
+        self.across().start()
+        self.along().start()
+
+    def wait_grads(self):
+        self.own().wait()
+        self.other().wait()
+
+    def wait_sums(self):
+        self.along().wait()
+        self.across().wait()
+
+
+BIG = (2, 2, 2, 2, 128, 256)
+MID = BIG[1:]
+LESS = BIG[2:]
+LEAST = BIG[3:]
+OUT = (2, 2, 2, 2, 32, 256)
+HALF = (2, 2, 2, 2, 64, 256)
+
+
+def sum_up(sums, inner_low, entering):
+    core = my_core()
+
+    @pl.loop(0, 4)
+    def _(z):
+        for y in range(2):
+            low = dot(inner_low[:, block(z * 2 + y, 256)], entering[...], 0, 0).astype(BF)
+            high = z // 2
+            for kept in range(2):
+                for s in range(2):
+                    sums[
+                        core if kept == 0 else 1 - core, s, y, lax.rem(z, 2), 1 - high if kept else high, :, :
+                    ] = low[kept * 128 : (kept + 1) * 128, s * 256 : (s + 1) * 256]
+
+
+def sum_down(sums, branch_low, act):
+    core = my_core()
+
+    @pl.loop(0, act.shape[1] // 512)
+    def _(column):
+        for index in range(2):
+            low = dot(branch_low[:, index * 256 : (index + 1) * 256], act[:, block(column, 512)], 0, 0).astype(BF)
+            for part in range(8):
+                place = index * 8 + part
+                z, y, kept = place >> 2, (place >> 1) & 1, place & 1
+                for piece in range(2):
+                    slot = lax.rem(column, 2) * 2 + piece
+                    sums[
+                        core if kept == 0 else 1 - core, column // 2, y, z & 1, (z >> 1) ^ kept, block(slot, 32), :
+                    ] = low[part * 32 : (part + 1) * 32, piece * 256 : (piece + 1) * 256]
+
+
+def sum_out(sums, mixed_low, att):
+    core = my_core()
+
+    @pl.loop(0, 2)
+    def _(s):
+        low = dot(mixed_low[...], att[:, block(s, 256)], 0, 0).astype(BF)
+        for place in range(16):
+            z, y, kept = place >> 2, (place >> 1) & 1, place & 1
+            sums[core if kept == 0 else 1 - core, s, y, z & 1, (z >> 1) ^ kept, :, :] = low[
+                place * 32 : (place + 1) * 32, :
+            ]
+
+
+def split_halvings(unit, bufs, totals, sems, slot):
+    upper, lower = unit.at[:, :, :, :, pl.ds(0, 64)], unit.at[:, :, :, :, pl.ds(64, 64)]
+    return (
+        Halving(upper, 0, X, bufs.at[0], totals.at[0], sems, slot),
+        Halving(lower, 1, Y, bufs.at[1], totals.at[1], sems, slot + 1),
+    )
+
+
+def join_halvings(source, less, both, last, final, total, sems, slot):
+    return (
+        Halving(source.at[0], 0, Y, less.at[0], both.at[0], sems, slot),
+        Halving(source.at[1], 0, X, less.at[1], both.at[1], sems, slot + 1),
+        Halving(both, 1, LOW, last.at[0], last.at[1], sems, slot + 2),
+        Halving(last.at[1], 1, HIGH, final, total, sems, slot + 3),
+    )
+
+
+def decode_last_layers(r):
+    @over_tiles(r.first.shape[0])
+    def _(here):
+        unit, scale = normed(r.first[here, :] + dot(r.att[here, :], r.out_w[...]))
+        r.unit0[here, :] = unit
+        r.scale0[here, :] = scale
+        second = unit * r.dec_gain[1:2, :] + r.dec_shift[1:2, :]
+        low = second.astype(BF)
+        r.entering[here, :] = low
+        for part in parts_of(r.up):
+            value, slope = gelu_and_slope(dot(low, r.up[:, part]) + r.up_bias[:, part])
+            r.act[here, part] = value.astype(BF)
+            r.inner_low[here, part] = slope.astype(BF)
+        unit, scale = normed(second + dot(r.act[here, :], r.down[...]) + r.down_bias[...])
+        r.unit1[here, :] = unit
+        r.scale1[here, :] = scale
+        r.decoded[here, :] = (unit * r.dec_gain[2:3, :] + r.dec_shift[2:3, :]).astype(BF)
+        r.grad[here, :] = r.upstream[here, :].astype(F32)
+
+
+def layers_back(r, which):
+    vectors = r.vectors
+
+    def add(place, value):
+        vectors[which, place : place + 1, :] += value
+
+    @over_tiles(r.grad.shape[0])
+    def _(here):
+        grad, unit = r.grad[here, :], r.unit1[here, :]
+        add(7, column_sum(grad * unit))
+        add(8, column_sum(grad))
+        grad = normed_back(grad, unit, r.scale1[here, :], r.gains[which, 1:2, :])
+        branch = grad.astype(BF)
+        r.branch_low[here, :] = branch
+        add(4, column_sum(branch.astype(F32)))
+        for place, part in enumerate(parts_of(r.up)):
+            inner = (dot(branch, r.down[part, :], 1, 1) * r.inner_low[here, part].astype(F32)).astype(BF)
+            r.inner_low[here, part] = inner
+            add(place, column_sum(inner.astype(F32)))
+        grad = grad + dot(r.inner_low[here, :], r.up[...], 1, 1)
+        unit = r.unit0[here, :]
+        add(5, column_sum(grad * unit))
+        add(6, column_sum(grad))
+        grad = normed_back(grad, unit, r.scale0[here, :], r.gains[which, 0:1, :])
+        r.pre[which, here, :] = grad
+        mixed = grad.astype(BF)
+        r.mixed_low[here, :] = mixed
+        r.att_grad[here, :] = dot(mixed, r.out_w[...], 1, 1).astype(BF)
+
+
+def middle_body(r):
+    step = pl.program_id(0)
+    mine, _ = places()
+    core = mine[CORE]
+    sems = r.sems
+    rows, width = r.first.shape[0], r.d_all.shape[2]
+    cross = 2
+    before = Copies(
+        [(r.first_far, r.first), (r.att_far.at[2], r.att), (r.upstream_far, r.upstream), (r.cross_out, r.out_w)], r.load_sems
+    )
+    dec_layer = Copies([(r.dec_up, r.up), (r.dec_down, r.down)], r.load_sems, 4)
+    around = Copies(
+        [
+            (r.queries_far.at[pl.ds(2, 1)], r.queries), (r.keys_far.at[pl.ds(2, 1)], r.keys),
+            (r.values_far.at[pl.ds(2, 1)], r.values), (r.wide_far.at[pl.ds(2, 1)], r.wide), (r.x_far.at[pl.ds(2, 2)], r.x_all),
+        ],
+        r.load_sems,
+        6,
+    )
+    first_layer = Copies(
+        [
+            (r.cross_qkv, r.cross_w), (r.dec_out, r.dec_w), (r.first_unit_far, r.first_unit),
+            (r.first_scale_far, r.first_scale), (r.att_far.at[1], r.dec_att),
+        ],
+        r.load_sems,
+        11,
+    )
+    enc_layer = Copies(
+        [
+            (r.enc_up, r.up), (r.enc_down, r.down), (r.enc_out, r.out_w), (r.unit0_far, r.unit0), (r.scale0_far, r.scale0),
+            (r.unit1_far, r.unit1), (r.scale1_far, r.scale1), (r.hidden_far, r.entering), (r.act_far, r.act),
+            (r.slope_far, r.inner_low), (r.att_far.at[0], r.att),
+        ],
+        r.load_sems,
+        16,
+    )
+    down_x = Halving(r.down_sums.at[0], 0, X, r.got_a, r.mid_a, sems, 0)
+    up_y = Halving(r.up_sums.at[0], 1, Y, r.got_b, r.mid_b, sems, 1)
+    down_y = Halving(r.mid_a, 0, Y, r.got_c, r.pair.at[0], sems, 2)
+    up_x = Halving(r.mid_b, 0, X, r.got_d, r.pair.at[1], sems, 3)
+    both_low = Halving(r.pair, 1, LOW, r.got_e, r.mid_e, sems, 4)
+    both_high = Halving(r.mid_e, 1, HIGH, r.got_f, r.dec_sums, sems, 5)
+    cross_x, cross_y = split_halvings(r.unit, r.got_g, r.cross_half, sems, 6)
+    end = BackEnd(r, 0, r.unit, 0, 1, r.end_sems)
+    shared = [
+        Across(r.down_sums, r.down_got, sems, 8),
+        Across(r.up_sums, r.up_got, sems, 9),
+        Across(r.out_sums, r.out_got, sems, 10),
+    ]
+    dec_shared = Across(r.dec_out_sums, r.dec_out_got, sems, 11)
+    lanes, other_lanes = block(core, width), block(1 - core, width)
+    there = block(core, rows)
+
+    def grads_of(source, target, slot):
+        across = sending(source.at[:, other_lanes], target.at[there], sems, slot, CORE)
+        stay = pltpu.make_async_copy(source.at[:, lanes], target.at[there], sems.at[2, slot])
+        return across, stay
+
+    cross_grads = grads_of(r.att_grad, r.grad_all.at[0], 12)
+    dec_grads = grads_of(r.dec_att_grad, r.grads_far.at[1], 13)
+    enc_grads = grads_of(r.att_grad, r.grads_far.at[0], 14)
+    beside = pltpu.make_async_copy(r.out_sums.at[0], r.unit.at[:, :, :, :, pl.ds(0, 32)], sems.at[2, 15])
+    results = Copies(
+        [
+            (r.down_sums.at[0], r.down_unit), (r.up_sums.at[0], r.up_unit), (r.out_sums.at[0], r.out_units.at[0]),
+            (r.dec_out_sums.at[0], r.out_units.at[1]), (r.pre, r.pre_far),
+        ],
+        r.load_sems,
+        27,
+    )
+
+    @pl.when(step == 0)
+    def _():
+        call_out(ALL)
+        before.start()
+        dec_layer.start()
+        around.start()
+        r.vectors[...] = jnp.zeros_like(r.vectors)
+        for place, (ref, row) in enumerate(((r.dec_gain, 1), (r.dec_gain, 2), (r.enc_gain, 0), (r.enc_gain, 1))):
+            r.gains[place // 2, place % 2 : place % 2 + 1, :] = ref[row : row + 1, :]
+        before.wait()
+        dec_layer.wait()
+        decode_last_layers(r)
+        hear(ALL)
+        start_swap(r.decoded, r.decoded_there, sems, 16)
+
+    @pl.when(step == 6)
+    def _():
+        beside.wait()
+        end.wait_sums()
+        cross_y.start()
+        cross_x.start()
+        end.wait_grads()
+
+        @over_tiles(rows)
+        def _(here):
+            r.grad[here, :] = dot(r.d_full[0, 1, here, :], r.cross_w[1], 1, 1) + dot(
+                r.d_full[0, 2, here, :], r.cross_w[2], 1, 1
+            )
+            grad = r.pre[0, here, :] + dot(r.d_full[0, 0, here, :], r.cross_w[0], 1, 1)
+            unit = r.first_unit[here, :]
+            r.vectors[2, 0:1, :] += column_sum(grad * unit)
+            r.vectors[2, 1:2, :] += column_sum(grad)
+            grad = normed_back(grad, unit, r.first_scale[here, :], r.dec_gain[0:1, :])
+            r.pre[0, here, :] = grad
+            mixed = grad.astype(BF)
+            r.dec_mixed[here, :] = mixed
+            r.dec_att_grad[here, :] = dot(mixed, r.dec_w[...], 1, 1).astype(BF)
+
+        for copy in dec_grads:
+            copy.start()
+        sum_out(r.dec_out_sums, r.dec_mixed, r.dec_att)
+        dec_shared.start()
+
+    @pl.when(step == 7)
+    def _():
+        enc_layer.wait()
+
+    @pl.when((step == 1) | (step == 7))
+    def _():
+        layers_back(r, step // 7)
+
+    @pl.when(step == 1)
+    def _():
+        for copy in cross_grads:
+            copy.start()
+
+    @pl.when(step == 7)
+    def _():
+        for copy in enc_grads:
+            copy.start()
+        down_y.finish()
+        up_x.finish()
+        both_low.start()
+
+    @pl.when((step == 1) | (step == 7))
+    def _():
+        sum_down(r.down_sums, r.branch_low, r.act)
+        shared[0].start()
+        sum_up(r.up_sums, r.inner_low, r.entering)
+        shared[1].start()
+        shared[0].finish()
+
+        @pl.when(step == 1)
+        def _():
+            down_x.start()
+
+        sum_out(r.out_sums, r.mixed_low, r.att)
+        shared[2].start()
+        shared[1].finish()
+
+        @pl.when(step == 1)
+        def _():
+            up_y.start()
+
+        shared[2].finish()
+
+    @pl.when(step == 1)
+    def _():
+        beside.start()
+        for copy in cross_grads:
+            copy.wait()
+        around.wait()
+        enc_layer.start()
+        first_layer.start()
+        back_begin(r, 0)
+
+    @pl.when((step >= 2) & (step < 6))
+    def _():
+        back_head(r, 0, step - 2, False)
+
+    @pl.when(step == 5)
+    def _():
+        first_layer.wait()
+        end.start()
+        down_x.finish()
+        up_y.finish()
+        down_y.start()
+        up_x.start()
+
+    @pl.when(step == 7)
+    def _():
+        dec_shared.finish()
+        results.start()
+        both_low.finish()
+        both_high.start()
+        for copy in (*dec_grads, *enc_grads):
+            copy.wait()
+        both_high.finish()
+        cross_y.finish()
+        cross_x.finish()
+        results.wait()
+        wait_swap(r.decoded, r.decoded_there, sems, 16)
+
+
+def last_body(r):
+    step = pl.program_id(0)
+    which = step // 4
+    mine, _ = places()
+    sems = r.sems
+    rows = r.pre.shape[1]
+
+    def side(att):
+        return Copies(
+            [
+                (r.queries_far.at[att], r.queries.at[att]), (r.keys_far.at[att], r.keys.at[att]),
+                (r.values_far.at[att], r.values.at[att]), (r.wide_far.at[att], r.wide.at[att]),
+                (r.grads_far.at[att], r.grad_all.at[att]), (r.x_far.at[att], r.x_all.at[att]),
+                ((r.enc_qkv, r.dec_qkv)[att], r.weights.at[att]), (r.pre_far.at[1 - att], r.pre.at[att]),
+                (r.out_units.at[att], r.units.at[att, :, :, :, :, pl.ds(0, 32)]),
+            ],
+            r.load_sems,
+            att * 9,
+        )
+
+    def layer_steps(unit, bufs, total, slot):
+        got, mid, less, least, last = bufs
+        return (
+            Halving(unit, 1, Y, got, mid, sems, slot, far=True),
+            Halving(mid, 1, LOW, less.at[0], less.at[1], sems, slot + 1),
+            Halving(less.at[1], 1, HIGH, least.at[0], least.at[1], sems, slot + 2),
+            Halving(least.at[1], 0, X, last, total, sems, slot + 3),
+        )
+
+    down = layer_steps(r.down_unit, r.down_bufs, r.enc_sums.at[0], 0)
+    up = layer_steps(r.up_unit, r.up_bufs, r.enc_sums.at[1], 4)
+    cross = join_halvings(r.cross_half, *r.cross_bufs, r.cross_sum, sems, 8)
+    enc_got, enc_mid, enc_less, enc_least, enc_final = r.enc_bufs
+    enc_att = (
+        Halving(r.units.at[0], 0, X, enc_got, enc_mid, sems, 17),
+        Halving(enc_mid, 0, Y, enc_less.at[0], enc_less.at[1], sems, 18),
+        Halving(enc_less.at[1], 0, LOW, enc_least.at[0], enc_least.at[1], sems, 19),
+        Halving(enc_least.at[1], 0, HIGH, enc_final, r.enc_att_sum, sems, 20),
+    )
+    dec_got, dec_mid, *dec_bufs = r.dec_bufs
+    dec_x, dec_y = split_halvings(r.units.at[1], dec_got, dec_mid, sems, 21)
+    dec_att = join_halvings(dec_mid, *dec_bufs, r.dec_att_sum, sems, 23)
+    vector_ways = (LOW, HIGH, CORE, X, Y)
+
+    def vector_parts(place):
+        source = r.vectors if place == 0 else r.vector_mid.at[place - 1]
+        total = r.vector_sum if place == 4 else r.vector_mid.at[place]
+        copy = sending(source, r.vector_got.at[place], sems, 12 + place, vector_ways[place])
+        return source, r.vector_got.at[place], total, copy
+
+    def vector_start(place):
+        vector_parts(place)[3].start()
+
+    def vector_finish(place):
+        source, got, total, copy = vector_parts(place)
+        copy.wait()
+        total[...] = source[...] + got[...]
+
+    end = BackEnd(r, which, r.units.at[which], which, which, r.end_sems)
+
+    def row_grads(index, target):
+        @over_tiles(rows)
+        def _(here):
+            total = r.pre[index, here, :]
+            for kind in range(3):
+                total = total + dot(r.d_full[index, kind, here, :], r.weights[index, kind], 1, 1)
+            r.row_grad[index, here, :] = total.astype(BF)
+
+        start_swap(r.row_grad.at[index], target, sems, 27 + index)
+
+    @pl.when(step == 0)
+    def _():
+        call_out(ALL)
+        side(0).start()
+        side(1).start()
+        side(0).wait()
+
+    @pl.when(step == 4)
+    def _():
+        side(1).wait()
+
+    @pl.when((step == 0) | (step == 4))
+    def _():
+        back_begin(r, which)
+
+    @pl.when(step == 0)
+    def _():
+        hear(ALL)
+        cross[0].start()
+        cross[1].start()
+        down[0].start()
+        up[0].start()
+        vector_start(0)
+
+    @pl.when(step == 4)
+    def _():
+        end_of_enc = BackEnd(r, 0, r.units.at[0], 0, 0, r.end_sems)
+        end_of_enc.wait_sums()
+        enc_att[0].start()
+        vector_finish(3)
+        vector_start(4)
+        cross[3].finish()
+        end_of_enc.wait_grads()
+        row_grads(0, r.src_there)
+
+    @pl.when(step == 1)
+    def _():
+        vector_finish(0)
+        vector_start(1)
+
+    @pl.when(step == 2)
+    def _():
+        vector_finish(1)
+        vector_start(2)
+        cross[0].finish()
+        cross[1].finish()
+        cross[2].start()
+
+    @pl.when(step == 3)
+    def _():
+        vector_finish(2)
+        vector_start(3)
+        cross[2].finish()
+        cross[3].start()
+
+    @pl.when(step == 5)
+    def _():
+        down[1].finish()
+        down[2].start()
+
+    @pl.when(step == 7)
+    def _():
+        up[0].finish()
+        up[1].start()
+
+    @pl.when(step < 4)
+    def _():
+        back_head(r, 0, step, False)
+
+    @pl.when(step >= 4)
+    def _():
+        back_head(r, 1, step - 4, True)
+
+    @pl.when((step == 3) | (step == 7))
+    def _():
+        end.start()
+
+    @pl.when(step == 3)
+    def _():
+        down[0].finish()
+        down[1].start()
+
+    @pl.when(step == 7)
+    def _():
+        down[2].finish()
+        down[3].start()
+        enc_att[0].finish()
+        enc_att[1].start()
+        end_of_dec = BackEnd(r, 1, r.units.at[1], 1, 1, r.end_sems)
+        end_of_dec.wait_sums()
+        dec_x.start()
+        dec_y.start()
+        end_of_dec.wait_grads()
+        row_grads(1, r.tgt_there)
+        up[1].finish()
+        up[2].start()
+        vector_finish(4)
+        enc_att[1].finish()
+        enc_att[2].start()
+        dec_x.finish()
+        dec_att[0].start()
+        dec_y.finish()
+        dec_att[1].start()
+        down[3].finish()
+        up[2].finish()
+        up[3].start()
+        enc_att[2].finish()
+        enc_att[3].start()
+        dec_att[0].finish()
+        dec_att[1].finish()
+        dec_att[2].start()
+        enc_att[3].finish()
+        up[3].finish()
+        dec_att[2].finish()
+        dec_att[3].start()
+        dec_att[3].finish()
+        wait_swap(r.row_grad.at[0], r.src_there, sems, 27)
+        wait_swap(r.row_grad.at[1], r.tgt_there, sems, 28)
+
+
+def finish_body(r):
+    r.decoded_out[...] = r.decoded[...]
+    r.src_out[...] = r.src[...]
+    r.tgt_out[...] = r.tgt[...]
+    for sums, down, up in ((r.dec_sums, r.dec_down, r.dec_up), (r.enc_sums, r.enc_down, r.enc_up)):
+        for slot in range(4):
+            down[:, slot * 256 : (slot + 1) * 256] = sums[0, slot * 32 : (slot + 1) * 32, :]
+        up[...] = sums[1].T
+    cross, dec_att = [jnp.concatenate([one[0], one[1]], axis=0) for one in (r.cross_sum, r.dec_att_sum)]
+    for sums, out, qkv in (
+        (cross, r.cross_out, r.cross_qkv),
+        (r.enc_att_sum[...], r.enc_out, r.enc_qkv),
+        (dec_att, r.dec_out, r.dec_qkv),
+    ):
+        out[...] = sums[:32]
+        for kind in range(3):
+            qkv[kind] = sums[32 + kind * 32 : 64 + kind * 32]
+    vectors = r.vectors
+    for which, up_bias, down_bias in ((0, r.dec_up_bias, r.dec_down_bias), (1, r.enc_up_bias, r.enc_down_bias)):
+        for part in range(4):
+            up_bias[:, part * 512 : (part + 1) * 512] = vectors[which, part : part + 1, :]
+        down_bias[...] = vectors[which, 4:5, :]
+    for ref, found in (
+        (r.dec_gain, ((2, 0), (0, 5), (0, 7))),
+        (r.dec_shift, ((2, 1), (0, 6), (0, 8))),
+        (r.enc_gain, ((1, 5), (1, 7))),
+        (r.enc_shift, ((1, 6), (1, 8))),
+    ):
+        for index, (which, place) in enumerate(found):
+            ref[index : index + 1, :] = vectors[which, place : place + 1, :]
+
+
+def launch(body, micros, grid, meeting, ins, far, blocks, outs, far_outs, scratch):
+    def once(shape):
+        rank = len(shape)
+        return pl.BlockSpec(shape, lambda step: (0,) * rank, pipeline_mode=pl.Buffered(1))
+
+    names, arrays, in_specs, out_names, shapes, out_specs = [], [], [], [], [], []
+    for name, array in {**ins, **far}.items():
+        names.append(name)
+        arrays.append(array)
+        in_specs.append(once(array.shape) if name in ins else ANY)
+    for name, (shape, kind) in {**outs, **far_outs}.items():
+        out_names.append(name)
+        shapes.append(jax.ShapeDtypeStruct(shape, kind))
+        out_specs.append(once(shape) if name in outs else ANY)
+    for name, (array, part, index, is_out) in blocks.items():
+        spec = pl.BlockSpec(part, index)
+        if is_out:
+            out_names.append(name)
+            shapes.append(jax.ShapeDtypeStruct(*array))
+            out_specs.append(spec)
+        else:
+            names.append(name)
+            arrays.append(array)
+            in_specs.append(spec)
+    every = (*names, *out_names, *scratch)
+
+    def kernel(*refs):
+        body(types.SimpleNamespace(**dict(zip(every, refs))))
+
+    results = pl.pallas_call(
+        kernel,
+        grid=(grid,),
+        out_shape=shapes,
+        in_specs=in_specs,
+        out_specs=out_specs,
+        scratch_shapes=list(scratch.values()),
+        compiler_params=pltpu.CompilerParams(
+            vmem_limit_bytes=60 * 2**20, collective_id=meeting, has_side_effects=meeting is not None
+        ),
+        cost_estimate=pl.CostEstimate(flops=int(micros * 1e9), bytes_accessed=0, transcendentals=0),
+        name=body.__name__,
+    )(*arrays)
+    return types.SimpleNamespace(**dict(zip(out_names, results)))
+
+
+def low(*shape):
+    return pltpu.VMEM(shape, BF)
+
+
+def wide(*shape):
+    return pltpu.VMEM(shape, F32)
+
+
+def fast_shards(source, target, source_ids, target_ids, out_grad, *params):
+    (
+        enc_qkv, enc_out, enc_up, enc_up_bias, enc_down, enc_down_bias, enc_gain, enc_shift, dec_qkv, dec_out,
+        cross_qkv, cross_out, dec_up, dec_up_bias, dec_down, dec_down_bias, dec_gain, dec_shift,
+    ) = params
+    source, target, upstream = source[0], target[0], out_grad[0]
+    rows, size = source.shape
+    length, inner, width = 2 * rows, enc_up.shape[1], size // 2
+    heads = width // HEAD_DIM
+    sem = pltpu.SemaphoreType.DMA
+    full, thin, low_full, low_inner = ((rows, size), F32), ((rows, 1), F32), ((rows, size), BF), ((rows, inner), BF)
+    biases = [one[None, :] for one in (enc_up_bias, enc_down_bias, dec_up_bias, dec_down_bias)]
+    enc_up_b, enc_down_b, dec_up_b, dec_down_b = biases
+    head_block = (1, length, length)
+    per_head = (heads, length, 2 * HEAD_DIM)
+
+    f = launch(
+        forward_body,
+        60,
+        13,
+        0,
+        dict(up_bias=enc_up_b, down_bias=enc_down_b, enc_gain=enc_gain, enc_shift=enc_shift, dec_gain=dec_gain, dec_shift=dec_shift),
+        dict(
+            source=source, target=target, source_ids=source_ids, target_ids=target_ids, upstream=upstream,
+            enc_qkv=enc_qkv, dec_qkv=dec_qkv, cross_qkv=cross_qkv, enc_out_far=enc_out, dec_out_far=dec_out,
+            up_far=enc_up, down_far=enc_down,
+        ),
+        dict(
+            chances=(
+                ((3 * heads, length, length), BF),
+                head_block,
+                lambda step: (jnp.where(step < 8, step, jnp.maximum(step - 1, 8)), 0, 0),
+                True,
+            )
+        ),
+        {},
+        dict(
+            x_far=((4, length, size), BF), upstream_there=low_full, queries_far=((3, *per_head), BF),
+            keys_far=((3, *per_head), BF), values_far=((3, *per_head), BF), wide_far=((3, length, width), F32),
+            att_far=((3, rows, size), BF), unit0_far=full, scale0_far=thin, unit1_far=full, scale1_far=thin,
+            hidden_far=low_full, act_far=low_inner, slope_far=low_inner, first_far=full, first_unit_far=full,
+            first_scale_far=thin,
+        ),
+        dict(
+            sems=sem((2, 31)), near_sems=sem((4,)), load_sems=sem((7,)), save_sems=sem((24,)),
+            x_all=low(4, length, size), ids=pltpu.VMEM((2, 2, 1, rows), jnp.int32), weights=low(3, 3, size, size),
+            queries=low(2, *per_head), keys=low(2, *per_head), values=low(2, *per_head),
+            outs=wide(heads, length, HEAD_DIM), wide=wide(3, length, width), att_all=low(3, rows, size),
+            att_send=low(3, rows, width), enc_out=low(size, size), dec_out=low(size, size), up=low(size, inner),
+            down=low(inner, size), unit0=wide(rows, size), scale0=wide(rows, 1), unit1=wide(rows, size),
+            scale1=wide(rows, 1), hidden_low=low(rows, size), act=low(rows, inner), slope=low(rows, inner),
+            first=wide(rows, size), first_unit=wide(rows, size), first_scale=wide(rows, 1),
+        ),
+    )
+    work = dict(
+        grads=low(*per_head), score_grads=low(length, length), dq=low(heads, length, HEAD_DIM), dk=wide(width, length),
+        dv=wide(width, length), d_all=low(3, length, width), shares=low(2, 2, 2, 2, 96, 256), end_sems=sem((3, 4)),
+    )
+    sums_out = ((2, 128, 256), F32)
+    halves = ((2, 64, 256), F32)
+    m = launch(
+        middle_body,
+        50,
+        8,
+        1,
+        dict(dec_gain=dec_gain, dec_shift=dec_shift, enc_gain=enc_gain, up_bias=dec_up_b, down_bias=dec_down_b),
+        dict(
+            first_far=f.first_far, att_far=f.att_far, upstream_far=f.upstream_there, cross_out=cross_out, dec_up=dec_up,
+            dec_down=dec_down, queries_far=f.queries_far, keys_far=f.keys_far, values_far=f.values_far,
+            wide_far=f.wide_far, x_far=f.x_far, cross_qkv=cross_qkv, dec_out=dec_out, first_unit_far=f.first_unit_far,
+            first_scale_far=f.first_scale_far, enc_up=enc_up, enc_down=enc_down, enc_out=enc_out,
+            unit0_far=f.unit0_far, scale0_far=f.scale0_far, unit1_far=f.unit1_far, scale1_far=f.scale1_far,
+            hidden_far=f.hidden_far, act_far=f.act_far, slope_far=f.slope_far,
+        ),
+        dict(chances=(f.chances, head_block, lambda step: (8 + jnp.clip(step - 2, 0, 3), 0, 0), False)),
+        dict(dec_sums=sums_out, cross_half=(HALF, BF), vectors=((3, 16, size), F32)),
+        dict(
+            decoded_there=low_full, grads_far=((2, length, width), BF), down_unit=(BIG, BF), up_unit=(BIG, BF),
+            out_units=((2, *OUT), BF), pre_far=((2, rows, size), F32),
+        ),
+        dict(
+            sems=sem((3, 17)), load_sems=sem((32,)), **work,
+            first=wide(rows, size), att=low(rows, size), upstream=low(rows, size), out_w=low(size, size),
+            up=low(size, inner), down=low(inner, size), queries=low(1, *per_head), keys=low(1, *per_head),
+            values=low(1, *per_head), wide=wide(1, length, width), x_all=low(2, length, size), cross_w=low(3, size, size),
+            dec_w=low(size, size), first_unit=wide(rows, size), first_scale=wide(rows, 1), dec_att=low(rows, size),
+            unit0=wide(rows, size), scale0=wide(rows, 1), unit1=wide(rows, size), scale1=wide(rows, 1),
+            entering=low(rows, size), act=low(rows, inner), inner_low=low(rows, inner), branch_low=low(rows, size),
+            mixed_low=low(rows, size), att_grad=low(rows, size), dec_att_grad=low(rows, size), dec_mixed=low(rows, size),
+            grad=wide(rows, size), pre=wide(2, rows, size), gains=wide(2, 2, size), decoded=low(rows, size),
+            grad_all=low(1, length, width), d_full=low(1, 3, rows, size), unit=low(*BIG),
+            down_sums=low(2, *BIG), up_sums=low(2, *BIG), out_sums=low(2, *OUT), dec_out_sums=low(2, *OUT),
+            down_got=low(*BIG), up_got=low(*BIG), out_got=low(*OUT), dec_out_got=low(*OUT),
+            got_a=low(*MID), mid_a=low(*MID), got_b=low(*MID), mid_b=low(*MID), got_c=low(*LESS), got_d=low(*LESS),
+            pair=low(2, *LESS), got_e=low(2, *LEAST), mid_e=low(2, *LEAST), got_f=low(2, 128, 256), got_g=low(*HALF),
+        ),
+    )
+    less, least = (2, 2, 2, 64, 256), (2, 64, 256)
+    layer_bufs = [low(*MID), low(*MID), low(2, *LESS), low(2, *LEAST), low(128, 256)]
+    join_bufs = [low(*less), low(*less), low(*less), low(*least)]
+    b = launch(
+        last_body,
+        60,
+        8,
+        2,
+        dict(cross_half=m.cross_half, vectors=m.vectors),
+        dict(
+            queries_far=f.queries_far, keys_far=f.keys_far, values_far=f.values_far, wide_far=f.wide_far, x_far=f.x_far,
+            grads_far=m.grads_far, enc_qkv=enc_qkv, dec_qkv=dec_qkv, pre_far=m.pre_far, out_units=m.out_units,
+            down_unit=m.down_unit, up_unit=m.up_unit,
+        ),
+        dict(chances=(f.chances, head_block, lambda step: (step, 0, 0), False)),
+        dict(
+            enc_sums=sums_out, cross_sum=halves, enc_att_sum=((128, 256), F32), dec_att_sum=halves,
+            vector_sum=((3, 16, size), F32),
+        ),
+        dict(src_there=low_full, tgt_there=low_full),
+        dict(
+            sems=sem((3, 29)), load_sems=sem((18,)), **work,
+            queries=low(2, *per_head), keys=low(2, *per_head), values=low(2, *per_head), wide=wide(2, length, width),
+            grad_all=low(2, length, width), x_all=low(2, length, size), weights=low(2, 3, size, size),
+            pre=wide(2, rows, size), d_full=low(2, 3, rows, size), units=low(2, *BIG), row_grad=low(2, rows, size),
+            vector_got=wide(5, 3, 16, size), vector_mid=wide(4, 3, 16, size), down_bufs=layer_bufs, up_bufs=layer_bufs,
+            enc_bufs=layer_bufs, cross_bufs=join_bufs, dec_bufs=[low(*HALF), low(*HALF), *join_bufs],
+        ),
+    )
+    cut3, cut, pair, triple = ((3, 32, 256), F32), ((32, 256), F32), ((2, size), F32), ((3, size), F32)
+    up_cut, down_cut, up_b, down_b = ((256, 128), F32), ((32, 1024), F32), ((1, inner), F32), ((1, size), F32)
+    o = launch(
+        finish_body,
+        2,
+        1,
+        None,
+        dict(
+            decoded=m.decoded_there, src=b.src_there, tgt=b.tgt_there, dec_sums=m.dec_sums, enc_sums=b.enc_sums,
+            cross_sum=b.cross_sum, enc_att_sum=b.enc_att_sum, dec_att_sum=b.dec_att_sum, vectors=b.vector_sum,
+        ),
+        {},
+        {},
+        dict(
+            decoded_out=low_full, src_out=low_full, tgt_out=low_full, enc_qkv=cut3, enc_out=cut, enc_up=up_cut,
+            enc_up_bias=up_b, enc_down=down_cut, enc_down_bias=down_b, enc_gain=pair, enc_shift=pair, dec_qkv=cut3,
+            dec_out=cut, cross_qkv=cut3, cross_out=cut, dec_up=up_cut, dec_up_bias=up_b, dec_down=down_cut,
+            dec_down_bias=down_b, dec_gain=triple, dec_shift=triple,
+        ),
+        {},
+        {},
+    )
+
+    def turned(value):
+        return jnp.swapaxes(value, -1, -2)
+
+    return (
+        o.decoded_out[None], o.src_out[None], o.tgt_out[None], turned(o.enc_qkv), turned(o.enc_out), o.enc_up,
+        o.enc_up_bias[0], turned(o.enc_down), o.enc_down_bias[0], o.enc_gain, o.enc_shift, turned(o.dec_qkv),
+        turned(o.dec_out), turned(o.cross_qkv), turned(o.cross_out), o.dec_up, o.dec_up_bias[0], turned(o.dec_down),
+        o.dec_down_bias[0], o.dec_gain, o.dec_shift,
+    )
+
+
+def solution(mesh):
+    if mesh.shape[SEQ] != 2 or mesh.shape[BATCH] != 16:
+        return general(mesh)
+    tokens = P(BATCH, SEQ, None)
+    ids = P(BATCH, SEQ)
+    cut, cut3 = P(SEQ, BATCH), P(None, SEQ, BATCH)
+    return jax.shard_map(
+        fast_shards,
+        mesh=mesh,
+        in_specs=(tokens, tokens, ids, ids, tokens) + (P(),) * 18,
+        out_specs=(
+            tokens, tokens, tokens, cut3, cut, cut, P(), cut, P(), P(), P(), cut3, cut, cut3, cut, cut, P(), cut,
+            P(), P(), P(),
+        ),
+        check_vma=False,
+    )

time: 1290 us -> 206 us (0.16)
  waiting for transfers between devices: 820 us -> 0 us
  matrix products: 209 us -> 0 us
  Pallas kernels: 0 us -> 203 us
  local copies, waits for them, and re-layouts: 90 us -> 0 us
  blocking collectives: 51.4 us -> 0 us
  loops' own time: 48.7 us -> 0 us
  other arithmetic: 40 us -> 0 us
  between operations: 17.2 us -> 0.86 us
    unnamed x40 -> x0, waiting for transfers between devices: 448 us -> none
    reduce_scatter x18 -> x0, waiting for transfers between devices: 372 us -> none  [the longest x1 57.7 us: shards(): lax.psum_scatter(all_rows[0].astype(jnp.bfloat16), 'batch', scatter_dimen...]
    dot_general x90 -> x0, matrix products: 209 us -> none  [the longest x16 40.1 us: weight_grad(): lax.dot_general(inputs, grad, (((0,), (0,)), ((), ())), preferred_element...]
    pallas_call x0 -> x4, Pallas kernels: none -> 203 us  [launch(): pl.pallas_call(kernel, grid=(grid,), out_shape=shapes, in_specs=in_specs,...]
    another operation x27 -> x0, loops' own time: 48.7 us -> none  [the longest x3 16 us: attend_forward(): largest, total = lax.fori_loop(0, count, first_pass, initial)]
    psum x1 -> x0, blocking collectives: 42.5 us -> none  [shards(): lax.psum((enc_up_bias_g, enc_down_bias_g, enc_gain_g, enc_shift_g, dec_up...]
    unnamed x281 -> x0, local copies, waits for them, and re-layouts: 40.8 us -> none
    reduce_sum x19 -> x0, other arithmetic: 18.9 us -> none  [the longest x6 12.2 us: first_compute(): return (newest, total * jnp.exp(largest - newest) + jnp.sum(terms, axis=-1))]
  transfers between devices with their start and end apart: 32 -> 0, of which waited for: 20 -> 0; matrix products, arithmetic and copies ran while one was open for 21% -> 0% of each run, Pallas kernels for 0% -> 0%
where the time goes in v2:
time: 206 us; the launch traced here: 203 us
  Pallas kernels  203 us (99%)
    pallas_call x4, Pallas kernels, launch(): pl.pallas_call(kernel, grid=(grid,), out_shape=shapes, in_specs=in_specs,...  203 us

profile of v2, /device:TPU:2, one launch (start us, length us, event | category | flops | bytes accessed | tf_op | source)
XLA Modules:
  0.0 203.4 jit_solution(1486319048430178772)
XLA Ops:
  0.7 64.9 %forward_body.1 = (bf16[4,1024,512]{2,1,0:T(8,128)(2,1)}, bf16[512,512]{1,0:T(8,128)(2,1)}, bf16[3,4,1024,128]{3,2,1,0:T(8,128)(2,1)}, bf16[3,4,1024,128]{3,2,1,...) custom-call(f32[1,2048]{1,0:T(1,128)} %bitcast.25, ...), custom_call_target="tpu_custom_call" | custom-call | flops 60000002048 | tf_op jit(solution)/shard_map/forward_body/pallas_call | solution.py:1714
  65.6 63.6 %middle_body.1 = (f32[2,128,256]{2,1,0:T(8,128)}, bf16[2,2,2,2,64,256]{5,4,3,2,1,0:T(8,128)(2,1)}, f32[3,16,512]{2,1,0:T(8,128)}, bf16[512,512]{1,0:T(8,128)(2,1...) custom-call(f32[3,512]{1,0:T(4,128)} %refs_0_.1, ...), custom_call_target="tpu_custom_call" | custom-call | flops 49999998976 | tf_op jit(solution)/shard_map/middle_body/pallas_call | solution.py:1714
  129.2 70.8 %last_body.1 = (f32[2,128,256]{2,1,0:T(8,128)}, f32[2,64,256]{2,1,0:T(8,128)}, f32[128,256]{1,0:T(8,128)}, f32[2,64,256]{2,1,0:T(8,128)}, f32[3,16,512]{2,1,0:T(...) custom-call(bf16[2,2,2,2,64,256]{5,4,3,2,1,0:T(8,128)(2,1)} %get-tuple-element.95.refs_0_, ...), custom_call_target="tpu_custom_call" | custom-call | flops 60000002048 | tf_op jit(solution)/shard_map/last_body/pallas_call | solution.py:1714
  200.0 3.2 %finish_body.1 = (bf16[512,512]{1,0:T(8,128)(2,1)}, bf16[512,512]{1,0:T(8,128)(2,1)}, bf16[512,512]{1,0:T(8,128)(2,1)}, f32[3,32,256]{2,1,0:T(8,128)}, f32[32,25...) custom-call(bf16[512,512]{1,0:T(8,128)(2,1)} %get-tuple-element.94.r, ...), custom_call_target="tpu_custom_call" | custom-call | flops 2000000000 | tf_op jit(solution)/shard_map/finish_body/pallas_call | solution.py:1714

commit v3 on v2

--- a/solution.py
+++ b/solution.py
@@ -829,7 +829,7 @@
     q_side, k_side = jnp.minimum(att, 1), att * (2 - att)
     which = lax.rem(att, 2)
     place = lax.broadcasted_iota(jnp.int32, (HEAD_DIM, TILE), 0)
-    ones = (lax.broadcasted_iota(jnp.int32, (TILE, HEAD_DIM), 1) < 3).astype(BF)
+    ones = jnp.ones((TILE, HEAD_DIM), BF)
     half_tiles = r.ids.shape[3] // TILE
 
     @pl.loop(0, r.x_all.shape[1] // TILE)
@@ -853,23 +853,28 @@
 
 def attend_head(r, which, head, causal):
     length = r.queries.shape[2]
-    if causal:
-        lower = lax.broadcasted_iota(jnp.int32, (TILE, TILE), 0) >= lax.broadcasted_iota(
-            jnp.int32, (TILE, TILE), 1
-        )
-    for tile in range(length // TILE):
+    count = length // TILE
+    lower = lax.broadcasted_iota(jnp.int32, (TILE, TILE), 0) >= lax.broadcasted_iota(jnp.int32, (TILE, TILE), 1)
+
+    def seen(tile):
+        return (tile + 1) * TILE if causal else length
+
+    def scores_of(tile):
         here = slice(tile * TILE, (tile + 1) * TILE)
-        seen = (tile + 1) * TILE if causal else length
-        scores = dot(r.queries[which, head, here, :], r.keys[which, head, :seen, :], 1, 1)
-        if causal:
-            last = jnp.where(lower, scores[:, seen - TILE :], NEGATIVE)
-            scores = last if tile == 0 else jnp.concatenate([scores[:, : seen - TILE], last], axis=1)
-        largest = jnp.max(scores, axis=-1, keepdims=True)
-        terms = jnp.exp(scores - largest)
-        total = jnp.sum(terms, axis=-1, keepdims=True)
-        low = (terms * (1.0 / total)).astype(BF)
-        r.chances[0, here, :seen] = low
-        r.outs[head, here, :] = dot(low, r.values[which, head, :seen, :])[:, :HEAD_DIM]
+        scores = dot(r.queries[which, head, here, :], r.keys[which, head, : seen(tile), :], 1, 1)
+        if not causal:
+            return scores
+        last = jnp.where(lower, scores[:, seen(tile) - TILE :], NEGATIVE)
+        return last if tile == 0 else jnp.concatenate([scores[:, : seen(tile) - TILE], last], axis=1)
+
+    scores = scores_of(0)
+    for tile in range(count):
+        here = slice(tile * TILE, (tile + 1) * TILE)
+        later = scores_of(tile + 1) if tile + 1 < count else None
+        low = jnp.exp(scores - jnp.max(scores, axis=-1, keepdims=True)).astype(BF)
+        r.chances[0, here, : seen(tile)] = low
+        r.outs[which, head, here, :] = dot(low, r.values[which, head, : seen(tile), :])
+        scores = later
 
 
 def forward_body(r):
@@ -877,7 +882,8 @@
     core = my_core()
     att = jnp.minimum(step // 4, 2)
     rows = r.source.shape[0]
-    width = r.outs.shape[0] * HEAD_DIM
+    heads = r.outs.shape[1]
+    width = heads * HEAD_DIM
     sems = r.sems
 
     def rows_of(side):
@@ -921,7 +927,7 @@
         return Copies(
             [
                 (r.queries.at[which], r.queries_far.at[index]), (r.keys.at[which], r.keys_far.at[index]),
-                (r.values.at[which], r.values_far.at[index]), (r.wide.at[index], r.wide_far.at[index]),
+                (r.values.at[which], r.values_far.at[index]), (r.outs.at[which], r.outs_far.at[index]),
             ],
             r.save_sems,
             index * 4,
@@ -988,12 +994,12 @@
     def _():
         for half in (1 - core, core):
             there = block(half, rows)
-            joined = jnp.concatenate([r.outs[head, there, :] for head in range(r.outs.shape[0])], axis=1)
-            r.wide[att, there, :] = joined
+            parts = [r.outs[lax.rem(att, 2), head, there, :] for head in range(heads)]
+            joined = jnp.concatenate([part[:, :HEAD_DIM] / part[:, HEAD_DIM:] for part in parts], axis=1).astype(BF)
             if half is core:
-                r.att_all[att, :, block(core, width)] = joined.astype(BF)
+                r.att_all[att, :, block(core, width)] = joined
             else:
-                r.att_send[att] = joined.astype(BF)
+                r.att_send[att] = joined
                 att_across(att).start()
 
     for index, last in enumerate((3, 7, 12)):
@@ -1052,41 +1058,64 @@
 
 def back_begin(r, which):
     heads = r.queries.shape[1]
-    lane = lax.broadcasted_iota(jnp.int32, (TILE, HEAD_DIM), 1)
+    width = heads * HEAD_DIM
+    lane = lax.rem(lax.broadcasted_iota(jnp.int32, (TILE, width), 1), HEAD_DIM)
+    same_head = (
+        lax.broadcasted_iota(jnp.int32, (width, width), 0) // HEAD_DIM
+        == lax.broadcasted_iota(jnp.int32, (width, width), 1) // HEAD_DIM
+    ).astype(BF)
 
     @over_tiles(r.queries.shape[2])
     def _(here):
-        grad = r.grad_all[which, here, :]
-        both = grad.astype(F32) * r.wide[which, here, :]
+        grad = r.grad_all[which, here, :].astype(F32)
+        lows, boths = [], []
         for head in range(heads):
-            part = slice(head * HEAD_DIM, (head + 1) * HEAD_DIM)
-            settle = -jnp.sum(both[:, part], axis=-1, keepdims=True)
-            first = settle.astype(BF).astype(F32)
-            second = (settle - first).astype(BF).astype(F32)
-            third = settle - first - second
-            extra = jnp.where(
-                lane == 0, first, jnp.where(lane == 1, second, jnp.where(lane == 2, third, 0.0))
+            out = r.outs[which, head, here, :]
+            over = 1.0 / out[:, HEAD_DIM:]
+            low = (grad[:, head * HEAD_DIM : (head + 1) * HEAD_DIM] * over).astype(BF)
+            lows.append(low)
+            boths.append(low.astype(F32) * (out[:, :HEAD_DIM] * over))
+        both = jnp.concatenate(boths, axis=1)
+        high = both.astype(BF)
+        rest = (both - high.astype(F32)).astype(BF)
+        settle = -dot(high, same_head) - dot(rest, same_head)
+        first = settle.astype(BF).astype(F32)
+        second = (settle - first).astype(BF).astype(F32)
+        extra = jnp.where(lane == 0, first, jnp.where(lane == 1, second, jnp.where(lane == 2, settle - first - second, 0.0)))
+        extra = extra.astype(BF)
+        for head in range(heads):
+            r.grads[head, here, :] = jnp.concatenate(
+                [lows[head], extra[:, head * HEAD_DIM : (head + 1) * HEAD_DIM]], axis=1
             )
-            r.grads[head, here, :] = jnp.concatenate([grad[:, part], extra.astype(BF)], axis=1)
 
 
 def back_head(r, which, head, causal):
     length = r.queries.shape[2]
-    for tile in range(length // TILE):
+    count = length // TILE
+
+    def seen(tile):
+        return (tile + 1) * TILE if causal else length
+
+    def change_of(tile):
         here = slice(tile * TILE, (tile + 1) * TILE)
-        seen = (tile + 1) * TILE if causal else length
-        change = dot(r.grads[head, here, :], r.values[which, head, :seen, :], 1, 1)
-        low = (r.chances[0, here, :seen].astype(F32) * change).astype(BF)
-        r.score_grads[here, :seen] = low
-        r.dq[head, here, :] = (dot(low, r.keys[which, head, :seen, :])[:, :HEAD_DIM] * 0.125).astype(BF)
-    for tile in range(length // TILE if causal else 1):
+        return dot(r.grads[head, here, :], r.values[which, head, : seen(tile), :], 1, 1)
+
+    change = change_of(0)
+    for tile in range(count):
+        here = slice(tile * TILE, (tile + 1) * TILE)
+        later = change_of(tile + 1) if tile + 1 < count else None
+        low = (r.chances[0, here, : seen(tile)].astype(F32) * change).astype(BF)
+        r.score_grads[here, : seen(tile)] = low
+        r.dq[head, here, :] = (dot(low, r.keys[which, head, : seen(tile), :])[:, :HEAD_DIM] * 0.125).astype(BF)
+        change = later
+    for tile in range(count if causal else 1):
         here = slice(tile * TILE, (tile + 1) * TILE) if causal else slice(0, length)
         below = slice(tile * TILE, length)
+        r.dv[block(head, HEAD_DIM), here] = dot(
+            r.grads[head, below, :HEAD_DIM], r.chances[0, below, here], 0, 0
+        )
         r.dk[block(head, HEAD_DIM), here] = dot(
             r.queries[which, head, below, :HEAD_DIM], r.score_grads[below, here], 0, 0
-        )
-        r.dv[block(head, HEAD_DIM), here] = dot(
-            r.grads[head, below, :HEAD_DIM], r.chances[0, below, here], 0, 0
         )
 
 
@@ -1279,7 +1308,7 @@
     around = Copies(
         [
             (r.queries_far.at[pl.ds(2, 1)], r.queries), (r.keys_far.at[pl.ds(2, 1)], r.keys),
-            (r.values_far.at[pl.ds(2, 1)], r.values), (r.wide_far.at[pl.ds(2, 1)], r.wide), (r.x_far.at[pl.ds(2, 2)], r.x_all),
+            (r.values_far.at[pl.ds(2, 1)], r.values), (r.outs_far.at[pl.ds(2, 1)], r.outs), (r.x_far.at[pl.ds(2, 2)], r.x_all),
         ],
         r.load_sems,
         6,
@@ -1305,8 +1334,9 @@
     up_y = Halving(r.up_sums.at[0], 1, Y, r.got_b, r.mid_b, sems, 1)
     down_y = Halving(r.mid_a, 0, Y, r.got_c, r.pair.at[0], sems, 2)
     up_x = Halving(r.mid_b, 0, X, r.got_d, r.pair.at[1], sems, 3)
-    both_low = Halving(r.pair, 1, LOW, r.got_e, r.mid_e, sems, 4)
-    both_high = Halving(r.mid_e, 1, HIGH, r.got_f, r.dec_sums, sems, 5)
+    down_low = Halving(r.pair.at[0], 0, LOW, r.got_e.at[0], r.mid_e, sems, 4)
+    up_low = Halving(r.pair.at[1], 0, LOW, r.got_e.at[1], r.up_rest, sems, 17)
+    down_high = Halving(r.mid_e, 0, HIGH, r.got_f, r.dec_down_sum, sems, 5)
     cross_x, cross_y = split_halvings(r.unit, r.got_g, r.cross_half, sems, 6)
     end = BackEnd(r, 0, r.unit, 0, 1, r.end_sems)
     shared = [
@@ -1381,6 +1411,8 @@
 
     @pl.when(step == 7)
     def _():
+        down_y.finish()
+        down_low.start()
         enc_layer.wait()
 
     @pl.when((step == 1) | (step == 7))
@@ -1396,9 +1428,10 @@
     def _():
         for copy in enc_grads:
             copy.start()
-        down_y.finish()
+        down_low.finish()
+        down_high.start()
         up_x.finish()
-        both_low.start()
+        up_low.start()
 
     @pl.when((step == 1) | (step == 7))
     def _():
@@ -1432,6 +1465,11 @@
         first_layer.start()
         back_begin(r, 0)
 
+    @pl.when(step == 5)
+    def _():
+        down_x.finish()
+        down_y.start()
+
     @pl.when((step >= 2) & (step < 6))
     def _():
         back_head(r, 0, step - 2, False)
@@ -1440,20 +1478,17 @@
     def _():
         first_layer.wait()
         end.start()
-        down_x.finish()
         up_y.finish()
-        down_y.start()
         up_x.start()
 
     @pl.when(step == 7)
     def _():
         dec_shared.finish()
         results.start()
-        both_low.finish()
-        both_high.start()
         for copy in (*dec_grads, *enc_grads):
             copy.wait()
-        both_high.finish()
+        down_high.finish()
+        up_low.finish()
         cross_y.finish()
         cross_x.finish()
         results.wait()
@@ -1471,7 +1506,7 @@
         return Copies(
             [
                 (r.queries_far.at[att], r.queries.at[att]), (r.keys_far.at[att], r.keys.at[att]),
-                (r.values_far.at[att], r.values.at[att]), (r.wide_far.at[att], r.wide.at[att]),
+                (r.values_far.at[att], r.values.at[att]), (r.outs_far.at[att], r.outs.at[att]),
                 (r.grads_far.at[att], r.grad_all.at[att]), (r.x_far.at[att], r.x_all.at[att]),
                 ((r.enc_qkv, r.dec_qkv)[att], r.weights.at[att]), (r.pre_far.at[1 - att], r.pre.at[att]),
                 (r.out_units.at[att], r.units.at[att, :, :, :, :, pl.ds(0, 32)]),
@@ -1480,29 +1515,26 @@
             att * 9,
         )
 
-    def layer_steps(unit, bufs, total, slot):
-        got, mid, less, least, last = bufs
-        return (
-            Halving(unit, 1, Y, got, mid, sems, slot, far=True),
-            Halving(mid, 1, LOW, less.at[0], less.at[1], sems, slot + 1),
-            Halving(less.at[1], 1, HIGH, least.at[0], least.at[1], sems, slot + 2),
-            Halving(least.at[1], 0, X, last, total, sems, slot + 3),
-        )
-
-    down = layer_steps(r.down_unit, r.down_bufs, r.enc_sums.at[0], 0)
-    up = layer_steps(r.up_unit, r.up_bufs, r.enc_sums.at[1], 4)
+    def layer_steps(unit, bufs, total, slot, ways):
+        left, steps, source = [X, Y, LOW, HIGH], [], unit
+        for place, way in enumerate(ways):
+            got, kept = (bufs[2 * place], bufs[2 * place + 1]) if place < 3 else (bufs[6], total)
+            steps.append(Halving(source, left.index(way), way, got, kept, sems, slot + place, far=place == 0))
+            left.remove(way)
+            source = kept
+        return steps
+
+    down = layer_steps(r.down_unit, r.down_bufs, r.enc_sums.at[0], 0, (X, Y, LOW, HIGH))
+    up = layer_steps(r.up_unit, r.up_bufs, r.enc_sums.at[1], 4, (Y, LOW, HIGH, X))
     cross = join_halvings(r.cross_half, *r.cross_bufs, r.cross_sum, sems, 8)
-    enc_got, enc_mid, enc_less, enc_least, enc_final = r.enc_bufs
-    enc_att = (
-        Halving(r.units.at[0], 0, X, enc_got, enc_mid, sems, 17),
-        Halving(enc_mid, 0, Y, enc_less.at[0], enc_less.at[1], sems, 18),
-        Halving(enc_less.at[1], 0, LOW, enc_least.at[0], enc_least.at[1], sems, 19),
-        Halving(enc_least.at[1], 0, HIGH, enc_final, r.enc_att_sum, sems, 20),
-    )
+    dec_up_high = Halving(r.up_rest, 0, HIGH, r.rest_got, r.dec_up_sum, sems, 17)
+    enc_got, enc_mid, *enc_bufs = r.enc_bufs
+    enc_x, enc_y = split_halvings(r.units.at[0], enc_got, enc_mid, sems, 18)
+    enc_att = join_halvings(enc_mid, *enc_bufs, r.enc_att_sum, sems, 20)
     dec_got, dec_mid, *dec_bufs = r.dec_bufs
-    dec_x, dec_y = split_halvings(r.units.at[1], dec_got, dec_mid, sems, 21)
-    dec_att = join_halvings(dec_mid, *dec_bufs, r.dec_att_sum, sems, 23)
-    vector_ways = (LOW, HIGH, CORE, X, Y)
+    dec_x, dec_y = split_halvings(r.units.at[1], dec_got, dec_mid, sems, 24)
+    dec_att = join_halvings(dec_mid, *dec_bufs, r.dec_att_sum, sems, 26)
+    vector_ways = (CORE, LOW, HIGH, X, Y)
 
     def vector_parts(place):
         source = r.vectors if place == 0 else r.vector_mid.at[place - 1]
@@ -1520,7 +1552,7 @@
 
     end = BackEnd(r, which, r.units.at[which], which, which, r.end_sems)
 
-    def row_grads(index, target):
+    def row_grads(index):
         @over_tiles(rows)
         def _(here):
             total = r.pre[index, here, :]
@@ -1528,7 +1560,8 @@
                 total = total + dot(r.d_full[index, kind, here, :], r.weights[index, kind], 1, 1)
             r.row_grad[index, here, :] = total.astype(BF)
 
-        start_swap(r.row_grad.at[index], target, sems, 27 + index)
+    src_swap = (r.row_grad.at[0], r.src_there, sems, 30)
+    tgt_swap = (r.row_grad.at[1], r.tgt_there, sems, 31)
 
     @pl.when(step == 0)
     def _():
@@ -1536,18 +1569,8 @@
         side(0).start()
         side(1).start()
         side(0).wait()
-
-    @pl.when(step == 4)
-    def _():
-        side(1).wait()
-
-    @pl.when((step == 0) | (step == 4))
-    def _():
-        back_begin(r, which)
-
-    @pl.when(step == 0)
-    def _():
         hear(ALL)
+        dec_up_high.start()
         cross[0].start()
         cross[1].start()
         down[0].start()
@@ -1556,112 +1579,129 @@
 
     @pl.when(step == 4)
     def _():
-        end_of_enc = BackEnd(r, 0, r.units.at[0], 0, 0, r.end_sems)
-        end_of_enc.wait_sums()
-        enc_att[0].start()
+        side(1).wait()
+        BackEnd(r, 0, r.units.at[0], 0, 0, r.end_sems).wait_sums()
+        enc_x.start()
+        enc_y.start()
+
+    @pl.when((step == 0) | (step == 4))
+    def _():
+        back_begin(r, which)
+
+    @pl.when(step == 1)
+    def _():
+        vector_finish(0)
+        vector_start(1)
+
+    @pl.when(step == 2)
+    def _():
+        vector_finish(1)
+        vector_start(2)
+        dec_up_high.finish()
+        cross[0].finish()
+        cross[1].finish()
+        cross[2].start()
+
+    @pl.when(step == 3)
+    def _():
+        vector_finish(2)
+        vector_start(3)
+
+    @pl.when(step == 4)
+    def _():
+        BackEnd(r, 0, r.units.at[0], 0, 0, r.end_sems).wait_grads()
+        row_grads(0)
+        start_swap(*src_swap)
+        down[0].finish()
+        down[1].start()
+        up[0].finish()
+        up[1].start()
+
+    @pl.when(step == 5)
+    def _():
         vector_finish(3)
         vector_start(4)
         cross[3].finish()
-        end_of_enc.wait_grads()
-        row_grads(0, r.src_there)
-
-    @pl.when(step == 1)
-    def _():
-        vector_finish(0)
-        vector_start(1)
-
-    @pl.when(step == 2)
-    def _():
-        vector_finish(1)
-        vector_start(2)
-        cross[0].finish()
-        cross[1].finish()
-        cross[2].start()
+
+    @pl.when(step == 7)
+    def _():
+        enc_x.finish()
+        enc_att[0].start()
+        enc_y.finish()
+        enc_att[1].start()
+
+    @pl.when(step < 4)
+    def _():
+        back_head(r, 0, step, False)
+
+    @pl.when(step >= 4)
+    def _():
+        back_head(r, 1, step - 4, True)
+
+    @pl.when((step == 3) | (step == 7))
+    def _():
+        end.start()
 
     @pl.when(step == 3)
     def _():
-        vector_finish(2)
-        vector_start(3)
         cross[2].finish()
         cross[3].start()
 
-    @pl.when(step == 5)
-    def _():
-        down[1].finish()
-        down[2].start()
-
     @pl.when(step == 7)
     def _():
-        up[0].finish()
-        up[1].start()
-
-    @pl.when(step < 4)
-    def _():
-        back_head(r, 0, step, False)
-
-    @pl.when(step >= 4)
-    def _():
-        back_head(r, 1, step - 4, True)
-
-    @pl.when((step == 3) | (step == 7))
-    def _():
-        end.start()
-
-    @pl.when(step == 3)
-    def _():
-        down[0].finish()
-        down[1].start()
-
-    @pl.when(step == 7)
-    def _():
-        down[2].finish()
-        down[3].start()
-        enc_att[0].finish()
-        enc_att[1].start()
+        up[1].finish()
+        up[2].start()
         end_of_dec = BackEnd(r, 1, r.units.at[1], 1, 1, r.end_sems)
         end_of_dec.wait_sums()
         dec_x.start()
         dec_y.start()
         end_of_dec.wait_grads()
-        row_grads(1, r.tgt_there)
-        up[1].finish()
-        up[2].start()
+        row_grads(1)
+        down[1].finish()
+        down[2].start()
         vector_finish(4)
+        enc_att[0].finish()
         enc_att[1].finish()
         enc_att[2].start()
+        up[2].finish()
+        up[3].start()
+        down[2].finish()
+        down[3].start()
         dec_x.finish()
         dec_att[0].start()
         dec_y.finish()
         dec_att[1].start()
-        down[3].finish()
-        up[2].finish()
-        up[3].start()
+        start_swap(*tgt_swap)
         enc_att[2].finish()
         enc_att[3].start()
+        down[3].finish()
+        up[3].finish()
         dec_att[0].finish()
         dec_att[1].finish()
         dec_att[2].start()
         enc_att[3].finish()
-        up[3].finish()
         dec_att[2].finish()
         dec_att[3].start()
         dec_att[3].finish()
-        wait_swap(r.row_grad.at[0], r.src_there, sems, 27)
-        wait_swap(r.row_grad.at[1], r.tgt_there, sems, 28)
+        wait_swap(*src_swap)
+        wait_swap(*tgt_swap)
 
 
 def finish_body(r):
     r.decoded_out[...] = r.decoded[...]
     r.src_out[...] = r.src[...]
     r.tgt_out[...] = r.tgt[...]
-    for sums, down, up in ((r.dec_sums, r.dec_down, r.dec_up), (r.enc_sums, r.enc_down, r.enc_up)):
+    for sums, down in ((r.dec_down_sum[...], r.dec_down), (r.enc_sums[0], r.enc_down)):
         for slot in range(4):
-            down[:, slot * 256 : (slot + 1) * 256] = sums[0, slot * 32 : (slot + 1) * 32, :]
-        up[...] = sums[1].T
-    cross, dec_att = [jnp.concatenate([one[0], one[1]], axis=0) for one in (r.cross_sum, r.dec_att_sum)]
+            down[:, slot * 256 : (slot + 1) * 256] = sums[slot * 32 : (slot + 1) * 32, :]
+    r.dec_up[...] = r.dec_up_sum[...].T
+    r.enc_up[...] = r.enc_sums[1].T
+    cross, enc_att, dec_att = [
+        jnp.concatenate([one[0], one[1]], axis=0) for one in (r.cross_sum, r.enc_att_sum, r.dec_att_sum)
+    ]
     for sums, out, qkv in (
         (cross, r.cross_out, r.cross_qkv),
-        (r.enc_att_sum[...], r.enc_out, r.enc_qkv),
+        (enc_att, r.enc_out, r.enc_qkv),
         (dec_att, r.dec_out, r.dec_qkv),
     ):
         out[...] = sums[:32]
@@ -1773,7 +1813,7 @@
         {},
         dict(
             x_far=((4, length, size), BF), upstream_there=low_full, queries_far=((3, *per_head), BF),
-            keys_far=((3, *per_head), BF), values_far=((3, *per_head), BF), wide_far=((3, length, width), F32),
+            keys_far=((3, *per_head), BF), values_far=((3, *per_head), BF), outs_far=((3, *per_head), F32),
             att_far=((3, rows, size), BF), unit0_far=full, scale0_far=thin, unit1_far=full, scale1_far=thin,
             hidden_far=low_full, act_far=low_inner, slope_far=low_inner, first_far=full, first_unit_far=full,
             first_scale_far=thin,
@@ -1782,7 +1822,7 @@
             sems=sem((2, 31)), near_sems=sem((4,)), load_sems=sem((7,)), save_sems=sem((24,)),
             x_all=low(4, length, size), ids=pltpu.VMEM((2, 2, 1, rows), jnp.int32), weights=low(3, 3, size, size),
             queries=low(2, *per_head), keys=low(2, *per_head), values=low(2, *per_head),
-            outs=wide(heads, length, HEAD_DIM), wide=wide(3, length, width), att_all=low(3, rows, size),
+            outs=wide(2, *per_head), att_all=low(3, rows, size),
             att_send=low(3, rows, width), enc_out=low(size, size), dec_out=low(size, size), up=low(size, inner),
             down=low(inner, size), unit0=wide(rows, size), scale0=wide(rows, 1), unit1=wide(rows, size),
             scale1=wide(rows, 1), hidden_low=low(rows, size), act=low(rows, inner), slope=low(rows, inner),
@@ -1793,6 +1833,7 @@
         grads=low(*per_head), score_grads=low(length, length), dq=low(heads, length, HEAD_DIM), dk=wide(width, length),
         dv=wide(width, length), d_all=low(3, length, width), shares=low(2, 2, 2, 2, 96, 256), end_sems=sem((3, 4)),
     )
+    one_sum = ((128, 256), F32)
     sums_out = ((2, 128, 256), F32)
     halves = ((2, 64, 256), F32)
     m = launch(
@@ -1804,22 +1845,22 @@
         dict(
             first_far=f.first_far, att_far=f.att_far, upstream_far=f.upstream_there, cross_out=cross_out, dec_up=dec_up,
             dec_down=dec_down, queries_far=f.queries_far, keys_far=f.keys_far, values_far=f.values_far,
-            wide_far=f.wide_far, x_far=f.x_far, cross_qkv=cross_qkv, dec_out=dec_out, first_unit_far=f.first_unit_far,
+            outs_far=f.outs_far, x_far=f.x_far, cross_qkv=cross_qkv, dec_out=dec_out, first_unit_far=f.first_unit_far,
             first_scale_far=f.first_scale_far, enc_up=enc_up, enc_down=enc_down, enc_out=enc_out,
             unit0_far=f.unit0_far, scale0_far=f.scale0_far, unit1_far=f.unit1_far, scale1_far=f.scale1_far,
             hidden_far=f.hidden_far, act_far=f.act_far, slope_far=f.slope_far,
         ),
         dict(chances=(f.chances, head_block, lambda step: (8 + jnp.clip(step - 2, 0, 3), 0, 0), False)),
-        dict(dec_sums=sums_out, cross_half=(HALF, BF), vectors=((3, 16, size), F32)),
+        dict(dec_down_sum=one_sum, up_rest=(LEAST, BF), cross_half=(HALF, BF), vectors=((3, 16, size), F32)),
         dict(
             decoded_there=low_full, grads_far=((2, length, width), BF), down_unit=(BIG, BF), up_unit=(BIG, BF),
             out_units=((2, *OUT), BF), pre_far=((2, rows, size), F32),
         ),
         dict(
-            sems=sem((3, 17)), load_sems=sem((32,)), **work,
+            sems=sem((3, 18)), load_sems=sem((32,)), **work,
             first=wide(rows, size), att=low(rows, size), upstream=low(rows, size), out_w=low(size, size),
             up=low(size, inner), down=low(inner, size), queries=low(1, *per_head), keys=low(1, *per_head),
-            values=low(1, *per_head), wide=wide(1, length, width), x_all=low(2, length, size), cross_w=low(3, size, size),
+            values=low(1, *per_head), outs=wide(1, *per_head), x_all=low(2, length, size), cross_w=low(3, size, size),
             dec_w=low(size, size), first_unit=wide(rows, size), first_scale=wide(rows, 1), dec_att=low(rows, size),
             unit0=wide(rows, size), scale0=wide(rows, 1), unit1=wide(rows, size), scale1=wide(rows, 1),
             entering=low(rows, size), act=low(rows, inner), inner_low=low(rows, inner), branch_low=low(rows, size),
@@ -1829,36 +1870,38 @@
             down_sums=low(2, *BIG), up_sums=low(2, *BIG), out_sums=low(2, *OUT), dec_out_sums=low(2, *OUT),
             down_got=low(*BIG), up_got=low(*BIG), out_got=low(*OUT), dec_out_got=low(*OUT),
             got_a=low(*MID), mid_a=low(*MID), got_b=low(*MID), mid_b=low(*MID), got_c=low(*LESS), got_d=low(*LESS),
-            pair=low(2, *LESS), got_e=low(2, *LEAST), mid_e=low(2, *LEAST), got_f=low(2, 128, 256), got_g=low(*HALF),
+            pair=low(2, *LESS), got_e=low(2, *LEAST), mid_e=low(*LEAST), got_f=low(128, 256), got_g=low(*HALF),
         ),
     )
     less, least = (2, 2, 2, 64, 256), (2, 64, 256)
-    layer_bufs = [low(*MID), low(*MID), low(2, *LESS), low(2, *LEAST), low(128, 256)]
+    down_bufs = [low(*MID), low(*MID), low(*LESS), low(*LESS), low(*LEAST), low(*LEAST), low(128, 256)]
+    up_bufs = [low(*MID), low(*MID), low(*LESS), low(*LESS), low(*LEAST), low(*LEAST), low(128, 256)]
     join_bufs = [low(*less), low(*less), low(*less), low(*least)]
+    split_bufs = [low(*HALF), low(*HALF), *join_bufs]
     b = launch(
         last_body,
         60,
         8,
         2,
-        dict(cross_half=m.cross_half, vectors=m.vectors),
+        dict(cross_half=m.cross_half, up_rest=m.up_rest, vectors=m.vectors),
         dict(
-            queries_far=f.queries_far, keys_far=f.keys_far, values_far=f.values_far, wide_far=f.wide_far, x_far=f.x_far,
+            queries_far=f.queries_far, keys_far=f.keys_far, values_far=f.values_far, outs_far=f.outs_far, x_far=f.x_far,
             grads_far=m.grads_far, enc_qkv=enc_qkv, dec_qkv=dec_qkv, pre_far=m.pre_far, out_units=m.out_units,
             down_unit=m.down_unit, up_unit=m.up_unit,
         ),
         dict(chances=(f.chances, head_block, lambda step: (step, 0, 0), False)),
         dict(
-            enc_sums=sums_out, cross_sum=halves, enc_att_sum=((128, 256), F32), dec_att_sum=halves,
+            enc_sums=sums_out, dec_up_sum=one_sum, cross_sum=halves, enc_att_sum=halves, dec_att_sum=halves,
             vector_sum=((3, 16, size), F32),
         ),
         dict(src_there=low_full, tgt_there=low_full),
         dict(
-            sems=sem((3, 29)), load_sems=sem((18,)), **work,
-            queries=low(2, *per_head), keys=low(2, *per_head), values=low(2, *per_head), wide=wide(2, length, width),
+            sems=sem((3, 32)), load_sems=sem((18,)), **work,
+            queries=low(2, *per_head), keys=low(2, *per_head), values=low(2, *per_head), outs=wide(2, *per_head),
             grad_all=low(2, length, width), x_all=low(2, length, size), weights=low(2, 3, size, size),
             pre=wide(2, rows, size), d_full=low(2, 3, rows, size), units=low(2, *BIG), row_grad=low(2, rows, size),
-            vector_got=wide(5, 3, 16, size), vector_mid=wide(4, 3, 16, size), down_bufs=layer_bufs, up_bufs=layer_bufs,
-            enc_bufs=layer_bufs, cross_bufs=join_bufs, dec_bufs=[low(*HALF), low(*HALF), *join_bufs],
+            vector_got=wide(5, 3, 16, size), vector_mid=wide(4, 3, 16, size), down_bufs=down_bufs, up_bufs=up_bufs,
+            enc_bufs=split_bufs, cross_bufs=join_bufs, dec_bufs=split_bufs, rest_got=low(128, 256),
         ),
     )
     cut3, cut, pair, triple = ((3, 32, 256), F32), ((32, 256), F32), ((2, size), F32), ((3, size), F32)
@@ -1869,7 +1912,8 @@
         1,
         None,
         dict(
-            decoded=m.decoded_there, src=b.src_there, tgt=b.tgt_there, dec_sums=m.dec_sums, enc_sums=b.enc_sums,
+            decoded=m.decoded_there, src=b.src_there, tgt=b.tgt_there, dec_down_sum=m.dec_down_sum, dec_up_sum=b.dec_up_sum,
+            enc_sums=b.enc_sums,
             cross_sum=b.cross_sum, enc_att_sum=b.enc_att_sum, dec_att_sum=b.dec_att_sum, vectors=b.vector_sum,
         ),
         {},

time: 206 us -> 183 us (0.89)
  Pallas kernels: 203 us -> 181 us
    pallas_call x4, Pallas kernels: 203 us -> 181 us  [launch(): pl.pallas_call(kernel, grid=(grid,), out_shape=shapes, in_specs=in_specs,...]
where the time goes in v3:
time: 183 us; the launch traced here: 182 us
  Pallas kernels  181 us (99%)
    pallas_call x4, Pallas kernels, launch(): pl.pallas_call(kernel, grid=(grid,), out_shape=shapes, in_specs=in_specs,...  181 us

profile of v3, /device:TPU:2, one launch (start us, length us, event | category | flops | bytes accessed | tf_op | source)
XLA Modules:
  0.0 181.6 jit_solution(10077203968277550409)
XLA Ops:
  0.7 53.7 %forward_body.1 = (bf16[4,1024,512]{2,1,0:T(8,128)(2,1)}, bf16[512,512]{1,0:T(8,128)(2,1)}, bf16[3,4,1024,128]{3,2,1,0:T(8,128)(2,1)}, bf16[3,4,1024,128]{3,2,1,...) custom-call(f32[1,2048]{1,0:T(1,128)} %bitcast.25, ...), custom_call_target="tpu_custom_call" | custom-call | flops 60000002048 | tf_op jit(solution)/shard_map/forward_body/pallas_call | solution.py:1754
  54.4 57.3 %middle_body.1 = (f32[128,256]{1,0:T(8,128)}, bf16[2,128,256]{2,1,0:T(8,128)(2,1)}, bf16[2,2,2,2,64,256]{5,4,3,2,1,0:T(8,128)(2,1)}, f32[3,16,512]{2,1,0:T(8,128...) custom-call(f32[3,512]{1,0:T(4,128)} %refs_0_.1, ...), custom_call_target="tpu_custom_call" | custom-call | flops 49999998976 | tf_op jit(solution)/shard_map/middle_body/pallas_call | solution.py:1754
  111.7 66.4 %last_body.1 = (f32[2,128,256]{2,1,0:T(8,128)}, f32[128,256]{1,0:T(8,128)}, f32[2,64,256]{2,1,0:T(8,128)}, f32[2,64,256]{2,1,0:T(8,128)}, f32[2,64,256]{2,1,0:T(...) custom-call(bf16[2,2,2,2,64,256]{5,4,3,2,1,0:T(8,128)(2,1)} %get-tuple-element.97.refs_0_, ...), custom_call_target="tpu_custom_call" | custom-call | flops 60000002048 | tf_op jit(solution)/shard_map/last_body/pallas_call | solution.py:1754
  178.2 3.2 %finish_body.1 = (bf16[512,512]{1,0:T(8,128)(2,1)}, bf16[512,512]{1,0:T(8,128)(2,1)}, bf16[512,512]{1,0:T(8,128)(2,1)}, f32[3,32,256]{2,1,0:T(8,128)}, f32[32,25...) custom-call(bf16[512,512]{1,0:T(8,128)(2,1)} %get-tuple-element.96.r, ...), custom_call_target="tpu_custom_call" | custom-call | flops 2000000000 | tf_op jit(solution)/shard_map/finish_body/pallas_call | solution.py:1754

commit v4 on v3

--- a/solution.py
+++ b/solution.py
@@ -635,7 +635,7 @@
 
 def over_tiles(rows):
     def run(body):
-        @pl.loop(0, rows // TILE)
+        @pl.loop(0, rows // TILE, unroll=2)
         def _(tile):
             body(block(tile, TILE))
 
@@ -832,7 +832,7 @@
     ones = jnp.ones((TILE, HEAD_DIM), BF)
     half_tiles = r.ids.shape[3] // TILE
 
-    @pl.loop(0, r.x_all.shape[1] // TILE)
+    @pl.loop(0, r.x_all.shape[1] // TILE, unroll=4)
     def _(tile):
         here = block(tile, TILE)
         lanes = block(lax.rem(tile, half_tiles), TILE)
@@ -851,36 +851,36 @@
             r.values[which, head, here, :] = jnp.concatenate([v_tile[:, part], ones], axis=1)
 
 
-def attend_head(r, which, head, causal):
+def attend_heads(r, which, first, causal):
     length = r.queries.shape[2]
-    count = length // TILE
     lower = lax.broadcasted_iota(jnp.int32, (TILE, TILE), 0) >= lax.broadcasted_iota(jnp.int32, (TILE, TILE), 1)
+    work = [(head, tile) for head in range(2) for tile in range(length // TILE)]
 
     def seen(tile):
         return (tile + 1) * TILE if causal else length
 
-    def scores_of(tile):
+    def scores_of(head, tile):
         here = slice(tile * TILE, (tile + 1) * TILE)
-        scores = dot(r.queries[which, head, here, :], r.keys[which, head, : seen(tile), :], 1, 1)
+        scores = dot(r.queries[which, first + head, here, :], r.keys[which, first + head, : seen(tile), :], 1, 1)
         if not causal:
             return scores
         last = jnp.where(lower, scores[:, seen(tile) - TILE :], NEGATIVE)
         return last if tile == 0 else jnp.concatenate([scores[:, : seen(tile) - TILE], last], axis=1)
 
-    scores = scores_of(0)
-    for tile in range(count):
+    scores = scores_of(*work[0])
+    for place, (head, tile) in enumerate(work):
         here = slice(tile * TILE, (tile + 1) * TILE)
-        later = scores_of(tile + 1) if tile + 1 < count else None
+        later = scores_of(*work[place + 1]) if place + 1 < len(work) else None
         low = jnp.exp(scores - jnp.max(scores, axis=-1, keepdims=True)).astype(BF)
-        r.chances[0, here, : seen(tile)] = low
-        r.outs[which, head, here, :] = dot(low, r.values[which, head, : seen(tile), :])
+        r.chances[head, here, : seen(tile)] = low
+        r.outs[which, first + head, here, :] = dot(low, r.values[which, first + head, : seen(tile), :])
         scores = later
 
 
 def forward_body(r):
     step = pl.program_id(0)
     core = my_core()
-    att = jnp.minimum(step // 4, 2)
+    att = jnp.minimum(step // 2, 2)
     rows = r.source.shape[0]
     heads = r.outs.shape[1]
     width = heads * HEAD_DIM
@@ -962,12 +962,12 @@
         source.finish()
         loads.wait()
 
-    @pl.when(step == 4)
+    @pl.when(step == 2)
     def _():
         target.pass_on()
         target.finish()
 
-    @pl.when(step == 9)
+    @pl.when(step == 5)
     def _():
         saved(0).wait()
         first_across.wait()
@@ -978,19 +978,19 @@
 
         kept.start()
 
-    @pl.when((step == 0) | (step == 4) | (step == 9))
+    @pl.when((step == 0) | (step == 2) | (step == 5))
     def _():
         attend_begin(r, att)
 
-    @pl.when((step < 4) | (step > 8))
-    def _():
-        attend_head(r, 0, lax.rem(step - att // 2, 4), False)
-
-    @pl.when((step >= 4) & (step < 8))
-    def _():
-        attend_head(r, 1, step - 4, True)
-
-    @pl.when((step == 3) | (step == 7) | (step == 12))
+    @pl.when((step < 2) | (step > 4))
+    def _():
+        attend_heads(r, 0, 2 * lax.rem(step - att // 2, 2), False)
+
+    @pl.when((step == 2) | (step == 3))
+    def _():
+        attend_heads(r, 1, 2 * (step - 2), True)
+
+    @pl.when((step == 1) | (step == 3) | (step == 6))
     def _():
         for half in (1 - core, core):
             there = block(half, rows)
@@ -1002,13 +1002,13 @@
                 r.att_send[att] = joined
                 att_across(att).start()
 
-    for index, last in enumerate((3, 7, 12)):
+    for index, last in enumerate((1, 3, 6)):
 
         @pl.when(step == last)
         def _(index=index):
             saved(index).start()
 
-    @pl.when(step == 8)
+    @pl.when(step == 4)
     def _():
         att_across(0).wait()
         att_across(1).wait()
@@ -1045,7 +1045,7 @@
             r.x_all[3, own, :] = (unit * r.enc_gain[1:2, :] + r.enc_shift[1:2, :]).astype(BF)
             memory_across(tile).start()
 
-    @pl.when(step == 12)
+    @pl.when(step == 6)
     def _():
         kept.wait()
         saved(1).wait()
@@ -1141,7 +1141,7 @@
         core = my_core()
         rows, heads = r.d_full.shape[2], r.dq.shape[0]
 
-        @pl.loop(0, 2)
+        @pl.loop(0, 2, unroll=2)
         def _(half):
             there = block(half, rows)
             r.d_all[0, there, :] = jnp.concatenate([r.dq[head, there, :] for head in range(heads)], axis=1)
@@ -1151,7 +1151,7 @@
         self.other().start()
         self.own().start()
 
-        @pl.loop(0, 3)
+        @pl.loop(0, 3, unroll=3)
         def _(kind):
             x_from = jnp.where(kind == 0, self.q_from, self.k_from)
             low = dot(r.d_all[kind], r.x_all[x_from], 0, 0).astype(BF)
@@ -1185,7 +1185,7 @@
 def sum_up(sums, inner_low, entering):
     core = my_core()
 
-    @pl.loop(0, 4)
+    @pl.loop(0, 4, unroll=4)
     def _(z):
         for y in range(2):
             low = dot(inner_low[:, block(z * 2 + y, 256)], entering[...], 0, 0).astype(BF)
@@ -1200,7 +1200,7 @@
 def sum_down(sums, branch_low, act):
     core = my_core()
 
-    @pl.loop(0, act.shape[1] // 512)
+    @pl.loop(0, act.shape[1] // 512, unroll=4)
     def _(column):
         for index in range(2):
             low = dot(branch_low[:, index * 256 : (index + 1) * 256], act[:, block(column, 512)], 0, 0).astype(BF)
@@ -1217,7 +1217,7 @@
 def sum_out(sums, mixed_low, att):
     core = my_core()
 
-    @pl.loop(0, 2)
+    @pl.loop(0, 2, unroll=2)
     def _(s):
         low = dot(mixed_low[...], att[:, block(s, 256)], 0, 0).astype(BF)
         for place in range(16):
@@ -1534,7 +1534,7 @@
     dec_got, dec_mid, *dec_bufs = r.dec_bufs
     dec_x, dec_y = split_halvings(r.units.at[1], dec_got, dec_mid, sems, 24)
     dec_att = join_halvings(dec_mid, *dec_bufs, r.dec_att_sum, sems, 26)
-    vector_ways = (CORE, LOW, HIGH, X, Y)
+    vector_ways = (X, Y, CORE, LOW, HIGH)
 
     def vector_parts(place):
         source = r.vectors if place == 0 else r.vector_mid.at[place - 1]
@@ -1570,12 +1570,12 @@
         side(1).start()
         side(0).wait()
         hear(ALL)
+        vector_start(0)
         dec_up_high.start()
         cross[0].start()
         cross[1].start()
         down[0].start()
         up[0].start()
-        vector_start(0)
 
     @pl.when(step == 4)
     def _():
@@ -1595,17 +1595,10 @@
 
     @pl.when(step == 2)
     def _():
-        vector_finish(1)
-        vector_start(2)
         dec_up_high.finish()
         cross[0].finish()
         cross[1].finish()
         cross[2].start()
-
-    @pl.when(step == 3)
-    def _():
-        vector_finish(2)
-        vector_start(3)
 
     @pl.when(step == 4)
     def _():
@@ -1617,10 +1610,15 @@
         up[0].finish()
         up[1].start()
 
+    @pl.when(step == 6)
+    def _():
+        vector_finish(2)
+        vector_start(3)
+
     @pl.when(step == 5)
     def _():
-        vector_finish(3)
-        vector_start(4)
+        vector_finish(1)
+        vector_start(2)
         cross[3].finish()
 
     @pl.when(step == 7)
@@ -1659,12 +1657,11 @@
         row_grads(1)
         down[1].finish()
         down[2].start()
-        vector_finish(4)
         enc_att[0].finish()
         enc_att[1].finish()
         enc_att[2].start()
-        up[2].finish()
-        up[3].start()
+        vector_finish(3)
+        vector_start(4)
         down[2].finish()
         down[3].start()
         dec_x.finish()
@@ -1672,13 +1669,16 @@
         dec_y.finish()
         dec_att[1].start()
         start_swap(*tgt_swap)
+        up[2].finish()
+        up[3].start()
         enc_att[2].finish()
         enc_att[3].start()
-        down[3].finish()
-        up[3].finish()
         dec_att[0].finish()
         dec_att[1].finish()
         dec_att[2].start()
+        vector_finish(4)
+        down[3].finish()
+        up[3].finish()
         enc_att[3].finish()
         dec_att[2].finish()
         dec_att[3].start()
@@ -1794,7 +1794,7 @@
     f = launch(
         forward_body,
         60,
-        13,
+        7,
         0,
         dict(up_bias=enc_up_b, down_bias=enc_down_b, enc_gain=enc_gain, enc_shift=enc_shift, dec_gain=dec_gain, dec_shift=dec_shift),
         dict(
@@ -1805,8 +1805,8 @@
         dict(
             chances=(
                 ((3 * heads, length, length), BF),
-                head_block,
-                lambda step: (jnp.where(step < 8, step, jnp.maximum(step - 1, 8)), 0, 0),
+                (2, length, length),
+                lambda step: (jnp.where(step < 4, step, jnp.maximum(step - 1, 4)), 0, 0),
                 True,
             )
         ),

time: 183 us -> 172 us (0.940)
  Pallas kernels: 181 us -> 171 us
    pallas_call x4, Pallas kernels: 181 us -> 171 us  [launch(): pl.pallas_call(kernel, grid=(grid,), out_shape=shapes, in_specs=in_specs,...]
where the time goes in v4:
time: 172 us
  Pallas kernels  171 us (99%)
    pallas_call x4, Pallas kernels, launch(): pl.pallas_call(kernel, grid=(grid,), out_shape=shapes, in_specs=in_specs,...  171 us

profile of v4, /device:TPU:2, one launch (start us, length us, event | category | flops | bytes accessed | tf_op | source)
XLA Modules:
  0.0 171.7 jit_solution(7397120456727544510)
XLA Ops:
  0.7 49.3 %forward_body.1 = (bf16[4,1024,512]{2,1,0:T(8,128)(2,1)}, bf16[512,512]{1,0:T(8,128)(2,1)}, bf16[3,4,1024,128]{3,2,1,0:T(8,128)(2,1)}, bf16[3,4,1024,128]{3,2,1,...) custom-call(f32[1,2048]{1,0:T(1,128)} %bitcast.25, ...), custom_call_target="tpu_custom_call" | custom-call | flops 60000002048 | tf_op jit(solution)/shard_map/forward_body/pallas_call | solution.py:1754
  49.9 54.3 %middle_body.1 = (f32[128,256]{1,0:T(8,128)}, bf16[2,128,256]{2,1,0:T(8,128)(2,1)}, bf16[2,2,2,2,64,256]{5,4,3,2,1,0:T(8,128)(2,1)}, f32[3,16,512]{2,1,0:T(8,128...) custom-call(f32[3,512]{1,0:T(4,128)} %refs_0_.1, ...), custom_call_target="tpu_custom_call" | custom-call | flops 49999998976 | tf_op jit(solution)/shard_map/middle_body/pallas_call | solution.py:1754
  104.2 64.1 %last_body.1 = (f32[2,128,256]{2,1,0:T(8,128)}, f32[128,256]{1,0:T(8,128)}, f32[2,64,256]{2,1,0:T(8,128)}, f32[2,64,256]{2,1,0:T(8,128)}, f32[2,64,256]{2,1,0:T(...) custom-call(bf16[2,2,2,2,64,256]{5,4,3,2,1,0:T(8,128)(2,1)} %get-tuple-element.97.refs_0_, ...), custom_call_target="tpu_custom_call" | custom-call | flops 60000002048 | tf_op jit(solution)/shard_map/last_body/pallas_call | solution.py:1754
  168.3 3.2 %finish_body.1 = (bf16[512,512]{1,0:T(8,128)(2,1)}, bf16[512,512]{1,0:T(8,128)(2,1)}, bf16[512,512]{1,0:T(8,128)(2,1)}, f32[3,32,256]{2,1,0:T(8,128)}, f32[32,25...) custom-call(bf16[512,512]{1,0:T(8,128)(2,1)} %get-tuple-element.96.r, ...), custom_call_target="tpu_custom_call" | custom-call | flops 2000000000 | tf_op jit(solution)/shard_map/finish_body/pallas_call | solution.py:1754

commit v5 on v4

--- a/solution.py
+++ b/solution.py
@@ -732,6 +732,15 @@
 
         self.onward = onward
 
+    def finish_early(self):
+        @pl.when(self.here)
+        def _():
+            self.near().wait()
+
+        @pl.when(jnp.logical_not(self.here))
+        def _():
+            self.early().wait_recv()
+
     def start(self):
         @pl.when(self.here)
         def _():
@@ -753,14 +762,12 @@
     def finish(self):
         @pl.when(self.here)
         def _():
-            self.near().wait()
             self.early().wait_send()
             for k in self.pieces:
                 self.onward(k).wait_recv()
 
         @pl.when(jnp.logical_not(self.here))
         def _():
-            self.early().wait_recv()
             for k in self.pieces:
                 self.onward(k).wait_send()
 
@@ -821,7 +828,7 @@
             copy().wait()
 
 
-def attend_begin(r, att):
+def attend_begin(r, att, half):
     heads = r.queries.shape[1]
     width = heads * HEAD_DIM
     columns = block(my_core(), width)
@@ -832,12 +839,12 @@
     ones = jnp.ones((TILE, HEAD_DIM), BF)
     half_tiles = r.ids.shape[3] // TILE
 
-    @pl.loop(0, r.x_all.shape[1] // TILE, unroll=4)
+    @pl.loop(0, half_tiles, unroll=2)
     def _(tile):
-        here = block(tile, TILE)
-        lanes = block(lax.rem(tile, half_tiles), TILE)
-        q_ids = r.ids[q_side, tile // half_tiles, :, lanes]
-        k_ids = r.ids[k_side, tile // half_tiles, :, lanes]
+        here = pl.ds(pl.multiple_of(half * r.ids.shape[3] + tile * TILE, TILE), TILE)
+        lanes = block(tile, TILE)
+        q_ids = r.ids[q_side, half, :, lanes]
+        k_ids = r.ids[k_side, half, :, lanes]
         asks = jnp.where(place == q_ids, 1.0, 0.0).T.astype(BF)
         bars = jnp.where((place != k_ids) & (place < 3), NEGATIVE, 0.0).T.astype(BF)
         left_q, left_k = r.x_all[q_from, here, :], r.x_all[k_from, here, :]
@@ -879,7 +886,8 @@
 
 def forward_body(r):
     step = pl.program_id(0)
-    core = my_core()
+    mine, _ = places()
+    core = mine[CORE]
     att = jnp.minimum(step // 2, 2)
     rows = r.source.shape[0]
     heads = r.outs.shape[1]
@@ -927,11 +935,14 @@
         return Copies(
             [
                 (r.queries.at[which], r.queries_far.at[index]), (r.keys.at[which], r.keys_far.at[index]),
-                (r.values.at[which], r.values_far.at[index]), (r.outs.at[which], r.outs_far.at[index]),
+                (r.values.at[which], r.values_far.at[index]),
             ],
             r.save_sems,
             index * 4,
         )
+
+    def saved_outs(index):
+        return Copies([(r.outs.at[index % 2], r.outs_far.at[index])], r.save_sems, index * 4 + 3)
 
     kept = Copies(
         [
@@ -954,33 +965,56 @@
         source.start()
         target.start()
         start_swap(r.upstream, r.upstream_there, sems, 30)
+        loads.wait()
+        for one_side in ids:
+            one_side.finish_early()
+        source.finish_early()
+
+    @pl.when(step == 2)
+    def _():
+        target.pass_on()
+        target.finish_early()
+
+    @pl.when(step == 5)
+    def _():
+        saved(0).wait()
+        saved_outs(0).wait()
+        first_across.wait()
+
+        @pl.loop(0, rows // TILE)
+        def _(tile):
+            memory_across(tile).wait()
+
+        kept.start()
+
+    begins = (step == 0) | (step == 2) | (step == 5)
+
+    @pl.when(begins)
+    def _():
+        attend_begin(r, att, mine[X])
+
+    @pl.when(step == 0)
+    def _():
         for one_side in ids:
             one_side.pass_on()
         source.pass_on()
         for one_side in ids:
             one_side.finish()
         source.finish()
-        loads.wait()
 
     @pl.when(step == 2)
     def _():
-        target.pass_on()
         target.finish()
 
-    @pl.when(step == 5)
-    def _():
-        saved(0).wait()
-        first_across.wait()
-
-        @pl.loop(0, rows // TILE)
-        def _(tile):
-            memory_across(tile).wait()
-
-        kept.start()
-
-    @pl.when((step == 0) | (step == 2) | (step == 5))
-    def _():
-        attend_begin(r, att)
+    @pl.when(begins)
+    def _():
+        attend_begin(r, att, 1 - mine[X])
+
+    for index, begun in enumerate((0, 2, 5)):
+
+        @pl.when(step == begun)
+        def _(index=index):
+            saved(index).start()
 
     @pl.when((step < 2) | (step > 4))
     def _():
@@ -1006,7 +1040,7 @@
 
         @pl.when(step == last)
         def _(index=index):
-            saved(index).start()
+            saved_outs(index).start()
 
     @pl.when(step == 4)
     def _():
@@ -1049,10 +1083,12 @@
     def _():
         kept.wait()
         saved(1).wait()
+        saved_outs(1).wait()
         wait_swap(r.upstream, r.upstream_there, sems, 30)
         att_across(2).wait()
         att_kept.start()
         saved(2).wait()
+        saved_outs(2).wait()
         att_kept.wait()
 
 
@@ -1447,6 +1483,14 @@
 
         sum_out(r.out_sums, r.mixed_low, r.att)
         shared[2].start()
+
+        @pl.when(step == 1)
+        def _():
+            for copy in cross_grads:
+                copy.wait()
+            around.wait()
+            back_begin(r, 0)
+
         shared[1].finish()
 
         @pl.when(step == 1)
@@ -1458,12 +1502,8 @@
     @pl.when(step == 1)
     def _():
         beside.start()
-        for copy in cross_grads:
-            copy.wait()
-        around.wait()
         enc_layer.start()
         first_layer.start()
-        back_begin(r, 0)
 
     @pl.when(step == 5)
     def _():

time: 172 us -> 171 us (level)
  Pallas kernels: 171 us -> 169 us
where the time goes in v5:
time: 171 us; the launch traced here: 170 us
  Pallas kernels  169 us (99%)
    pallas_call x4, Pallas kernels, launch(): pl.pallas_call(kernel, grid=(grid,), out_shape=shapes, in_specs=in_specs,...  169 us

profile of v5, /device:TPU:2, one launch (start us, length us, event | category | flops | bytes accessed | tf_op | source)
XLA Modules:
  0.0 170.3 jit_solution(4636601679660122433)
XLA Ops:
  0.7 47.9 %forward_body.1 = (bf16[4,1024,512]{2,1,0:T(8,128)(2,1)}, bf16[512,512]{1,0:T(8,128)(2,1)}, bf16[3,4,1024,128]{3,2,1,0:T(8,128)(2,1)}, bf16[3,4,1024,128]{3,2,1,...) custom-call(f32[1,2048]{1,0:T(1,128)} %bitcast.25, ...), custom_call_target="tpu_custom_call" | custom-call | flops 60000002048 | tf_op jit(solution)/shard_map/forward_body/pallas_call | solution.py:1794
  48.6 55.3 %middle_body.1 = (f32[128,256]{1,0:T(8,128)}, bf16[2,128,256]{2,1,0:T(8,128)(2,1)}, bf16[2,2,2,2,64,256]{5,4,3,2,1,0:T(8,128)(2,1)}, f32[3,16,512]{2,1,0:T(8,128...) custom-call(f32[3,512]{1,0:T(4,128)} %refs_0_.1, ...), custom_call_target="tpu_custom_call" | custom-call | flops 49999998976 | tf_op jit(solution)/shard_map/middle_body/pallas_call | solution.py:1794
  103.9 63.0 %last_body.1 = (f32[2,128,256]{2,1,0:T(8,128)}, f32[128,256]{1,0:T(8,128)}, f32[2,64,256]{2,1,0:T(8,128)}, f32[2,64,256]{2,1,0:T(8,128)}, f32[2,64,256]{2,1,0:T(...) custom-call(bf16[2,2,2,2,64,256]{5,4,3,2,1,0:T(8,128)(2,1)} %get-tuple-element.97.refs_0_, ...), custom_call_target="tpu_custom_call" | custom-call | flops 60000002048 | tf_op jit(solution)/shard_map/last_body/pallas_call | solution.py:1794
  166.9 3.2 %finish_body.1 = (bf16[512,512]{1,0:T(8,128)(2,1)}, bf16[512,512]{1,0:T(8,128)(2,1)}, bf16[512,512]{1,0:T(8,128)(2,1)}, f32[3,32,256]{2,1,0:T(8,128)}, f32[32,25...) custom-call(bf16[512,512]{1,0:T(8,128)(2,1)} %get-tuple-element.96.r, ...), custom_call_target="tpu_custom_call" | custom-call | flops 2000000000 | tf_op jit(solution)/shard_map/finish_body/pallas_call | solution.py:1794

commit v6 on v5

--- a/solution.py
+++ b/solution.py
@@ -1396,11 +1396,12 @@
     results = Copies(
         [
             (r.down_sums.at[0], r.down_unit), (r.up_sums.at[0], r.up_unit), (r.out_sums.at[0], r.out_units.at[0]),
-            (r.dec_out_sums.at[0], r.out_units.at[1]), (r.pre, r.pre_far),
+            (r.dec_out_sums.at[0], r.out_units.at[1]),
         ],
         r.load_sems,
         27,
     )
+    pre_result = Copies([(r.pre, r.pre_far)], r.load_sems, 31)
 
     @pl.when(step == 0)
     def _():
@@ -1464,6 +1465,7 @@
     def _():
         for copy in enc_grads:
             copy.start()
+        pre_result.start()
         down_low.finish()
         down_high.start()
         up_x.finish()
@@ -1532,6 +1534,7 @@
         cross_y.finish()
         cross_x.finish()
         results.wait()
+        pre_result.wait()
         wait_swap(r.decoded, r.decoded_there, sems, 16)
 
 

time: 171 us -> 171 us (level)
  no operation moved by 1% of the time
where the time goes in v6:
time: 171 us; the launch traced here: 170 us
  Pallas kernels  169 us (99%)
    pallas_call x4, Pallas kernels, launch(): pl.pallas_call(kernel, grid=(grid,), out_shape=shapes, in_specs=in_specs,...  169 us

profile of v6, /device:TPU:2, one launch (start us, length us, event | category | flops | bytes accessed | tf_op | source)
XLA Modules:
  0.0 169.5 jit_solution(11412297483433131642)
XLA Ops:
  0.7 47.9 %forward_body.1 = (bf16[4,1024,512]{2,1,0:T(8,128)(2,1)}, bf16[512,512]{1,0:T(8,128)(2,1)}, bf16[3,4,1024,128]{3,2,1,0:T(8,128)(2,1)}, bf16[3,4,1024,128]{3,2,1,...) custom-call(f32[1,2048]{1,0:T(1,128)} %bitcast.25, ...), custom_call_target="tpu_custom_call" | custom-call | flops 60000002048 | tf_op jit(solution)/shard_map/forward_body/pallas_call | solution.py:1797
  48.6 54.5 %middle_body.1 = (f32[128,256]{1,0:T(8,128)}, bf16[2,128,256]{2,1,0:T(8,128)(2,1)}, bf16[2,2,2,2,64,256]{5,4,3,2,1,0:T(8,128)(2,1)}, f32[3,16,512]{2,1,0:T(8,128...) custom-call(f32[3,512]{1,0:T(4,128)} %refs_0_.1, ...), custom_call_target="tpu_custom_call" | custom-call | flops 49999998976 | tf_op jit(solution)/shard_map/middle_body/pallas_call | solution.py:1797
  103.1 63.0 %last_body.1 = (f32[2,128,256]{2,1,0:T(8,128)}, f32[128,256]{1,0:T(8,128)}, f32[2,64,256]{2,1,0:T(8,128)}, f32[2,64,256]{2,1,0:T(8,128)}, f32[2,64,256]{2,1,0:T(...) custom-call(bf16[2,2,2,2,64,256]{5,4,3,2,1,0:T(8,128)(2,1)} %get-tuple-element.97.refs_0_, ...), custom_call_target="tpu_custom_call" | custom-call | flops 60000002048 | tf_op jit(solution)/shard_map/last_body/pallas_call | solution.py:1797
  166.1 3.2 %finish_body.1 = (bf16[512,512]{1,0:T(8,128)(2,1)}, bf16[512,512]{1,0:T(8,128)(2,1)}, bf16[512,512]{1,0:T(8,128)(2,1)}, f32[3,32,256]{2,1,0:T(8,128)}, f32[32,25...) custom-call(bf16[512,512]{1,0:T(8,128)(2,1)} %get-tuple-element.96.r, ...), custom_call_target="tpu_custom_call" | custom-call | flops 2000000000 | tf_op jit(solution)/shard_map/finish_body/pallas_call | solution.py:1797
